TPU v7x, 32 devices: a whole 2x2x4 slice. The times are simulated.
32 devices in a mesh: group: 2 (over y), dp: 4 (over z), expert: 4 (over x, core).
Axes of the slice: x: 2, y: 2, z: 4, core: 2. Of those that a mesh axis runs over, the one named last changes fastest.
Arguments:
- tokens: bfloat16 [1024, 6144], P(('group', 'dp'), 'expert'), parts along dimension 0, may hold values from -6 to 6
- cotangent: bfloat16 [1024, 6144], P(('group', 'dp'), 'expert'), parts along dimension 0, may hold values from -6 to 6
- expert_ids: int32 [1024, 2], P(('group', 'dp')), parts along dimension 0, may hold values from 0 to 7, as said below
- quantized: int32 [1024, 2], P(('group', 'dp')), parts along dimension 0, may hold values from 1 to 65535
- weight_in: bfloat16 [2, 8192, 6144], P(None, 'dp', 'expert'), may hold values from -0.078125 to 0.078125
- weight_out: bfloat16 [8192, 6144], P('dp', 'expert'), may hold values from -0.0625 to 0.0625
Outputs:
- input_grad: bfloat16 [1024, 6144], P(('group', 'dp'), 'expert'), parts along dimension 0
- weight_grad: bfloat16 [1024, 2], P(('group', 'dp')), parts along dimension 0
- grad_weight_in: float32 [4, 8192, 6144], P('group', 'dp', 'expert'), parts along dimension 0
- grad_weight_out: float32 [16384, 6144], P(('group', 'dp'), 'expert'), parts along dimension 0
There are 2 independent parts, one for each index of `group`. A program takes and returns all parts, laid end to end along the dimension named above; an argument that names none is the same for every part. Nothing has to cross between parts.
Inputs may be any that keep to these rules, and one draw needn't show every extreme that they name: `expert_ids`: each row names 2 different experts. Among the 128 rows of one index of dp at most 32 name expert 0, and for some index exactly 32 do.
All inputs are finite; a program needn't handle non-finite values.
Results may differ from a plain program's by a relative error of at most 0.008.
Values may be sent and summed in bfloat16 or wider, within the bound.
No kernel may reach another device: no remote copies, remote signals or barrier semaphores. Data moves between devices by JAX's collectives and lax.ppermute only.
A program may use at most 128 MiB of HBM per device.

v0:
```python
import jax
import jax.numpy as jnp
from jax import lax
from jax.sharding import PartitionSpec as P


def routing_weights(quantized):
    scaled = quantized.astype(jnp.float32)
    return (scaled / jnp.sum(scaled, axis=1, keepdims=True)).astype(jnp.bfloat16)


def gating(projected, back_hidden, rate_rows):
    gate_pre = projected[:, 0]
    up_pre = projected[:, 1]
    sigmoid_gate = jax.nn.sigmoid(gate_pre)
    hidden = (gate_pre * sigmoid_gate * up_pre).astype(jnp.bfloat16)
    route_part = jnp.sum(hidden.astype(jnp.float32) * back_hidden, axis=1)
    hidden_grad = rate_rows[:, None] * back_hidden
    gate_grad = hidden_grad * up_pre * sigmoid_gate * (1.0 + gate_pre * (1.0 - sigmoid_gate))
    up_grad = hidden_grad * gate_pre * sigmoid_gate
    pre_grad = jnp.stack([gate_grad, up_grad], axis=1).astype(jnp.bfloat16)
    return (hidden, pre_grad, route_part)


def per_device(tokens, cotangent, expert_ids, quantized, weight_in, weight_out):
    tok_rows = tokens.shape[0]
    capacity = tok_rows // 4
    routing = routing_weights(quantized)
    chosen = expert_ids == 0
    routed = jnp.any(chosen, axis=1).astype(jnp.int32)
    position = jnp.cumsum(routed) - routed
    slot_of = jnp.where(routed > 0, position, capacity)
    selector = (slot_of[None, :] == jnp.arange(capacity, dtype=jnp.int32)[:, None]).astype(
        jnp.float32
    )
    picker = selector.astype(jnp.bfloat16)
    rate = jnp.sum(
        jnp.where(chosen, routing.astype(jnp.float32), jnp.zeros((), jnp.float32)), axis=1
    )
    send_in = jnp.dot(picker, tokens, preferred_element_type=jnp.float32).astype(jnp.bfloat16)
    send_grad = jnp.dot(picker, cotangent, preferred_element_type=jnp.float32).astype(jnp.bfloat16)
    send_rate = jnp.sum(selector * rate[None, :], axis=1).astype(jnp.bfloat16)
    rows_in, rows_grad, rows_rate = (
        lax.all_gather(send_in, "dp", axis=0, tiled=True),
        lax.all_gather(send_grad, "dp", axis=0, tiled=True),
        lax.all_gather(send_rate, "dp", axis=0, tiled=True),
    )
    rate_rows = rows_rate.astype(jnp.float32)
    part_proj = jnp.einsum("rd,khd->rkh", rows_in, weight_in, preferred_element_type=jnp.float32)
    part_back = jnp.einsum("rd,hd->rh", rows_grad, weight_out, preferred_element_type=jnp.float32)
    projected, back_hidden = lax.psum((part_proj, part_back), "expert")
    hidden, pre_grad, route_part = gating(projected, back_hidden, rate_rows)
    out_grad = (rate_rows[:, None] * rows_grad.astype(jnp.float32)).astype(jnp.bfloat16)
    grad_weight_out = jnp.einsum("rh,rd->hd", hidden, out_grad, preferred_element_type=jnp.float32)
    grad_weight_in = jnp.einsum(
        "rkh,rd->khd", pre_grad, rows_in, preferred_element_type=jnp.float32
    )
    row_part = jnp.einsum("rkh,khd->rd", pre_grad, weight_in, preferred_element_type=jnp.float32)
    own_rows, own_route = (
        lax.psum_scatter(row_part, "dp", scatter_dimension=0, tiled=True),
        lax.psum_scatter(route_part, "dp", scatter_dimension=0, tiled=True),
    )
    back_rows = own_rows.astype(jnp.bfloat16)
    input_grad = jnp.einsum(
        "ct,cd->td", picker, back_rows, preferred_element_type=jnp.float32
    ).astype(jnp.bfloat16)
    route_tokens = jnp.sum(selector * own_route[:, None], axis=0)
    weight_grad = jnp.where(chosen, route_tokens[:, None], jnp.zeros((), jnp.float32)).astype(
        jnp.bfloat16
    )
    return (input_grad, weight_grad, grad_weight_in, grad_weight_out)


def solution(mesh):
    return jax.shard_map(
        per_device,
        mesh=mesh,
        in_specs=(
            P(("group", "dp"), "expert"),
            P(("group", "dp"), "expert"),
            P(("group", "dp"), None),
            P(("group", "dp"), None),
            P(None, "dp", "expert"),
            P("dp", "expert"),
        ),
        out_specs=(
            P(("group", "dp"), "expert"),
            P(("group", "dp"), None),
            P("group", "dp", "expert"),
            P(("group", "dp"), "expert"),
        ),
        check_vma=False,
    )
```

profile of v0, /device:TPU:0, one launch (start us, length us, event | category | flops | bytes accessed | tf_op | source)
XLA Modules:
  0.0 187.7 jit_solution(17347929592079588777)
XLA Ops:
  7.2 0.0 copy-start
  7.2 0.0 slice-start
  7.2 0.0 all-reduce.5.cloned.1.call-start
  7.2 0.8 fusion.15
  8.1 0.1 copy.16
  8.2 0.2 reduce-window.8
  8.4 0.1 reduce
  8.5 0.0 copy-done
  8.5 0.2 convolution_convert_fusion.1
  8.7 16.2 %all_gather.11 = bf16[128,1536]{1,0:T(8,128)(2,1)S(1)} all-gather(bf16[32,1536]{1,0:T(8,128)(2,1)S(1)} %convolution_convert_fusion.1), channel_id=1, replica_groups=mesh['group'=2,'dp'=4,'expert'=4] {'dp'}, dimensions={0}, use_global_device_ids=true | all-gather | bytes 491520 | tf_op jit(solution)/shard_map/all_gather | solution.py:44
  24.9 1.2 convolution_convert_fusion.2
  26.1 15.4 %all_gather.10 = bf16[128,1536]{1,0:T(8,128)(2,1)S(1)} all-gather(bf16[32,1536]{1,0:T(8,128)(2,1)S(1)} %convolution_convert_fusion.2), channel_id=1, replica_groups=mesh['group'=2,'dp'=4,'expert'=4] {'dp'}, dimensions={0}, use_global_device_ids=true | all-gather | bytes 491520 | tf_op jit(solution)/shard_map/all_gather | solution.py:45
  41.5 0.0 slice-start.1
  41.5 0.0 copy-start.3
  41.5 0.0 copy-start.4
  41.5 0.0 copy-start.2
  41.6 10.1 %fusion.5 = f32[128,2,2048]{2,0,1:T(8,128)} fusion(bf16[2,2048,1536]{2,1,0:T(8,128)(2,1)} %param.10, bf16[128,1536]{1,0:T(8,128)(2,1)S(1)} %all_gather.11), kind=kOutput, calls=%fused_computation.18 | convolution fusion | flops 1610612736 | bytes 15073280 | tf_op jit(solution)/shard_map/rd,khd->rkh/dot_general | solution.py:49
  51.7 0.0 slice-done
  51.7 0.0 slice-done.1
  51.7 3.1 %fusion.17 = f32[128,2048]{1,0:T(8,128)} fusion(bf16[128,1536]{1,0:T(8,128)(2,1)S(1)} %all_gather.10, bf16[2048,1536]{1,0:T(8,128)(2,1)S(1)} %bitcast.45), kind=kOutput, calls=%fused_computation.41 | convolution fusion | flops 805306368 | bytes 7733248 | tf_op jit(solution)/shard_map/rd,hd->rh/dot_general | solution.py:50
  54.7 0.0 all-reduce.5.cloned.1.call-update
  54.8 0.0 reduce-scatter.2.cloned.1.call-start
  54.8 0.0 copy-done.3
  54.8 0.6 fusion.16
  56.7 0.0 copy-done.4
  56.8 0.0 copy-done.2
  56.8 67.4 %all-reduce.5.cloned.1.call-done = (f32[128,2,2048]{2,0,1:T(8,128)}, f32[128,2048]{1,0:T(8,128)}) async-done(((f32[128,2,2048]{2,0,1:T(8,128)}, f32[128,2048]{1,0:T(8,128)}), (f32[128,2,2048]{2,0,1:T(8,128)}, f32[128,2048]{1,0:T(8,128)})) %all-reduce.5.cloned.1.call-update) | async-done | bytes 3145744 | tf_op jit(solution)/shard_map/psum | solution.py:51
  124.2 2.3 %multiply_reduce_fusion = (f32[128]{0:T(128)S(1)}, bf16[128,2048]{1,0:T(8,128)(2,1)S(1)}) fusion(f32[128,2048]{1,0:T(8,128)} %get-tuple-element.7, f32[128,2,2048]{2,0,1:T(8,128)} %get-tuple-element.6), kind=kLoop, calls=%fused_computation.7 | loop fusion | flops 2359168 | bytes 3670528 | tf_op jit(solution)/shard_map/reduce_sum | solution.py:17
  126.5 11.7 %all-reduce.1 = f32[128]{0:T(128)S(1)} all-reduce(f32[128]{0:T(128)S(1)} %get-tuple-element.8), channel_id=3, replica_groups=mesh['group'=2,'dp'=4,'expert'=4] {'dp'}, use_global_device_ids=true, to_apply=%region_9.10.clone | all-reduce | flops 128 | bytes 1024
  138.2 0.1 dynamic-slice.2
  138.3 0.1 select_reduce_fusion
  138.4 0.2 dynamic-update-slice
  138.7 8.3 %all-reduce = bf16[128]{0:T(256)(128)(2,1)S(1)} all-reduce(bf16[128]{0:T(256)(128)(2,1)S(1)} %dynamic-update-slice), channel_id=1, replica_groups=mesh['group'=2,'dp'=4,'expert'=4] {'dp'}, use_global_device_ids=true, to_apply=%add | all-reduce | flops 128 | bytes 512
  147.0 2.4 %fusion.2 = (bf16[128,1,2048]{2,0,1:T(8,128)(2,1)S(1)}, bf16[128,1,2048]{2,0,1:T(8,128)(2,1)S(1)}) fusion(f32[128,2,2048]{2,0,1:T(8,128)} %get-tuple-element.6, f32[128,2048]{1,0:T(8,128)} %get-tuple-element.7, f32[128]{0:T(128)S(1)} %convert_element_type.79), kind=kLoop, calls=%fused_computation.15 | loop fusion | flops 3670016 | bytes 4194816 | tf_op jit(solution)/shard_map/stack | solution.py:21
  149.4 7.3 %convolution_bitcast_fusion = f32[128,1536]{1,0:T(8,128)} fusion(bf16[2,2048,1536]{2,1,0:T(8,128)(2,1)} %param.10, bf16[128,1,2048]{2,0,1:T(8,128)(2,1)S(1)} %get-tuple-element.11, bf16[128,1,2048]{2,0,1:T(8,128)(2,1)S(1)} %get-tuple-element.10), kind=kOutput, calls=%fused_computation | convolution fusion | flops 1611137024 | bytes 14417920 | tf_op jit(solution)/shard_map/rkh,khd->rd/dot_general | solution.py:58
  156.7 0.0 reduce-scatter.2.cloned.1.call-update
  156.7 0.5 select_convert_fusion
  157.2 0.0 copy-start.1
  157.2 6.7 %fusion.3 = f32[2048,1536]{1,0:T(8,128)} fusion(bf16[128,2048]{1,0:T(8,128)(2,1)S(1)} %get-tuple-element.9, bf16[128,1536]{1,0:T(8,128)(2,1)S(1)} %all_gather.10, f32[128]{0:T(128)S(1)} %convert_element_type.79), kind=kOutput, calls=%fused_computation.16 | convolution fusion | flops 805896192 | bytes 13500928 | tf_op jit(solution)/shard_map/rh,rd->hd/dot_general | solution.py:54
  163.9 10.7 %fusion = f32[2,2048,1536]{2,1,0:T(8,128)} fusion(bf16[128,1,2048]{2,0,1:T(8,128)(2,1)S(1)} %get-tuple-element.11, bf16[128,1,2048]{2,0,1:T(8,128)(2,1)S(1)} %get-tuple-element.10, bf16[128,1536]{1,0:T(8,128)(2,1)S(1)} %all_gather.11), kind=kOutput, calls=%fused_computation.13 | convolution fusion | flops 1611137024 | bytes 26607616 | tf_op jit(solution)/shard_map/rkh,rd->khd/dot_general | solution.py:55
  174.6 4.3 %reduce-scatter.2.cloned.1.call-done = f32[32,1536]{1,0:T(8,128)} async-done(((f32[128,1536]{1,0:T(8,128)}), f32[32,1536]{1,0:T(8,128)}) %reduce-scatter.2.cloned.1.call-update) | async-done | bytes 196624 | tf_op jit(solution)/shard_map/reduce_scatter | solution.py:60
  178.9 2.0 %convolution_convert_fusion = bf16[128,1536]{1,0:T(8,128)(2,1)} fusion(f32[32,1536]{1,0:T(8,128)} %reduce-scatter.2.cloned.1.call-done, s32[128]{0:T(128)S(1)} %compare_select_fusion), kind=kOutput, calls=%fused_computation.1 | convolution fusion | flops 12840960 | bytes 590336 | tf_op jit(solution)/shard_map/ct,cd->td/dot_general | solution.py:64
  180.9 0.0 copy-done.1
  (7 shorter events, 0.1 us)
Async XLA Ops:
  7.2 1.3 copy-start
  7.2 44.5 %slice-start = ((s8[6291456]{0:T(1024)(128)(4,1)}), s8[2097152]{0:T(1024)(128)(4,1)S(1)}, s32[]{:S(2)}) async-start(s8[6291456]{0:T(1024)(128)(4,1)} %bitcast.44), calls=%async_computation.3 | async-start | bytes 4194304
  7.2 117.0 %all-reduce.5.cloned.1.call-start = ((), (), s32[]{:S(2)}) async-start(), calls=%async_computation.2 | async-start | bytes 6291456 | tf_op jit(solution)/shard_map/psum | solution.py:51
  41.5 10.1 %slice-start.1 = ((s8[6291456]{0:T(1024)(128)(4,1)}), s8[4194304]{0:T(1024)(128)(4,1)S(1)}, s32[]{:S(2)}) async-start(s8[6291456]{0:T(1024)(128)(4,1)} %bitcast.44), calls=%async_computation.4 | async-start | bytes 8388608
  41.5 13.3 %copy-start.3 = (u32[32]{0:T(128)S(1)}, u32[32]{0:T(128)}, u32[]{:S(2)}) copy-start(u32[32]{0:T(128)} %constant.18) | copy-start | bytes 388
  41.5 15.2 %copy-start.4 = (s32[128,2]{0,1:T(2,128)S(1)}, s32[128,2]{0,1:T(2,128)}, u32[]{:S(2)}) copy-start(s32[128,2]{0,1:T(2,128)} %param.9) | copy-start | bytes 3076
  41.5 15.2 %copy-start.2 = (s32[128,2]{0,1:T(2,128)S(1)}, s32[128,2]{0,1:T(2,128)}, u32[]{:S(2)}) copy-start(s32[128,2]{0,1:T(2,128)} %param.8) | copy-start | bytes 3076
  54.8 124.1 %reduce-scatter.2.cloned.1.call-start = ((), (), s32[]{:S(2)}) async-start(), calls=%async_computation.1 | async-start | bytes 983040 | tf_op jit(solution)/shard_map/reduce_scatter | solution.py:60
  157.2 23.6 %copy-start.1 = (bf16[128,1536]{1,0:T(8,128)(2,1)S(1)}, bf16[128,1536]{1,0:T(8,128)(2,1)}, u32[]{:S(2)}) copy-start(bf16[128,1536]{1,0:T(8,128)(2,1)} %param.6) | copy-start | bytes 1179652
Sparse Core Ops, SparseCore 0:
  54.9 69.2 all-reduce.4
  156.8 22.0 reduce-scatter.1
where the time goes:
time: 188 us
  waiting for transfers between devices  71.7 us (38%)
  blocking collectives  51.8 us (28%)
  matrix products  41.1 us (22%)
  between operations  15.4 us (8%)
  other arithmetic  6.5 us (3%)
    psum x1, waiting for transfers between devices, per_device(): projected, back_hidden = lax.psum((part_proj, part_back), 'expert')  67.4 us
    unnamed x2, blocking collectives  20.1 us
    all_gather x1, blocking collectives, per_device(): lax.all_gather(send_in, 'dp', axis=0, tiled=True)  16.2 us
    all_gather x1, blocking collectives, per_device(): lax.all_gather(send_grad, 'dp', axis=0, tiled=True)  15.4 us
    dot_general x1, matrix products, per_device(): jnp.einsum('rkh,rd->khd', pre_grad, rows_in, preferred_element_type=jnp.f...  10.7 us
    dot_general x1, matrix products, per_device(): jnp.einsum('rd,khd->rkh', rows_in, weight_in, preferred_element_type=jnp....  10.1 us
    dot_general x1, matrix products, per_device(): jnp.einsum('rkh,khd->rd', pre_grad, weight_in, preferred_element_type=jnp...  7.25 us
    dot_general x1, matrix products, per_device(): jnp.einsum('rh,rd->hd', hidden, out_grad, preferred_element_type=jnp.floa...  6.66 us
  transfers between devices with their start and end apart: 2, of which 2 were waited for; matrix products, arithmetic and copies ran while one was open for 10% of the time, Pallas kernels for 0%

commit v1 on v0

v1 whole, which is shorter than its diff:
```python
import functools

import jax
import jax.numpy as jnp
from jax import lax
from jax.experimental import pallas as pl
from jax.experimental.pallas import tpu as pltpu
from jax.sharding import PartitionSpec as P

F32 = jnp.float32
BF16 = jnp.bfloat16
VMEM = pl.BlockSpec(memory_space=pltpu.VMEM)
SMEM = pl.BlockSpec(memory_space=pltpu.SMEM)
ANY = pl.BlockSpec(memory_space=pl.ANY)
LANES = 128
MIB = 2**20

NT = (((1,), (1,)), ((), ()))
TN = (((0,), (0,)), ((), ()))


def params(mib):
    return pltpu.CompilerParams(vmem_limit_bytes=mib * MIB)


def cost(flops, nbytes):
    return pl.CostEstimate(flops=int(flops), bytes_accessed=int(nbytes), transcendentals=0)


def slot_selector(ids, capacity):
    tok_rows = ids.shape[0]
    routed = jnp.logical_or(ids[:, 0:1] == 0, ids[:, 1:2] == 0)
    row = lax.broadcasted_iota(jnp.int32, (tok_rows, tok_rows), 0)
    col = lax.broadcasted_iota(jnp.int32, (tok_rows, tok_rows), 1)
    before = jnp.where(col < row, 1.0, 0.0).astype(BF16)
    flags = jnp.broadcast_to(jnp.where(routed, 1.0, 0.0), (tok_rows, capacity))
    position = jnp.dot(before, flags.astype(BF16), preferred_element_type=F32)
    slot = lax.broadcasted_iota(jnp.int32, (tok_rows, capacity), 1).astype(F32)
    return jnp.where(position == slot, flags, 0.0)


def select_kernel(tok_ref, cot_ref, ids_ref, quant_ref, in_ref, grad_ref):
    capacity, width = in_ref.shape
    ids = ids_ref[...]
    picker = slot_selector(ids, capacity).astype(BF16)
    scaled = quant_ref[...].astype(F32)
    total = scaled[:, 0:1] + scaled[:, 1:2]
    routing = (scaled / total).astype(BF16).astype(F32)
    weight = jnp.where(ids == 0, routing, 0.0)
    rate = jnp.broadcast_to(weight[:, 0:1] + weight[:, 1:2], (ids.shape[0], LANES)).astype(BF16)
    in_ref[...] = lax.dot_general(picker, tok_ref[...], TN, preferred_element_type=F32).astype(BF16)
    grad_ref[:, :width] = lax.dot_general(
        picker, cot_ref[...], TN, preferred_element_type=F32
    ).astype(BF16)
    grad_ref[:, width:] = lax.dot_general(picker, rate, TN, preferred_element_type=F32).astype(BF16)


def select(tokens, cotangent, expert_ids, quantized):
    capacity, width = tokens.shape[0] // 4, tokens.shape[1]
    return pl.pallas_call(
        select_kernel,
        in_specs=[VMEM] * 4,
        out_specs=[VMEM] * 2,
        out_shape=[
            jax.ShapeDtypeStruct((capacity, width), BF16),
            jax.ShapeDtypeStruct((capacity, width + LANES), BF16),
        ],
        compiler_params=params(8),
        name="select",
    )(tokens, cotangent, expert_ids, quantized)


def project_kernel(nblocks, width, first_ref, *refs):
    blocks, (w_ref, out_ref) = refs[:nblocks], refs[nblocks:]
    kinds = w_ref.shape[0]
    half = out_ref.shape[1] // kinds
    rows = jnp.concatenate([b[:, :width] for b in blocks], axis=0)
    start = pl.multiple_of(first_ref[0], half)
    step = min(half, 512)
    for kind in range(kinds):
        for j in range(0, half, step):
            out_ref[:, kind * half + j : kind * half + j + step] = lax.dot_general(
                rows, w_ref[kind, pl.ds(start + j, step), :], NT, preferred_element_type=F32
            ).astype(out_ref.dtype)


def project(blocks, weight, first, out_type):
    kinds, hidden, width = weight.shape
    half = hidden // 2
    rows = sum(b.shape[0] for b in blocks)
    return pl.pallas_call(
        functools.partial(project_kernel, len(blocks), width),
        in_specs=[SMEM] + [VMEM] * (len(blocks) + 1),
        out_specs=VMEM,
        out_shape=jax.ShapeDtypeStruct((rows, kinds * half), out_type),
        compiler_params=params(24),
        cost_estimate=cost(2 * rows * kinds * half * width, 2 * kinds * half * width),
        name="project",
    )(first, *blocks, weight)


def gated(sums):
    half = sums.shape[1] // 2
    gate, up = sums[:, :half], sums[:, half:]
    return gate, up, jax.nn.sigmoid(gate)


def hidden_kernel(ngroups, nparts, *refs):
    out_ref = refs[-1]
    parts = refs[:-1]
    at = 0
    for g in range(ngroups):
        group = parts[g * nparts : (g + 1) * nparts]
        sums = sum(p[...].astype(F32) for p in group)
        gate, up, s = gated(sums)
        rows = gate.shape[0]
        out_ref[at : at + rows, :] = (gate * s * up).astype(BF16)
        at += rows


def hidden_units(groups):
    half = groups[0][0].shape[1] // 2
    rows = sum(g[0].shape[0] for g in groups)
    flat = [p for g in groups for p in g]
    return pl.pallas_call(
        functools.partial(hidden_kernel, len(groups), len(groups[0])),
        in_specs=[VMEM] * len(flat),
        out_specs=VMEM,
        out_shape=jax.ShapeDtypeStruct((rows, half), BF16),
        compiler_params=params(16),
        name="hidden",
    )(*flat)


def pre_kernel(ngroups, nparts, nblocks, width, *refs):
    gu = refs[: ngroups * nparts]
    back_parts = refs[ngroups * nparts : ngroups * nparts + nparts]
    blocks = refs[ngroups * nparts + nparts : -1]
    out_ref = refs[-1]
    half = back_parts[0].shape[1]
    at = 0
    for g in range(ngroups):
        group = gu[g * nparts : (g + 1) * nparts]
        sums = sum(p[...].astype(F32) for p in group)
        gate, up, s = gated(sums)
        rows = gate.shape[0]
        back = sum(p[at : at + rows, :].astype(F32) for p in back_parts)
        cap = blocks[0].shape[0]
        rate = jnp.concatenate(
            [
                blocks[i][:, width : width + 1].astype(F32)
                for i in range(at // cap, (at + rows) // cap)
            ],
            axis=0,
        )
        hidden = (gate * s * up).astype(BF16).astype(F32)
        route = jnp.sum(hidden * back, axis=1, keepdims=True)
        grad = rate * back
        gate_grad = grad * up * s * (1.0 + gate * (1.0 - s))
        up_grad = grad * gate * s
        out_ref[at : at + rows, :half] = gate_grad.astype(BF16)
        out_ref[at : at + rows, half : 2 * half] = up_grad.astype(BF16)
        out_ref[at : at + rows, 2 * half :] = high_low(route)
        at += rows


def high_low(value):
    high = value.astype(BF16).astype(F32)
    low = value - high
    lane = lax.broadcasted_iota(jnp.int32, (value.shape[0], LANES), 1)
    return jnp.where(lane == 0, high, jnp.where(lane == 1, low, 0.0)).astype(BF16)


def pre_grads(groups, back_parts, blocks, width):
    half = back_parts[0].shape[1]
    rows = back_parts[0].shape[0]
    flat = [p for g in groups for p in g]
    return pl.pallas_call(
        functools.partial(pre_kernel, len(groups), len(groups[0]), len(blocks), width),
        in_specs=[VMEM] * (len(flat) + len(back_parts) + len(blocks)),
        out_specs=VMEM,
        out_shape=jax.ShapeDtypeStruct((rows, 2 * half + LANES), BF16),
        compiler_params=params(16),
        name="pre",
    )(*flat, *back_parts, *blocks)


def row_own_kernel(first_ref, pre_ref, w_ref, out_ref):
    half = (pre_ref.shape[1] - LANES) // 2
    start = pl.multiple_of(first_ref[0], half)
    out_ref[...] = jnp.dot(
        pre_ref[:, :half], w_ref[0, pl.ds(start, half), :], preferred_element_type=F32
    ) + jnp.dot(
        pre_ref[:, half : 2 * half], w_ref[1, pl.ds(start, half), :], preferred_element_type=F32
    )


def row_own(pre, weight, first):
    rows, width = pre.shape[0], weight.shape[2]
    return pl.pallas_call(
        row_own_kernel,
        in_specs=[SMEM, VMEM, VMEM],
        out_specs=VMEM,
        out_shape=jax.ShapeDtypeStruct((rows, width), F32),
        compiler_params=params(24),
        cost_estimate=cost(2 * rows * weight.shape[1] * width, 2 * weight.shape[1] * width),
        name="row_own",
    )(first, pre, weight)


def row_rest_kernel(first_ref, own_ref, mine_ref, pre_ref, w_ref, *out_refs):
    half = (pre_ref.shape[1] - LANES) // 2
    width = own_ref.shape[1]
    start = pl.multiple_of(first_ref[0], half)
    total = (
        own_ref[...]
        + jnp.dot(pre_ref[:, :half], w_ref[0, pl.ds(start, half), :], preferred_element_type=F32)
        + jnp.dot(
            pre_ref[:, half : 2 * half], w_ref[1, pl.ds(start, half), :], preferred_element_type=F32
        )
    )
    lanes = mine_ref[:, 2 * half :].astype(F32) + pre_ref[:, 2 * half :].astype(F32)
    route = lanes[:, 0:1] + lanes[:, 1:2]
    at = 0
    for out in out_refs:
        rows = out.shape[0]
        out[:, :width] = total[at : at + rows].astype(out.dtype)
        if out.dtype == F32:
            out[:, width:] = jnp.broadcast_to(route[at : at + rows], (rows, LANES)) * jnp.where(
                lax.broadcasted_iota(jnp.int32, (rows, LANES), 1) == 0, 1.0, 0.0
            )
        else:
            out[:, width:] = high_low(route[at : at + rows])
        at += rows


def row_rest(own, mine, pre, weight, first, outs):
    rows, width = own.shape
    return pl.pallas_call(
        row_rest_kernel,
        in_specs=[SMEM] + [VMEM] * 4,
        out_specs=[VMEM] * len(outs),
        out_shape=[jax.ShapeDtypeStruct((n, width + LANES), kind) for n, kind in outs],
        compiler_params=params(24),
        cost_estimate=cost(2 * rows * weight.shape[1] * width, 2 * weight.shape[1] * width),
        name="row_rest",
    )(first, own, mine, pre, weight)


def write_tiles(tiles, make, out_at, buf, sem):
    ring = buf.shape[0]
    copies = []
    for i, tile in enumerate(tiles):
        slot = i % ring
        if i >= ring:
            copies[i - ring].wait()
        buf[slot] = make(tile)
        copy = pltpu.make_async_copy(buf.at[slot], out_at(tile), sem.at[slot])
        copy.start()
        copies.append(copy)
    for copy in copies[max(0, len(copies) - ring) :]:
        copy.wait()


def grad_out_kernel(nblocks, first_ref, mine_ref, peer_ref, *refs):
    blocks = refs[:nblocks]
    out_ref, cot, buf, sem = refs[nblocks:]
    width = out_ref.shape[1]
    half = mine_ref.shape[1]
    step = buf.shape[1]
    at = 0
    for b in blocks:
        rows = b.shape[0]
        cot[at : at + rows, :] = (
            b[:, width : width + 1].astype(F32) * b[:, :width].astype(F32)
        ).astype(BF16)
        at += rows
    starts = (pl.multiple_of(first_ref[0], half), pl.multiple_of(first_ref[1], half))
    sources = (mine_ref, peer_ref)
    tiles = [(s, j) for s in range(2) for j in range(0, half, step)]

    def make(tile):
        s, j = tile
        return lax.dot_general(
            sources[s][:, j : j + step], cot[...], TN, preferred_element_type=F32
        )

    def out_at(tile):
        s, j = tile
        return out_ref.at[pl.ds(starts[s] + j, step)]

    write_tiles(tiles, make, out_at, buf, sem)


def grad_out(mine, peer, blocks, firsts, width):
    rows, half = mine.shape
    step = min(half, 256)
    ring = min(8, 2 * half // step)
    return pl.pallas_call(
        functools.partial(grad_out_kernel, len(blocks)),
        in_specs=[SMEM] + [VMEM] * (2 + len(blocks)),
        out_specs=ANY,
        out_shape=jax.ShapeDtypeStruct((2 * half, width), F32),
        scratch_shapes=[
            pltpu.VMEM((rows, width), BF16),
            pltpu.VMEM((ring, step, width), F32),
            pltpu.SemaphoreType.DMA((ring,)),
        ],
        compiler_params=params(28),
        cost_estimate=cost(4 * rows * half * width, 8 * half * width),
        name="grad_out",
    )(firsts, mine, peer, *blocks)


def grad_in_kernel(nblocks, first_ref, mine_ref, peer_ref, *refs):
    blocks = refs[:nblocks]
    out_ref, tok, buf, sem = refs[nblocks:]
    half = (mine_ref.shape[1] - LANES) // 2
    step = buf.shape[1]
    at = 0
    for b in blocks:
        rows = b.shape[0]
        tok[at : at + rows, :] = b[...]
        at += rows
    starts = (pl.multiple_of(first_ref[0], half), pl.multiple_of(first_ref[1], half))
    sources = (mine_ref, peer_ref)
    tiles = [(s, c, j) for s in range(2) for c in range(2) for j in range(0, half, step)]

    def make(tile):
        s, c, j = tile
        at = c * half + j
        return lax.dot_general(
            sources[s][:, at : at + step], tok[...], TN, preferred_element_type=F32
        )

    def out_at(tile):
        s, c, j = tile
        return out_ref.at[c, pl.ds(starts[s] + j, step)]

    write_tiles(tiles, make, out_at, buf, sem)


def grad_in(mine, peer, blocks, firsts, width):
    rows = mine.shape[0]
    half = (mine.shape[1] - LANES) // 2
    step = min(half, 256)
    ring = min(8, 4 * half // step)
    return pl.pallas_call(
        functools.partial(grad_in_kernel, len(blocks)),
        in_specs=[SMEM] + [VMEM] * (2 + len(blocks)),
        out_specs=ANY,
        out_shape=jax.ShapeDtypeStruct((2, 2 * half, width), F32),
        scratch_shapes=[
            pltpu.VMEM((rows, width), BF16),
            pltpu.VMEM((ring, step, width), F32),
            pltpu.SemaphoreType.DMA((ring,)),
        ],
        compiler_params=params(28),
        cost_estimate=cost(8 * rows * half * width, 16 * half * width),
        name="grad_in",
    )(firsts, mine, peer, *blocks)


def place_kernel(nblocks, ids_ref, *refs):
    blocks, (in_ref, weight_ref) = refs[:nblocks], refs[nblocks:]
    width = in_ref.shape[1]
    capacity = blocks[0].shape[0]
    total = sum(b[:, :width].astype(F32) for b in blocks)
    lanes = sum(b[:, width:].astype(F32) for b in blocks)
    ids = ids_ref[...]
    picker = slot_selector(ids, capacity).astype(BF16)
    in_ref[...] = jnp.dot(picker, total.astype(BF16), preferred_element_type=F32).astype(BF16)
    route = jnp.broadcast_to(lanes[:, 0:1] + lanes[:, 1:2], (capacity, LANES))
    high = route.astype(BF16)
    low = (route - high.astype(F32)).astype(BF16)
    spread = jnp.dot(picker, high, preferred_element_type=F32) + jnp.dot(
        picker, low, preferred_element_type=F32
    )
    weight_ref[...] = jnp.where(ids == 0, spread[:, : ids.shape[1]], 0.0).astype(BF16)


def place(expert_ids, blocks):
    tok_rows = expert_ids.shape[0]
    width = blocks[0].shape[1] - LANES
    return pl.pallas_call(
        functools.partial(place_kernel, len(blocks)),
        in_specs=[VMEM] * (1 + len(blocks)),
        out_specs=[VMEM] * 2,
        out_shape=[
            jax.ShapeDtypeStruct((tok_rows, width), BF16),
            jax.ShapeDtypeStruct(expert_ids.shape, BF16),
        ],
        compiler_params=params(8),
        name="place",
    )(expert_ids, *blocks)


def swap(array, axis, size, distance):
    return lax.ppermute(array, axis, [(i, i ^ distance) for i in range(size)])


def per_device(dp, chips, tokens, cotangent, expert_ids, quantized, weight_in, weight_out):
    experts = 2 * chips
    width = tokens.shape[1]
    hidden = weight_in.shape[1]
    half = hidden // 2
    core = lax.rem(lax.axis_index("expert"), 2)
    own = (core * half).astype(jnp.int32).reshape(1)
    other = ((1 - core) * half).astype(jnp.int32).reshape(1)
    firsts = jnp.concatenate([own, other])
    direct = dp == 4

    weight_out = weight_out.reshape((1,) + weight_out.shape)
    send_in, send_grad = select(tokens, cotangent, expert_ids, quantized)
    if direct:
        tok_blocks = [send_in] + [swap(send_in, "dp", dp, d) for d in range(1, dp)]
        cot_blocks = [send_grad] + [swap(send_grad, "dp", dp, d) for d in range(1, dp)]
        groups = [tok_blocks[:2], tok_blocks[2:]]
    else:
        tok_blocks = [lax.all_gather(send_in, "dp", axis=0, tiled=True)]
        cot_blocks = [lax.all_gather(send_grad, "dp", axis=0, tiled=True)]
        groups = [tok_blocks]

    weight_in = pltpu.with_memory_space_constraint(weight_in, pltpu.VMEM)
    weight_out = pltpu.with_memory_space_constraint(weight_out, pltpu.VMEM)

    def summed(blocks, weight):
        theirs = project(blocks, weight, other, BF16)
        arrived = swap(theirs, "expert", experts, 1)
        mine = project(blocks, weight, own, F32)
        chip = (mine + arrived.astype(F32)).astype(BF16)
        return [chip] + [swap(chip, "expert", experts, 2 * k) for k in range(1, chips)]

    gu = [summed(blocks, weight_in) for blocks in groups]
    back = summed(cot_blocks, weight_out)

    units = hidden_units(gu)
    units_peer = swap(units, "expert", experts, 1)
    grad_weight_out = grad_out(units, units_peer, cot_blocks, firsts, width)

    pre = pre_grads(gu, back, cot_blocks, width)
    pre_peer = swap(pre, "expert", experts, 1)
    part = row_own(pre, weight_in, own)
    if direct:
        cap = send_in.shape[0]
        outs = [(cap, F32)] + [(cap, BF16)] * (dp - 1)
        sent = row_rest(part, pre, pre_peer, weight_in, other, outs)
        arrived = [sent[0]] + [swap(sent[d], "dp", dp, d) for d in range(1, dp)]
    else:
        sent = row_rest(part, pre, pre_peer, weight_in, other, [(part.shape[0], F32)])
        arrived = [lax.psum_scatter(sent[0], "dp", scatter_dimension=0, tiled=True)]
    grad_weight_in = grad_in(pre, pre_peer, tok_blocks, firsts, width)
    input_grad, weight_grad = place(expert_ids, arrived)
    return (input_grad, weight_grad, grad_weight_in, grad_weight_out)


def solution(mesh):
    return jax.shard_map(
        functools.partial(per_device, mesh.shape["dp"], mesh.shape["expert"] // 2),
        mesh=mesh,
        in_specs=(
            P(("group", "dp"), "expert"),
            P(("group", "dp"), "expert"),
            P(("group", "dp"), None),
            P(("group", "dp"), None),
            P(None, "dp", "expert"),
            P("dp", "expert"),
        ),
        out_specs=(
            P(("group", "dp"), "expert"),
            P(("group", "dp"), None),
            P("group", "dp", "expert"),
            P(("group", "dp"), "expert"),
        ),
        check_vma=False,
    )
```

time: 188 us -> 84.2 us (0.45)
  waiting for transfers between devices: 71.7 us -> 16.9 us
  blocking collectives: 51.8 us -> 0 us
  matrix products: 41.1 us -> 0 us
  Pallas kernels: 0 us -> 29.9 us
  starting transfers between devices: 0.08 us -> 20.2 us
  local copies, waits for them, and re-layouts: 1.07 us -> 15.8 us
  between operations: 15.4 us -> 0.89 us
  other arithmetic: 6.5 us -> 0.27 us
    psum x1 -> x0, waiting for transfers between devices: 67.4 us -> none  [per_device(): projected, back_hidden = lax.psum((part_proj, part_back), 'expert')]
    dot_general x8 -> x0, matrix products: 41.1 us -> none  [the longest x1 10.7 us: per_device(): jnp.einsum('rkh,rd->khd', pre_grad, rows_in, preferred_element_type=jnp.f...]
    all_gather x2 -> x0, blocking collectives: 31.7 us -> none  [the longest x1 16.2 us: per_device(): lax.all_gather(send_in, 'dp', axis=0, tiled=True)]
    pallas_call x0 -> x14, Pallas kernels: none -> 29.9 us  [the longest x6 10.3 us: project(): pl.pallas_call(functools.partial(project_kernel, len(blocks), width), in_...]
    ppermute x0 -> x17, starting transfers between devices: none -> 20.2 us  [swap(): return lax.ppermute(array, axis, [(i, i ^ distance) for i in range(size)])]
    unnamed x2 -> x0, blocking collectives: 20.1 us -> none
    ppermute x0 -> x17, waiting for transfers between devices: none -> 16.9 us  [swap(): return lax.ppermute(array, axis, [(i, i ^ distance) for i in range(size)])]
    unnamed x18 -> x17, local copies, waits for them, and re-layouts: 0.95 us -> 15.8 us
  transfers between devices with their start and end apart: 2 -> 17, of which waited for: 2 -> 5; matrix products, arithmetic and copies ran while one was open for 10% -> 0% of each run, Pallas kernels for 0% -> 32%
where the time goes in v1:
time: 84.2 us; the launch traced here: 83.9 us
  Pallas kernels  29.9 us (36%)
  starting transfers between devices  20.2 us (24%)
  waiting for transfers between devices  16.9 us (20%)
  local copies, waits for them, and re-layouts  15.8 us (19%)
  between operations  0.89 us (1%)
    ppermute x17, starting transfers between devices, swap(): return lax.ppermute(array, axis, [(i, i ^ distance) for i in range(size)])  20.2 us
    ppermute x17, waiting for transfers between devices, swap(): return lax.ppermute(array, axis, [(i, i ^ distance) for i in range(size)])  16.9 us
    unnamed x17, local copies, waits for them, and re-layouts  15.8 us
    pallas_call x6, Pallas kernels, project(): pl.pallas_call(functools.partial(project_kernel, len(blocks), width), in_...  10.3 us
    pallas_call x1, Pallas kernels, grad_in(): pl.pallas_call(functools.partial(grad_in_kernel, len(blocks)), in_specs=[...  9.37 us
    pallas_call x1, Pallas kernels, grad_out(): pl.pallas_call(functools.partial(grad_out_kernel, len(blocks)), in_specs=...  5.65 us
  transfers between devices with their start and end apart: 17, of which 5 were waited for; matrix products, arithmetic and copies ran while one was open for 0% of the time, Pallas kernels for 32%

profile of v1, /device:TPU:0, one launch (start us, length us, event | category | flops | bytes accessed | tf_op | source)
XLA Modules:
  0.0 83.9 jit_solution(12976876301620002729)
XLA Ops:
  0.6 0.8 copy.12.ids_ref
  1.4 0.8 copy.11.quant_ref
  2.2 1.0 %copy-done.3 = bf16[128,1536]{1,0:T(8,128)(2,1)S(1)} copy-done((bf16[128,1536]{1,0:T(8,128)(2,1)S(1)}, bf16[128,1536]{1,0:T(8,128)(2,1)}, u32[]{:S(2)}) %copy-start.3) | copy-done | bytes 393240
  3.2 1.0 %copy-done.4 = bf16[128,1536]{1,0:T(8,128)(2,1)S(1)} copy-done((bf16[128,1536]{1,0:T(8,128)(2,1)S(1)}, bf16[128,1536]{1,0:T(8,128)(2,1)}, u32[]{:S(2)}) %copy-start.4) | copy-done | bytes 393240
  4.2 0.6 select.3
  4.8 3.1 %collective-permute-start = (bf16[32,1536]{1,0:T(8,128)(2,1)S(1)}, bf16[32,1536]{1,0:T(8,128)(2,1)S(1)}, u32[]{:S(2)}, u32[]{:S(2)}) collective-permute-start(bf16[32,1536]{1,0:T(8,128)(2,1)S(1)} %get-tuple-element.12.refs_0_), channel_id=1, source_target_pairs={{0,4},{4,0},{8,12},{12,8},{1,5},{5,1},{9,13},{13,9},{2,6},{6,2},{1... | collective-permute-start | bytes 294920 | tf_op jit(solution)/shard_map/ppermute | solution.py:399
  7.8 2.6 %collective-permute-start.3 = (bf16[32,1536]{1,0:T(8,128)(2,1)S(1)}, bf16[32,1536]{1,0:T(8,128)(2,1)S(1)}, u32[]{:S(2)}, u32[]{:S(2)}) collective-permute-start(bf16[32,1536]{1,0:T(8,128)(2,1)S(1)} %get-tuple-element.12.refs_0_), channel_id=1, source_target_pairs={{0,8},{4,12},{8,0},{12,4},{1,9},{5,13},{9,1},{13,5},{2,10},{6,14},... | collective-permute-start | bytes 294920 | tf_op jit(solution)/shard_map/ppermute | solution.py:399
  10.4 0.2 collective-permute-done.refs_1_
  10.6 4.6 %copy-done = bf16[2,2048,1536]{2,1,0:T(8,128)(2,1)S(1)} copy-done((bf16[2,2048,1536]{2,1,0:T(8,128)(2,1)S(1)}, bf16[2,2048,1536]{2,1,0:T(8,128)(2,1)}, u32[]{:S(2)}) %copy-start) | copy-done | bytes 12582936
  15.2 2.0 %project.7 = bf16[64,2048]{1,0:T(8,128)(2,1)S(1)} custom-call(s32[1]{0:T(128)} %bitcast.first_ref, bf16[32,1536]{1,0:T(8,128)(2,1)S(1)} %get-tuple-element.12.refs_0_, bf16[32,1536]{1,0:T(8,128)(2,1)S(1)} %collective-permute-done.refs_1_, bf16[2,2048,1536]{2,1,0:T(8,128)(2,1)S(1)} %copy-done), custom_call_target="tpu_custom_call" | custom-call | flops 402653184 | bytes 6291456 | tf_op jit(solution)/shard_map/project/pallas_call | solution.py:91
  17.2 0.1 collective-permute-start.1
  17.3 1.9 %collective-permute-start.7 = (bf16[32,1664]{1,0:T(8,128)(2,1)S(1)}, bf16[32,1664]{1,0:T(8,128)(2,1)S(1)}, u32[]{:S(2)}, u32[]{:S(2)}) collective-permute-start(bf16[32,1664]{1,0:T(8,128)(2,1)S(1)} %get-tuple-element.13.refs_0_.refs_6_), channel_id=1, source_target_pairs={{0,4},{4,0},{8,12},{12,8},{1,5},{5,1},{9,13},{13,9},{2,6},{6,2},{1... | collective-permute-start | bytes 319496 | tf_op jit(solution)/shard_map/ppermute | solution.py:399
  19.2 3.6 %collective-permute-start.8 = (bf16[32,1664]{1,0:T(8,128)(2,1)S(1)}, bf16[32,1664]{1,0:T(8,128)(2,1)S(1)}, u32[]{:S(2)}, u32[]{:S(2)}) collective-permute-start(bf16[32,1664]{1,0:T(8,128)(2,1)S(1)} %get-tuple-element.13.refs_0_.refs_6_), channel_id=1, source_target_pairs={{0,8},{4,12},{8,0},{12,4},{1,9},{5,13},{9,1},{13,5},{2,10},{6,14},... | collective-permute-start | bytes 319496 | tf_op jit(solution)/shard_map/ppermute | solution.py:399
  22.8 0.0 collective-permute-done.4.refs_1_.refs_3_
  22.8 0.0 copy-start.1
  22.8 4.6 %copy-done.1 = bf16[2,2048,1536]{2,1,0:T(8,128)(2,1)S(1)} copy-done((bf16[2,2048,1536]{2,1,0:T(8,128)(2,1)S(1)}, bf16[2,2048,1536]{2,1,0:T(8,128)(2,1)}, u32[]{:S(2)}) %copy-start.1) | copy-done | bytes 12582936
  27.3 2.0 %project.9 = bf16[64,2048]{1,0:T(8,128)(2,1)S(1)} custom-call(s32[1]{0:T(128)} %bitcast.first_ref, bf16[32,1536]{1,0:T(8,128)(2,1)S(1)} %collective-permute-done.3.refs_0_.refs_2_, bf16[32,1536]{1,0:T(8,128)(2,1)S(1)} %collective-permute-done.4.refs_1_.refs_3_, bf16[2,2048,1536]{2,1,0:T(8,128)(2,1)S(1)} %copy-done.1), custom_call_target="tpu_custom_call" | custom-call | flops 402653184 | bytes 6291456 | tf_op jit(solution)/shard_map/project/pallas_call | solution.py:91
  29.3 0.1 collective-permute-start.5
  29.4 2.5 %copy-done.2 = bf16[2,2048,1536]{2,1,0:T(8,128)(2,1)S(1)} copy-done((bf16[2,2048,1536]{2,1,0:T(8,128)(2,1)S(1)}, bf16[2,2048,1536]{2,1,0:T(8,128)(2,1)}, u32[]{:S(2)}) %copy-start.2) | copy-done | bytes 12582936
  31.9 2.0 %project.6 = f32[64,2048]{1,0:T(8,128)S(1)} custom-call(s32[1]{0:T(128)} %bitcast.1.first_ref, bf16[32,1536]{1,0:T(8,128)(2,1)S(1)} %get-tuple-element.12.refs_0_, bf16[32,1536]{1,0:T(8,128)(2,1)S(1)} %collective-permute-done.refs_1_, bf16[2,2048,1536]{2,1,0:T(8,128)(2,1)S(1)} %copy-done.2), custom_call_target="tpu_custom_call" | custom-call | flops 402653184 | bytes 6291456 | tf_op jit(solution)/shard_map/project/pallas_call | solution.py:91
  33.9 0.0 slice-start.1
  33.9 2.0 %project.8 = f32[64,2048]{1,0:T(8,128)S(1)} custom-call(s32[1]{0:T(128)} %bitcast.1.first_ref, bf16[32,1536]{1,0:T(8,128)(2,1)S(1)} %collective-permute-done.3.refs_0_.refs_2_, bf16[32,1536]{1,0:T(8,128)(2,1)S(1)} %collective-permute-done.4.refs_1_.refs_3_, bf16[2,2048,1536]{2,1,0:T(8,128)(2,1)S(1)} %copy-done.2), custom_call_target="tpu_custom_call" | custom-call | flops 402653184 | bytes 6291456 | tf_op jit(solution)/shard_map/project/pallas_call | solution.py:91
  36.0 1.2 %project.11 = bf16[128,1024]{1,0:T(8,128)(2,1)S(1)} custom-call(s32[1]{0:T(128)} %bitcast.first_ref, bf16[32,1664]{1,0:T(8,128)(2,1)S(1)} %get-tuple-element.13.refs_0_.refs_6_, bf16[32,1664]{1,0:T(8,128)(2,1)S(1)} %collective-permute-done.7.refs_1_.refs_7_, bf16[32,1664]{1,0:T(8,128)(2,1)S(1)} %collective-permute-done.8.refs_2_.refs_8_, ...), custom_call_target="tpu_custom_call" | custom-call | flops 402653184 | bytes 3145728 | tf_op jit(solution)/shard_map/project/pallas_call | solution.py:91
  37.2 0.1 collective-permute-start.10
  37.2 1.2 %project.10 = f32[128,1024]{1,0:T(8,128)S(1)} custom-call(s32[1]{0:T(128)} %bitcast.1.first_ref, bf16[32,1664]{1,0:T(8,128)(2,1)S(1)} %get-tuple-element.13.refs_0_.refs_6_, bf16[32,1664]{1,0:T(8,128)(2,1)S(1)} %collective-permute-done.7.refs_1_.refs_7_, bf16[32,1664]{1,0:T(8,128)(2,1)S(1)} %collective-permute-done.8.refs_2_.refs_8_, ...), custom_call_target="tpu_custom_call" | custom-call | flops 402653184 | bytes 3145728 | tf_op jit(solution)/shard_map/project/pallas_call | solution.py:91
  38.4 0.1 add_convert_fusion.2.refs_0_
  38.5 1.5 %collective-permute-start.2 = (bf16[64,2048]{1,0:T(8,128)(2,1)S(1)}, bf16[64,2048]{1,0:T(8,128)(2,1)S(1)}, u32[]{:S(2)}, u32[]{:S(2)}) collective-permute-start(bf16[64,2048]{1,0:T(8,128)(2,1)S(1)} %add_convert_fusion.2.refs_0_), channel_id=1, source_target_pairs={{0,2},{1,3},{2,0},{3,1},{4,6},{5,7},{6,4},{7,5},{8,10},{9,11},{10,... | collective-permute-start | bytes 786440 | tf_op jit(solution)/shard_map/ppermute | solution.py:399
  40.0 0.1 add_convert_fusion.1.refs_2_
  40.1 0.6 collective-permute-start.6
  40.7 0.1 add_convert_fusion.refs_4_
  40.8 1.5 %collective-permute-start.11 = (bf16[128,1024]{1,0:T(8,128)(2,1)S(1)}, bf16[128,1024]{1,0:T(8,128)(2,1)S(1)}, u32[]{:S(2)}, u32[]{:S(2)}) collective-permute-start(bf16[128,1024]{1,0:T(8,128)(2,1)S(1)} %add_convert_fusion.refs_4_), channel_id=1, source_target_pairs={{0,2},{1,3},{2,0},{3,1},{4,6},{5,7},{6,4},{7,5},{8,10},{9,11},{10,... | collective-permute-start | bytes 786440 | tf_op jit(solution)/shard_map/ppermute | solution.py:399
  42.3 5.3 %collective-permute-done.2.refs_1_ = bf16[64,2048]{1,0:T(8,128)(2,1)S(1)} collective-permute-done((bf16[64,2048]{1,0:T(8,128)(2,1)S(1)}, bf16[64,2048]{1,0:T(8,128)(2,1)S(1)}, u32[]{:S(2)}, u32[]{:S(2)}) %collective-permute-start.2) | collective-permute-done | bytes 262176 | tf_op jit(solution)/shard_map/ppermute | solution.py:399
  47.7 5.6 %collective-permute-done.6.refs_3_ = bf16[64,2048]{1,0:T(8,128)(2,1)S(1)} collective-permute-done((bf16[64,2048]{1,0:T(8,128)(2,1)S(1)}, bf16[64,2048]{1,0:T(8,128)(2,1)S(1)}, u32[]{:S(2)}, u32[]{:S(2)}) %collective-permute-start.6) | collective-permute-done | bytes 262176 | tf_op jit(solution)/shard_map/ppermute | solution.py:399
  53.3 5.2 %collective-permute-done.11.refs_5_ = bf16[128,1024]{1,0:T(8,128)(2,1)S(1)} collective-permute-done((bf16[128,1024]{1,0:T(8,128)(2,1)S(1)}, bf16[128,1024]{1,0:T(8,128)(2,1)S(1)}, u32[]{:S(2)}, u32[]{:S(2)}) %collective-permute-start.11) | collective-permute-done | bytes 262176 | tf_op jit(solution)/shard_map/ppermute | solution.py:399
  58.5 0.6 pre.1.pre_ref.mine_ref
  59.1 0.1 collective-permute-start.12
  59.1 0.2 hidden.1.mine_ref
  59.3 0.6 collective-permute-start.16
  59.9 0.1 pad_add_fusion.first_ref
  60.0 1.0 %row_own.1.own_ref = f32[128,1536]{1,0:T(8,128)S(1)} custom-call(s32[1]{0:T(128)} %bitcast.1.first_ref, bf16[128,2176]{1,0:T(8,128)(2,1)S(1)} %pre.1.pre_ref.mine_ref, bf16[2,2048,1536]{2,1,0:T(8,128)(2,1)S(1)} %copy-done.2), custom_call_target="tpu_custom_call" | custom-call | flops 805306368 | bytes 6291456 | tf_op jit(solution)/shard_map/row_own/pallas_call | solution.py:200
  61.0 0.5 collective-permute-done.16.peer_ref
  61.5 5.6 %grad_out.1 = f32[2048,1536]{1,0:T(8,128)} custom-call(s32[2]{0:T(128)S(1)} %pad_add_fusion.first_ref, bf16[128,1024]{1,0:T(8,128)(2,1)S(1)} %hidden.1.mine_ref, bf16[128,1024]{1,0:T(8,128)(2,1)S(1)} %collective-permute-done.16.peer_ref, bf16[32,1664]{1,0:T(8,128)(2,1)S(1)} %get-tuple-element.13.refs_0_.refs_6_, ...), custom_call_target="tpu_custom_call" | custom-call | flops 805306368 | bytes 12582912 | tf_op jit(solution)/shard_map/grad_out/pallas_call | solution.py:299
  67.1 1.0 %row_rest.1 = (f32[32,1664]{1,0:T(8,128)S(1)}, bf16[32,1664]{1,0:T(8,128)(2,1)S(1)}, bf16[32,1664]{1,0:T(8,128)(2,1)S(1)}, bf16[32,1664]{1,0:T(8,128)(2,1)S(1)}) custom-call(s32[1]{0:T(128)} %bitcast.first_ref, f32[128,1536]{1,0:T(8,128)S(1)} %row_own.1.own_ref, bf16[128,2176]{1,0:T(8,128)(2,1)S(1)} %pre.1.pre_ref.mine_ref, ...), custom_call_target="tpu_custom_call" | custom-call | flops 805306368 | bytes 6291456 | tf_op jit(solution)/shard_map/row_rest/pallas_call | solution.py:239
  68.1 0.6 collective-permute-start.13
  68.8 3.8 %collective-permute-start.14 = (bf16[32,1664]{1,0:T(8,128)(2,1)S(1)}, bf16[32,1664]{1,0:T(8,128)(2,1)S(1)}, u32[]{:S(2)}, u32[]{:S(2)}) collective-permute-start(bf16[32,1664]{1,0:T(8,128)(2,1)S(1)} %get-tuple-element.16), channel_id=1, source_target_pairs={{0,8},{4,12},{8,0},{12,4},{1,9},{5,13},{9,1},{13,5},{2,10},{6,14},... | collective-permute-start | bytes 319496 | tf_op jit(solution)/shard_map/ppermute | solution.py:399
  72.6 9.4 %grad_in.1 = f32[2,2048,1536]{2,1,0:T(8,128)} custom-call(s32[2]{0:T(128)S(1)} %pad_add_fusion.first_ref, bf16[128,2176]{1,0:T(8,128)(2,1)S(1)} %pre.1.pre_ref.mine_ref, bf16[128,2176]{1,0:T(8,128)(2,1)S(1)} %collective-permute-done.12.pre_ref.peer_ref, bf16[32,1536]{1,0:T(8,128)(2,1)S(1)} %get-tuple-element.12.refs_0_, ...), custom_call_target="tpu_custom_call" | custom-call | flops 1610612736 | bytes 25165824 | tf_op jit(solution)/shard_map/grad_in/pallas_call | solution.py:348
  82.0 1.3 %place.1 = (bf16[128,1536]{1,0:T(8,128)(2,1)}, bf16[128,2]{1,0:T(8,128)(2,1)S(1)}) custom-call(s32[128,2]{1,0:T(8,128)S(1)} %copy.12.ids_ref, f32[32,1664]{1,0:T(8,128)S(1)} %get-tuple-element.14.refs_0_, bf16[32,1664]{1,0:T(8,128)(2,1)S(1)} %collective-permute-done.13.refs_1_, bf16[32,1664]{1,0:T(8,128)(2,1)S(1)} %collective-permute-done.14.refs_2_, ...), custom_call_target="tpu_custom_call" | custom-call | tf_op jit(solution)/shard_map/place/pallas_call | solution.py:385
  83.3 0.6 copy.13
  (22 shorter events, 0.0 us)
Async XLA Ops:
  2.2 1.0 %copy-start.3 = (bf16[128,1536]{1,0:T(8,128)(2,1)S(1)}, bf16[128,1536]{1,0:T(8,128)(2,1)}, u32[]{:S(2)}) copy-start(bf16[128,1536]{1,0:T(8,128)(2,1)} %tok_ref.1) | copy-start | bytes 1179652
  3.2 1.0 %copy-start.4 = (bf16[128,1536]{1,0:T(8,128)(2,1)S(1)}, bf16[128,1536]{1,0:T(8,128)(2,1)}, u32[]{:S(2)}) copy-start(bf16[128,1536]{1,0:T(8,128)(2,1)} %cot_ref.1) | copy-start | bytes 1179652
  4.8 5.9 %collective-permute-start = (bf16[32,1536]{1,0:T(8,128)(2,1)S(1)}, bf16[32,1536]{1,0:T(8,128)(2,1)S(1)}, u32[]{:S(2)}, u32[]{:S(2)}) collective-permute-start(bf16[32,1536]{1,0:T(8,128)(2,1)S(1)} %get-tuple-element.12.refs_0_), channel_id=1, source_target_pairs={{0,4},{4,0},{8,12},{12,8},{1,5},{5,1},{9,13},{13,9},{2,6},{6,2},{1... | collective-permute-start | bytes 294920 | tf_op jit(solution)/shard_map/ppermute | solution.py:399
  7.8 14.9 %collective-permute-start.3 = (bf16[32,1536]{1,0:T(8,128)(2,1)S(1)}, bf16[32,1536]{1,0:T(8,128)(2,1)S(1)}, u32[]{:S(2)}, u32[]{:S(2)}) collective-permute-start(bf16[32,1536]{1,0:T(8,128)(2,1)S(1)} %get-tuple-element.12.refs_0_), channel_id=1, source_target_pairs={{0,8},{4,12},{8,0},{12,4},{1,9},{5,13},{9,1},{13,5},{2,10},{6,14},... | collective-permute-start | bytes 294920 | tf_op jit(solution)/shard_map/ppermute | solution.py:399
  10.4 12.3 %collective-permute-start.4 = (bf16[32,1536]{1,0:T(8,128)(2,1)S(1)}, bf16[32,1536]{1,0:T(8,128)(2,1)S(1)}, u32[]{:S(2)}, u32[]{:S(2)}) collective-permute-start(bf16[32,1536]{1,0:T(8,128)(2,1)S(1)} %get-tuple-element.12.refs_0_), channel_id=1, source_target_pairs={{0,12},{4,8},{8,4},{12,0},{1,13},{5,9},{9,5},{13,1},{2,14},{6,10},... | collective-permute-start | bytes 294920 | tf_op jit(solution)/shard_map/ppermute | solution.py:399
  10.6 4.6 %copy-start = (bf16[2,2048,1536]{2,1,0:T(8,128)(2,1)S(1)}, bf16[2,2048,1536]{2,1,0:T(8,128)(2,1)}, u32[]{:S(2)}) copy-start(bf16[2,2048,1536]{2,1,0:T(8,128)(2,1)} %w_ref.3) | copy-start | bytes 37748740
  17.2 21.2 %collective-permute-start.1 = (bf16[64,2048]{1,0:T(8,128)(2,1)S(1)}, bf16[64,2048]{1,0:T(8,128)(2,1)S(1)}, u32[]{:S(2)}, u32[]{:S(2)}) collective-permute-start(bf16[64,2048]{1,0:T(8,128)(2,1)S(1)} %project.7), channel_id=1, source_target_pairs={{0,1},{1,0},{2,3},{3,2},{4,5},{5,4},{6,7},{7,6},{8,9},{9,8},{10,11... | collective-permute-start | bytes 786440 | tf_op jit(solution)/shard_map/ppermute | solution.py:399
  17.3 18.7 %collective-permute-start.7 = (bf16[32,1664]{1,0:T(8,128)(2,1)S(1)}, bf16[32,1664]{1,0:T(8,128)(2,1)S(1)}, u32[]{:S(2)}, u32[]{:S(2)}) collective-permute-start(bf16[32,1664]{1,0:T(8,128)(2,1)S(1)} %get-tuple-element.13.refs_0_.refs_6_), channel_id=1, source_target_pairs={{0,4},{4,0},{8,12},{12,8},{1,5},{5,1},{9,13},{13,9},{2,6},{6,2},{1... | collective-permute-start | bytes 319496 | tf_op jit(solution)/shard_map/ppermute | solution.py:399
  19.2 16.8 %collective-permute-start.8 = (bf16[32,1664]{1,0:T(8,128)(2,1)S(1)}, bf16[32,1664]{1,0:T(8,128)(2,1)S(1)}, u32[]{:S(2)}, u32[]{:S(2)}) collective-permute-start(bf16[32,1664]{1,0:T(8,128)(2,1)S(1)} %get-tuple-element.13.refs_0_.refs_6_), channel_id=1, source_target_pairs={{0,8},{4,12},{8,0},{12,4},{1,9},{5,13},{9,1},{13,5},{2,10},{6,14},... | collective-permute-start | bytes 319496 | tf_op jit(solution)/shard_map/ppermute | solution.py:399
  22.8 13.2 %collective-permute-start.9 = (bf16[32,1664]{1,0:T(8,128)(2,1)S(1)}, bf16[32,1664]{1,0:T(8,128)(2,1)S(1)}, u32[]{:S(2)}, u32[]{:S(2)}) collective-permute-start(bf16[32,1664]{1,0:T(8,128)(2,1)S(1)} %get-tuple-element.13.refs_0_.refs_6_), channel_id=1, source_target_pairs={{0,12},{4,8},{8,4},{12,0},{1,13},{5,9},{9,5},{13,1},{2,14},{6,10},... | collective-permute-start | bytes 319496 | tf_op jit(solution)/shard_map/ppermute | solution.py:399
  22.8 4.6 %copy-start.1 = (bf16[2,2048,1536]{2,1,0:T(8,128)(2,1)S(1)}, bf16[2,2048,1536]{2,1,0:T(8,128)(2,1)}, u32[]{:S(2)}) copy-start(bf16[2,2048,1536]{2,1,0:T(8,128)(2,1)} %w_ref.3) | copy-start | bytes 37748740
  27.3 4.6 %copy-start.2 = (bf16[2,2048,1536]{2,1,0:T(8,128)(2,1)S(1)}, bf16[2,2048,1536]{2,1,0:T(8,128)(2,1)}, u32[]{:S(2)}) copy-start(bf16[2,2048,1536]{2,1,0:T(8,128)(2,1)} %w_ref.3) | copy-start | bytes 37748740
  29.3 10.7 %collective-permute-start.5 = (bf16[64,2048]{1,0:T(8,128)(2,1)S(1)}, bf16[64,2048]{1,0:T(8,128)(2,1)S(1)}, u32[]{:S(2)}, u32[]{:S(2)}) collective-permute-start(bf16[64,2048]{1,0:T(8,128)(2,1)S(1)} %project.9), channel_id=1, source_target_pairs={{0,1},{1,0},{2,3},{3,2},{4,5},{5,4},{6,7},{7,6},{8,9},{9,8},{10,11... | collective-permute-start | bytes 786440 | tf_op jit(solution)/shard_map/ppermute | solution.py:399
  31.9 4.1 %slice-start = ((s8[6291456]{0:T(1024)(128)(4,1)}), s8[4194304]{0:T(1024)(128)(4,1)S(1)}, s32[]{:S(2)}) async-start(s8[6291456]{0:T(1024)(128)(4,1)} %bitcast.3), calls=%async_computation | async-start | bytes 8388608
  33.9 2.1 %slice-start.1 = ((s8[6291456]{0:T(1024)(128)(4,1)}), s8[2097152]{0:T(1024)(128)(4,1)S(1)}, s32[]{:S(2)}) async-start(s8[6291456]{0:T(1024)(128)(4,1)} %bitcast.3), calls=%async_computation.1 | async-start | bytes 4194304
  37.2 3.5 %collective-permute-start.10 = (bf16[128,1024]{1,0:T(8,128)(2,1)S(1)}, bf16[128,1024]{1,0:T(8,128)(2,1)S(1)}, u32[]{:S(2)}, u32[]{:S(2)}) collective-permute-start(bf16[128,1024]{1,0:T(8,128)(2,1)S(1)} %project.11), channel_id=1, source_target_pairs={{0,1},{1,0},{2,3},{3,2},{4,5},{5,4},{6,7},{7,6},{8,9},{9,8},{10,11... | collective-permute-start | bytes 786440 | tf_op jit(solution)/shard_map/ppermute | solution.py:399
  38.5 9.2 %collective-permute-start.2 = (bf16[64,2048]{1,0:T(8,128)(2,1)S(1)}, bf16[64,2048]{1,0:T(8,128)(2,1)S(1)}, u32[]{:S(2)}, u32[]{:S(2)}) collective-permute-start(bf16[64,2048]{1,0:T(8,128)(2,1)S(1)} %add_convert_fusion.2.refs_0_), channel_id=1, source_target_pairs={{0,2},{1,3},{2,0},{3,1},{4,6},{5,7},{6,4},{7,5},{8,10},{9,11},{10,... | collective-permute-start | bytes 786440 | tf_op jit(solution)/shard_map/ppermute | solution.py:399
  40.1 13.2 %collective-permute-start.6 = (bf16[64,2048]{1,0:T(8,128)(2,1)S(1)}, bf16[64,2048]{1,0:T(8,128)(2,1)S(1)}, u32[]{:S(2)}, u32[]{:S(2)}) collective-permute-start(bf16[64,2048]{1,0:T(8,128)(2,1)S(1)} %add_convert_fusion.1.refs_2_), channel_id=1, source_target_pairs={{0,2},{1,3},{2,0},{3,1},{4,6},{5,7},{6,4},{7,5},{8,10},{9,11},{10,... | collective-permute-start | bytes 786440 | tf_op jit(solution)/shard_map/ppermute | solution.py:399
  40.8 17.7 %collective-permute-start.11 = (bf16[128,1024]{1,0:T(8,128)(2,1)S(1)}, bf16[128,1024]{1,0:T(8,128)(2,1)S(1)}, u32[]{:S(2)}, u32[]{:S(2)}) collective-permute-start(bf16[128,1024]{1,0:T(8,128)(2,1)S(1)} %add_convert_fusion.refs_4_), channel_id=1, source_target_pairs={{0,2},{1,3},{2,0},{3,1},{4,6},{5,7},{6,4},{7,5},{8,10},{9,11},{10,... | collective-permute-start | bytes 786440 | tf_op jit(solution)/shard_map/ppermute | solution.py:399
  59.1 8.1 %collective-permute-start.12 = (bf16[128,2176]{1,0:T(8,128)(2,1)S(1)}, bf16[128,2176]{1,0:T(8,128)(2,1)S(1)}, u32[]{:S(2)}, u32[]{:S(2)}) collective-permute-start(bf16[128,2176]{1,0:T(8,128)(2,1)S(1)} %pre.1.pre_ref.mine_ref), channel_id=1, source_target_pairs={{0,1},{1,0},{2,3},{3,2},{4,5},{5,4},{6,7},{7,6},{8,9},{9,8},{10,11... | collective-permute-start | bytes 1671176 | tf_op jit(solution)/shard_map/ppermute | solution.py:399
  59.3 2.1 %collective-permute-start.16 = (bf16[128,1024]{1,0:T(8,128)(2,1)S(1)}, bf16[128,1024]{1,0:T(8,128)(2,1)S(1)}, u32[]{:S(2)}, u32[]{:S(2)}) collective-permute-start(bf16[128,1024]{1,0:T(8,128)(2,1)S(1)} %hidden.1.mine_ref), channel_id=1, source_target_pairs={{0,1},{1,0},{2,3},{3,2},{4,5},{5,4},{6,7},{7,6},{8,9},{9,8},{10,11... | collective-permute-start | bytes 786440 | tf_op jit(solution)/shard_map/ppermute | solution.py:399
  68.1 13.8 %collective-permute-start.13 = (bf16[32,1664]{1,0:T(8,128)(2,1)S(1)}, bf16[32,1664]{1,0:T(8,128)(2,1)S(1)}, u32[]{:S(2)}, u32[]{:S(2)}) collective-permute-start(bf16[32,1664]{1,0:T(8,128)(2,1)S(1)} %get-tuple-element.15), channel_id=1, source_target_pairs={{0,4},{4,0},{8,12},{12,8},{1,5},{5,1},{9,13},{13,9},{2,6},{6,2},{1... | collective-permute-start | bytes 319496 | tf_op jit(solution)/shard_map/ppermute | solution.py:399
  68.8 13.2 %collective-permute-start.14 = (bf16[32,1664]{1,0:T(8,128)(2,1)S(1)}, bf16[32,1664]{1,0:T(8,128)(2,1)S(1)}, u32[]{:S(2)}, u32[]{:S(2)}) collective-permute-start(bf16[32,1664]{1,0:T(8,128)(2,1)S(1)} %get-tuple-element.16), channel_id=1, source_target_pairs={{0,8},{4,12},{8,0},{12,4},{1,9},{5,13},{9,1},{13,5},{2,10},{6,14},... | collective-permute-start | bytes 319496 | tf_op jit(solution)/shard_map/ppermute | solution.py:399
  72.6 9.4 %collective-permute-start.15 = (bf16[32,1664]{1,0:T(8,128)(2,1)S(1)}, bf16[32,1664]{1,0:T(8,128)(2,1)S(1)}, u32[]{:S(2)}, u32[]{:S(2)}) collective-permute-start(bf16[32,1664]{1,0:T(8,128)(2,1)S(1)} %get-tuple-element.17), channel_id=1, source_target_pairs={{0,12},{4,8},{8,4},{12,0},{1,13},{5,9},{9,5},{13,1},{2,14},{6,10},... | collective-permute-start | bytes 319496 | tf_op jit(solution)/shard_map/ppermute | solution.py:399

commit v2 on v1

v2 whole, which is shorter than its diff:
```python
import functools

import jax
import jax.numpy as jnp
from jax import lax
from jax.experimental import pallas as pl
from jax.experimental.pallas import tpu as pltpu
from jax.sharding import PartitionSpec as P

F32 = jnp.float32
BF16 = jnp.bfloat16
VMEM = pl.BlockSpec(memory_space=pltpu.VMEM)
SMEM = pl.BlockSpec(memory_space=pltpu.SMEM)
ANY = pl.BlockSpec(memory_space=pl.ANY)
HBM = pl.BlockSpec(memory_space=pltpu.HBM)
LANES = 128
MIB = 2**20

NT = (((1,), (1,)), ((), ()))
TN = (((0,), (0,)), ((), ()))


def params(mib):
    return pltpu.CompilerParams(vmem_limit_bytes=mib * MIB)


def in_hbm(array):
    return pltpu.with_memory_space_constraint(array, pltpu.HBM)


def in_vmem(array):
    return pltpu.with_memory_space_constraint(array, pltpu.VMEM)


STEP = pl.CostEstimate(flops=7 * 10**9, bytes_accessed=1024, transcendentals=0)
FIRST = pl.CostEstimate(flops=12 * 10**9, bytes_accessed=1024, transcendentals=0)


def fetch(pairs, sems):
    copies = [pltpu.make_async_copy(a, b, sems.at[i]) for i, (a, b) in enumerate(pairs)]
    for copy in copies:
        copy.start()
    for copy in copies:
        copy.wait()


def load_kernel(pieces, *refs):
    w_ref, out_ref, sems = refs[0], refs[-2], refs[-1]
    kinds, hidden, _ = w_ref.shape
    step = hidden // pieces
    spans = [(k, pl.ds(j * step, step)) for k in range(kinds) for j in range(pieces)]
    fetch([(w_ref.at[s], out_ref.at[s]) for s in spans], sems)


def load(weight, after):
    kinds, pieces = weight.shape[0], 4
    return pl.pallas_call(
        functools.partial(load_kernel, pieces),
        in_specs=[HBM] + [ANY] * len(after),
        out_specs=VMEM,
        out_shape=pltpu.VMEM(weight.shape, weight.dtype),
        scratch_shapes=[pltpu.SemaphoreType.DMA((kinds * pieces,))],
        compiler_params=params(8),
        cost_estimate=STEP,
        name="load",
    )(in_hbm(weight), *after)


def slot_picker(ids, capacity):
    tok_rows = ids.shape[1]
    routed = jnp.logical_or(ids[0:1] == 0, ids[1:2] == 0)
    row = lax.broadcasted_iota(jnp.int32, (tok_rows, tok_rows), 0)
    col = lax.broadcasted_iota(jnp.int32, (tok_rows, tok_rows), 1)
    before = jnp.where(row < col, 1.0, 0.0).astype(BF16)
    flags = jnp.broadcast_to(jnp.where(routed, 1.0, 0.0), (capacity, tok_rows))
    position = jnp.dot(flags.astype(BF16), before, preferred_element_type=F32)
    slot = lax.broadcasted_iota(jnp.int32, (capacity, tok_rows), 0).astype(F32)
    return jnp.where(position == slot, flags, 0.0).astype(BF16)


def select_tokens_kernel(own_ref, other_ref, tok_hbm, ids_hbm, out_ref, tok_ref, ids_ref, sems):
    del own_ref, other_ref
    fetch([(tok_hbm, tok_ref), (ids_hbm, ids_ref)], sems)
    picker = slot_picker(ids_ref[...], out_ref.shape[0])
    out_ref[...] = jnp.dot(picker, tok_ref[...], preferred_element_type=F32).astype(BF16)


def select_tokens(firsts, tokens, expert_ids):
    capacity, width = tokens.shape[0] // 4, tokens.shape[1]
    return pl.pallas_call(
        select_tokens_kernel,
        in_specs=[SMEM] * 2 + [HBM] * 2,
        out_specs=VMEM,
        out_shape=jax.ShapeDtypeStruct((capacity, width), BF16),
        scratch_shapes=[pltpu.VMEM(a.shape, a.dtype) for a in (tokens, expert_ids)]
        + [pltpu.SemaphoreType.DMA((2,))],
        compiler_params=params(8),
        cost_estimate=FIRST,
        name="select",
    )(*firsts, *(in_hbm(a) for a in (tokens, expert_ids)))


def select_cotangent_kernel(after_ref, cot_hbm, ids_hbm, quant_hbm, out_ref, *scratch):
    del after_ref
    cot_ref, ids_ref, quant_ref, sems = scratch
    fetch([(cot_hbm, cot_ref), (ids_hbm, ids_ref), (quant_hbm, quant_ref)], sems)
    capacity, width = out_ref.shape[0], cot_ref.shape[1]
    ids = ids_ref[...]
    picker = slot_picker(ids, capacity)
    scaled = quant_ref[...].astype(F32)
    total = scaled[0:1] + scaled[1:2]
    routing = (scaled / total).astype(BF16).astype(F32)
    weight = jnp.where(ids == 0, routing, 0.0)
    rate = jnp.broadcast_to(weight[0:1] + weight[1:2], (LANES, ids.shape[1])).astype(BF16)
    out_ref[:, :width] = jnp.dot(picker, cot_ref[...], preferred_element_type=F32).astype(BF16)
    out_ref[:, width:] = lax.dot_general(picker, rate, NT, preferred_element_type=F32).astype(BF16)


def select_cotangent(after, cotangent, expert_ids, quantized):
    capacity, width = cotangent.shape[0] // 4, cotangent.shape[1]
    arrays = (cotangent, expert_ids, quantized)
    return pl.pallas_call(
        select_cotangent_kernel,
        in_specs=[ANY] + [HBM] * 3,
        out_specs=VMEM,
        out_shape=jax.ShapeDtypeStruct((capacity, width + LANES), BF16),
        scratch_shapes=[pltpu.VMEM(a.shape, a.dtype) for a in arrays]
        + [pltpu.SemaphoreType.DMA((3,))],
        compiler_params=params(8),
        cost_estimate=STEP,
        name="select_cot",
    )(after, *(in_hbm(a) for a in arrays))


def project_kernel(nblocks, width, offset, first_ref, *refs):
    blocks, w_ref, out_ref = refs[:nblocks], refs[nblocks], refs[-1]
    kinds = w_ref.shape[0]
    units = out_ref.shape[1] // kinds
    rows = jnp.concatenate([b[:, :width] for b in blocks], axis=0)
    start = pl.multiple_of(first_ref[0] + offset, units)
    step = min(units, 512)
    for kind in range(kinds):
        for j in range(0, units, step):
            out_ref[:, kind * units + j : kind * units + j + step] = lax.dot_general(
                rows, w_ref[kind, pl.ds(start + j, step), :], NT, preferred_element_type=F32
            ).astype(out_ref.dtype)


def project(blocks, weight, first, span, out_type, after=()):
    kinds, _, width = weight.shape
    offset, units = span
    rows = sum(b.shape[0] for b in blocks)
    return pl.pallas_call(
        functools.partial(project_kernel, len(blocks), width, offset),
        in_specs=[SMEM] + [VMEM] * (len(blocks) + 1) + [ANY] * len(after),
        out_specs=VMEM,
        out_shape=jax.ShapeDtypeStruct((rows, kinds * units), out_type),
        compiler_params=params(24),
        cost_estimate=STEP,
        name="project",
    )(first, *blocks, in_vmem(weight), *after)


def gated(sums):
    half = sums.shape[1] // 2
    gate, up = sums[:, :half], sums[:, half:]
    return gate, up, jax.nn.sigmoid(gate)


def hidden_kernel(nparts, *refs):
    out_ref = refs[-1]
    gate, up, s = gated(sum(p[...].astype(F32) for p in refs[:nparts]))
    out_ref[...] = (gate * s * up).astype(BF16)


def hidden_units(parts, after=()):
    rows, units = parts[0].shape[0], parts[0].shape[1] // 2
    return pl.pallas_call(
        functools.partial(hidden_kernel, len(parts)),
        in_specs=[VMEM] * len(parts) + [ANY] * len(after),
        out_specs=VMEM,
        out_shape=jax.ShapeDtypeStruct((rows, units), BF16),
        compiler_params=params(16),
        cost_estimate=STEP,
        name="hidden",
    )(*parts, *after)


def pre_kernel(nchunks, nparts, nblocks, width, *refs):
    chunks = [refs[i * nparts : (i + 1) * nparts] for i in range(nchunks)]
    back_parts = refs[nchunks * nparts :][:nparts]
    blocks = refs[(nchunks + 1) * nparts :][:nblocks]
    out_ref = refs[-1]
    half = back_parts[0].shape[1]
    rate = jnp.concatenate([b[:, width : width + 1].astype(F32) for b in blocks], axis=0)
    route = jnp.zeros_like(rate)
    at = 0
    for parts in chunks:
        gate, up, s = gated(sum(p[...].astype(F32) for p in parts))
        units = gate.shape[1]
        back = sum(p[:, at : at + units].astype(F32) for p in back_parts)
        hidden = (gate * s * up).astype(BF16).astype(F32)
        route += jnp.sum(hidden * back, axis=1, keepdims=True)
        grad = rate * back
        gate_grad = grad * up * s * (1.0 + gate * (1.0 - s))
        up_grad = grad * gate * s
        out_ref[:, at : at + units] = gate_grad.astype(BF16)
        out_ref[:, half + at : half + at + units] = up_grad.astype(BF16)
        at += units
    out_ref[:, 2 * half :] = high_low(route)


def high_low(value):
    high = value.astype(BF16).astype(F32)
    low = value - high
    lane = lax.broadcasted_iota(jnp.int32, (value.shape[0], LANES), 1)
    return jnp.where(lane == 0, high, jnp.where(lane == 1, low, 0.0)).astype(BF16)


def pre_grads(groups, back_parts, blocks, width, after=()):
    half = back_parts[0].shape[1]
    rows = back_parts[0].shape[0]
    flat = [p for g in groups for p in g]
    return pl.pallas_call(
        functools.partial(pre_kernel, len(groups), len(groups[0]), len(blocks), width),
        in_specs=[VMEM] * (len(flat) + len(back_parts) + len(blocks)) + [ANY] * len(after),
        out_specs=VMEM,
        out_shape=jax.ShapeDtypeStruct((rows, 2 * half + LANES), BF16),
        compiler_params=params(16),
        cost_estimate=STEP,
        name="pre",
    )(*flat, *back_parts, *blocks, *after)


def row_own_kernel(first_ref, pre_ref, w_ref, out_ref):
    half = (pre_ref.shape[1] - LANES) // 2
    start = pl.multiple_of(first_ref[0], half)
    out_ref[...] = jnp.dot(
        pre_ref[:, :half], w_ref[0, pl.ds(start, half), :], preferred_element_type=F32
    ) + jnp.dot(
        pre_ref[:, half : 2 * half], w_ref[1, pl.ds(start, half), :], preferred_element_type=F32
    )


def row_own(pre, weight, first):
    rows, width = pre.shape[0], weight.shape[2]
    return pl.pallas_call(
        row_own_kernel,
        in_specs=[SMEM, VMEM, VMEM],
        out_specs=VMEM,
        out_shape=jax.ShapeDtypeStruct((rows, width), F32),
        compiler_params=params(24),
        cost_estimate=STEP,
        name="row_own",
    )(first, pre, in_vmem(weight))


def row_rest_kernel(first_ref, own_ref, mine_ref, pre_ref, w_ref, *out_refs):
    half = (pre_ref.shape[1] - LANES) // 2
    width = own_ref.shape[1]
    start = pl.multiple_of(first_ref[0], half)
    total = (
        own_ref[...]
        + jnp.dot(pre_ref[:, :half], w_ref[0, pl.ds(start, half), :], preferred_element_type=F32)
        + jnp.dot(
            pre_ref[:, half : 2 * half], w_ref[1, pl.ds(start, half), :], preferred_element_type=F32
        )
    )
    lanes = mine_ref[:, 2 * half :].astype(F32) + pre_ref[:, 2 * half :].astype(F32)
    route = lanes[:, 0:1] + lanes[:, 1:2]
    at = 0
    for out in out_refs:
        rows = out.shape[0]
        out[:, :width] = total[at : at + rows].astype(out.dtype)
        if out.dtype == F32:
            out[:, width:] = jnp.broadcast_to(route[at : at + rows], (rows, LANES)) * jnp.where(
                lax.broadcasted_iota(jnp.int32, (rows, LANES), 1) == 0, 1.0, 0.0
            )
        else:
            out[:, width:] = high_low(route[at : at + rows])
        at += rows


def row_rest(own, mine, pre, weight, first, outs):
    rows, width = own.shape
    return pl.pallas_call(
        row_rest_kernel,
        in_specs=[SMEM] + [VMEM] * 4,
        out_specs=[VMEM] * len(outs),
        out_shape=[jax.ShapeDtypeStruct((n, width + LANES), kind) for n, kind in outs],
        compiler_params=params(24),
        cost_estimate=STEP,
        name="row_rest",
    )(first, own, mine, pre, in_vmem(weight))


def write_tiles(tiles, make, out_at, buf, sem):
    ring = buf.shape[0]
    copies = []
    for i, tile in enumerate(tiles):
        slot = i % ring
        if i >= ring:
            copies[i - ring].wait()
        buf[slot] = make(tile)
        copy = pltpu.make_async_copy(buf.at[slot], out_at(tile), sem.at[slot])
        copy.start()
        copies.append(copy)
    for copy in copies[max(0, len(copies) - ring) :]:
        copy.wait()


def grad_out_kernel(nblocks, places, nafter, own_ref, other_ref, *refs):
    sources, blocks = refs[: len(places)], refs[len(places) :][:nblocks]
    out_ref, mark_ref, cot, buf, sem = refs[len(places) + nblocks + nafter :]
    mark_ref[...] = jnp.zeros_like(mark_ref)
    width = out_ref.shape[1]
    half = out_ref.shape[0] // 2
    step = buf.shape[1]
    at = 0
    for b in blocks:
        rows = b.shape[0]
        cot[at : at + rows, :] = (
            b[:, width : width + 1].astype(F32) * b[:, :width].astype(F32)
        ).astype(BF16)
        at += rows
    starts = (pl.multiple_of(own_ref[0], half), pl.multiple_of(other_ref[0], half))
    tiles = [(s, j) for s in range(len(places)) for j in range(0, sources[s].shape[1], step)]

    def make(tile):
        s, j = tile
        return lax.dot_general(
            sources[s][:, j : j + step], cot[...], TN, preferred_element_type=F32
        )

    def out_at(tile):
        s, j = tile
        side, offset = places[s]
        return out_ref.at[pl.ds(starts[side] + offset + j, step)]

    write_tiles(tiles, make, out_at, buf, sem)


def grad_out(pieces, blocks, firsts, hidden, width, so_far, after=()):
    sources = [piece[0] for piece in pieces]
    places = [piece[1:] for piece in pieces]
    rows, units = sources[0].shape
    step = min(units, 256)
    ring = min(8, len(sources) * units // step)
    before = [] if so_far is None else [in_hbm(so_far)]
    return pl.pallas_call(
        functools.partial(grad_out_kernel, len(blocks), places, len(after) + len(before)),
        in_specs=[SMEM] * 2
        + [VMEM] * (len(sources) + len(blocks))
        + [ANY] * len(after)
        + [HBM] * len(before),
        out_specs=[HBM, VMEM],
        out_shape=[
            pltpu.HBM((hidden, width), F32),
            jax.ShapeDtypeStruct((8, LANES), F32),
        ],
        scratch_shapes=[
            pltpu.VMEM((rows, width), BF16),
            pltpu.VMEM((ring, step, width), F32),
            pltpu.SemaphoreType.DMA((ring,)),
        ],
        input_output_aliases=(
            {2 + len(sources) + len(blocks) + len(after): 0} if before else {}
        ),
        compiler_params=params(28),
        cost_estimate=STEP,
        name="grad_out",
    )(*firsts, *sources, *blocks, *after, *before)


def grad_in_kernel(nblocks, own_ref, other_ref, mine_ref, peer_ref, *refs):
    blocks = refs[:nblocks]
    out_ref, tok, buf, sem = refs[nblocks:]
    half = (mine_ref.shape[1] - LANES) // 2
    step = buf.shape[1]
    at = 0
    for b in blocks:
        rows = b.shape[0]
        tok[at : at + rows, :] = b[...]
        at += rows
    starts = (pl.multiple_of(own_ref[0], half), pl.multiple_of(other_ref[0], half))
    sources = (mine_ref, peer_ref)
    tiles = [(s, c, j) for s in range(2) for c in range(2) for j in range(0, half, step)]

    def make(tile):
        s, c, j = tile
        at = c * half + j
        return lax.dot_general(
            sources[s][:, at : at + step], tok[...], TN, preferred_element_type=F32
        )

    def out_at(tile):
        s, c, j = tile
        return out_ref.at[c, pl.ds(starts[s] + j, step)]

    write_tiles(tiles, make, out_at, buf, sem)


def grad_in(mine, peer, blocks, firsts, width):
    rows = mine.shape[0]
    half = (mine.shape[1] - LANES) // 2
    step = min(half, 256)
    ring = min(8, 4 * half // step)
    return pl.pallas_call(
        functools.partial(grad_in_kernel, len(blocks)),
        in_specs=[SMEM] * 2 + [VMEM] * (2 + len(blocks)),
        out_specs=HBM,
        out_shape=pltpu.HBM((2, 2 * half, width), F32),
        scratch_shapes=[
            pltpu.VMEM((rows, width), BF16),
            pltpu.VMEM((ring, step, width), F32),
            pltpu.SemaphoreType.DMA((ring,)),
        ],
        compiler_params=params(28),
        cost_estimate=STEP,
        name="grad_in",
    )(*firsts, mine, peer, *blocks)


def place_kernel(nblocks, ids_ref, *refs):
    blocks, (in_ref, weight_ref) = refs[:nblocks], refs[nblocks:]
    width = in_ref.shape[1]
    capacity = blocks[0].shape[0]
    total = sum(b[:, :width].astype(F32) for b in blocks)
    lanes = sum(b[:, width:].astype(F32) for b in blocks)
    ids = ids_ref[...]
    picker = slot_picker(ids, capacity)
    in_ref[...] = lax.dot_general(
        picker, total.astype(BF16), TN, preferred_element_type=F32
    ).astype(BF16)
    route = jnp.broadcast_to(lanes[:, 0:1] + lanes[:, 1:2], (capacity, LANES))
    high = route.astype(BF16)
    low = (route - high.astype(F32)).astype(BF16)
    spread = lax.dot_general(high, picker, TN, preferred_element_type=F32) + lax.dot_general(
        low, picker, TN, preferred_element_type=F32
    )
    weight_ref[...] = jnp.where(ids == 0, spread[: ids.shape[0]], 0.0).astype(BF16)


def place(expert_ids, blocks):
    tok_rows = expert_ids.shape[1]
    width = blocks[0].shape[1] - LANES
    return pl.pallas_call(
        functools.partial(place_kernel, len(blocks)),
        in_specs=[VMEM] * (1 + len(blocks)),
        out_specs=[VMEM] * 2,
        out_shape=[
            jax.ShapeDtypeStruct((tok_rows, width), BF16),
            jax.ShapeDtypeStruct(expert_ids.shape, BF16),
        ],
        compiler_params=params(8),
        cost_estimate=STEP,
        name="place",
    )(expert_ids, *blocks)


def swap(array, axis, size, distance):
    return lax.ppermute(array, axis, [(i, i ^ distance) for i in range(size)])


def relay_kernel(block_ref, after_ref, out_ref):
    del after_ref
    out_ref[...] = block_ref[...]


def relay(block, after):
    return pl.pallas_call(
        relay_kernel,
        in_specs=[VMEM, ANY],
        out_specs=VMEM,
        out_shape=jax.ShapeDtypeStruct(block.shape, block.dtype),
        compiler_params=params(8),
        cost_estimate=STEP,
        name="relay",
    )(block, after)


def per_device(dp, chips, tokens, cotangent, expert_ids, quantized, weight_in, weight_out):
    experts = 2 * chips
    width = tokens.shape[1]
    hidden = weight_in.shape[1]
    half = hidden // 2
    core = lax.rem(lax.axis_index("expert"), 2)
    firsts = [(c * half).astype(jnp.int32).reshape(1) for c in (core, 1 - core)]
    direct = dp == 4

    expert_ids, quantized = expert_ids.T, quantized.T
    weight_out = weight_out.reshape((1,) + weight_out.shape)
    send_in = select_tokens(firsts, tokens, expert_ids)
    if direct:
        across = swap(send_in, "dp", dp, 2)
        tok_blocks = [send_in, swap(send_in, "dp", dp, 1), across, swap(across, "dp", dp, 1)]
        send_grad = select_cotangent(across, cotangent, expert_ids, quantized)
        cot_blocks = [send_grad, swap(send_grad, "dp", dp, 1), swap(send_grad, "dp", dp, 2)]
    else:
        send_grad = select_cotangent(send_in, cotangent, expert_ids, quantized)
        tok_blocks = [lax.all_gather(send_in, "dp", axis=0, tiled=True)]
        cot_blocks = [lax.all_gather(send_grad, "dp", axis=0, tiled=True)]

    def summed(blocks, weight, span, after=()):
        theirs = project(blocks, weight, firsts[1], span, BF16, after)
        arrived = swap(theirs, "expert", experts, 1)
        mine = project(blocks, weight, firsts[0], span, F32, [theirs])
        chip = (mine + arrived.astype(F32)).astype(BF16)
        return theirs, [chip] + [swap(chip, "expert", experts, 2 * k) for k in range(1, chips)]

    pieces = 2 if half % 256 == 0 else 1
    units = half // pieces
    gu, last = [], send_grad
    for i in range(pieces):
        theirs, parts = summed(tok_blocks, weight_in, (i * units, units), [last])
        gu.append(parts)
        last = parts[0]
    if direct:
        cot_blocks.append(swap(relay(cot_blocks[2], theirs), "dp", dp, 1))
    _, back = summed(cot_blocks, weight_out, (0, half), [last])

    grad_weight_out, last, waiting = None, back[0], []
    for i, parts in enumerate(gu):
        mine = hidden_units(parts, [last])
        ready = waiting + [(mine, 0, i * units)]
        grad_weight_out, last = grad_out(ready, cot_blocks, firsts, hidden, width, grad_weight_out)
        waiting = [(swap(mine, "expert", experts, 1), 1, i * units)]
    grad_weight_out, mark = grad_out(
        waiting, cot_blocks, firsts, hidden, width, grad_weight_out, [last]
    )

    pre = pre_grads(gu, back, cot_blocks, width, [mark])
    pre_peer = swap(pre, "expert", experts, 1)
    part = row_own(pre, weight_in, firsts[0])
    if direct:
        cap = send_in.shape[0]
        outs = [(cap, F32)] + [(cap, BF16)] * (dp - 1)
        sent = row_rest(part, pre, pre_peer, weight_in, firsts[1], outs)
        arrived = [sent[0]] + [swap(sent[d], "dp", dp, d) for d in range(1, dp)]
    else:
        sent = row_rest(part, pre, pre_peer, weight_in, firsts[1], [(part.shape[0], F32)])
        arrived = [lax.psum_scatter(sent[0], "dp", scatter_dimension=0, tiled=True)]
    grad_weight_in = grad_in(pre, pre_peer, tok_blocks, firsts, width)
    input_grad, weight_grad = place(expert_ids, arrived)
    return (input_grad, weight_grad.T, grad_weight_in, grad_weight_out)


def solution(mesh):
    return jax.shard_map(
        functools.partial(per_device, mesh.shape["dp"], mesh.shape["expert"] // 2),
        mesh=mesh,
        in_specs=(
            P(("group", "dp"), "expert"),
            P(("group", "dp"), "expert"),
            P(("group", "dp"), None),
            P(("group", "dp"), None),
            P(None, "dp", "expert"),
            P("dp", "expert"),
        ),
        out_specs=(
            P(("group", "dp"), "expert"),
            P(("group", "dp"), None),
            P("group", "dp", "expert"),
            P(("group", "dp"), "expert"),
        ),
        check_vma=False,
    )
```

time: 84.2 us -> 58.6 us (0.70)
  local copies, waits for them, and re-layouts: 15.8 us -> 0.04 us
  waiting for transfers between devices: 16.9 us -> 7.1 us
    unnamed x17 -> x12, local copies, waits for them, and re-layouts: 15.8 us -> 0.04 us
    ppermute x17 -> x18, waiting for transfers between devices: 16.9 us -> 7.1 us  [swap(): return lax.ppermute(array, axis, [(i, i ^ distance) for i in range(size)])]
    pallas_call x9 -> x14, Pallas kernels: 16.7 us -> 17.5 us  [the longest x3 7.46 us: grad_out(): pl.pallas_call(functools.partial(grad_out_kernel, len(blocks), places, le...]
    ppermute x17 -> x18, starting transfers between devices: 20.2 us -> 20.2 us  [swap(): return lax.ppermute(array, axis, [(i, i ^ distance) for i in range(size)])]
  transfers between devices with their start and end apart: 17 -> 18, of which waited for: 5 -> 6; matrix products, arithmetic and copies ran while one was open for 0% -> 0% of each run, Pallas kernels for 32% -> 44%
where the time goes in v2:
time: 58.6 us; the launch traced here: 58.4 us
  Pallas kernels  30 us (51%)
  starting transfers between devices  20.2 us (34%)
  waiting for transfers between devices  7.1 us (12%)
  between operations  0.98 us (2%)
    ppermute x18, starting transfers between devices, swap(): return lax.ppermute(array, axis, [(i, i ^ distance) for i in range(size)])  20.2 us
    pallas_call x1, Pallas kernels, grad_in(): pl.pallas_call(functools.partial(grad_in_kernel, len(blocks)), in_specs=[...  8.82 us
    pallas_call x3, Pallas kernels, grad_out(): pl.pallas_call(functools.partial(grad_out_kernel, len(blocks), places, le...  7.46 us
    ppermute x18, waiting for transfers between devices, swap(): return lax.ppermute(array, axis, [(i, i ^ distance) for i in range(size)])  7.1 us
    pallas_call x6, Pallas kernels, project(): pl.pallas_call(functools.partial(project_kernel, len(blocks), width, offs...  6.79 us
    pallas_call x1, Pallas kernels, select_cotangent(): pl.pallas_call(select_cotangent_kernel, in_specs=[ANY] + [HBM] * 3, out_s...  1.51 us
    pallas_call x1, Pallas kernels, select_tokens(): pl.pallas_call(select_tokens_kernel, in_specs=[SMEM] * 2 + [HBM] * 2, out...  1.48 us
    pallas_call x1, Pallas kernels, place(): pl.pallas_call(functools.partial(place_kernel, len(blocks)), in_specs=[VM...  1.18 us
  transfers between devices with their start and end apart: 18, of which 6 were waited for; matrix products, arithmetic and copies ran while one was open for 0% of the time, Pallas kernels for 44%

profile of v2, /device:TPU:0, one launch (start us, length us, event | category | flops | bytes accessed | tf_op | source)
XLA Modules:
  0.0 58.4 jit_solution(3719633654635705914)
XLA Ops:
  0.6 0.0 slice-start
  0.7 1.5 %select.3.refs_0_ = bf16[32,1536]{1,0:T(8,128)(2,1)S(1)} custom-call(s32[1]{0:T(128)} %bitcast.2.own_ref.first_ref, s32[1]{0:T(128)} %bitcast.1.other_ref.first_ref, bf16[128,1536]{1,0:T(8,128)(2,1)} %tok_hbm.1, s32[2,128]{1,0:T(2,128)} %bitcast.12), custom_call_target="tpu_custom_call" | custom-call | flops 12000000000 | bytes 1024 | tf_op jit(solution)/shard_map/select/pallas_call | solution.py:90
  2.2 4.1 %collective-permute-start.1 = (bf16[32,1536]{1,0:T(8,128)(2,1)S(1)}, bf16[32,1536]{1,0:T(8,128)(2,1)S(1)}, u32[]{:S(2)}, u32[]{:S(2)}) collective-permute-start(bf16[32,1536]{1,0:T(8,128)(2,1)S(1)} %select.3.refs_0_), channel_id=1, source_target_pairs={{0,8},{4,12},{8,0},{12,4},{1,9},{5,13},{9,1},{13,5},{2,10},{6,14},... | collective-permute-start | bytes 294920 | tf_op jit(solution)/shard_map/ppermute | solution.py:462
  6.3 1.6 %collective-permute-start = (bf16[32,1536]{1,0:T(8,128)(2,1)S(1)}, bf16[32,1536]{1,0:T(8,128)(2,1)S(1)}, u32[]{:S(2)}, u32[]{:S(2)}) collective-permute-start(bf16[32,1536]{1,0:T(8,128)(2,1)S(1)} %select.3.refs_0_), channel_id=1, source_target_pairs={{0,4},{4,0},{8,12},{12,8},{1,5},{5,1},{9,13},{13,9},{2,6},{6,2},{1... | collective-permute-start | bytes 294920 | tf_op jit(solution)/shard_map/ppermute | solution.py:462
  7.8 3.2 %collective-permute-done.1.after_ref.refs_2_ = bf16[32,1536]{1,0:T(8,128)(2,1)S(1)} collective-permute-done((bf16[32,1536]{1,0:T(8,128)(2,1)S(1)}, bf16[32,1536]{1,0:T(8,128)(2,1)S(1)}, u32[]{:S(2)}, u32[]{:S(2)}) %collective-permute-start.1) | collective-permute-done | bytes 98336 | tf_op jit(solution)/shard_map/ppermute | solution.py:462
  11.0 0.8 %collective-permute-start.2 = (bf16[32,1536]{1,0:T(8,128)(2,1)S(1)}, bf16[32,1536]{1,0:T(8,128)(2,1)S(1)}, u32[]{:S(2)}, u32[]{:S(2)}) collective-permute-start(bf16[32,1536]{1,0:T(8,128)(2,1)S(1)} %collective-permute-done.1.after_ref.refs_2_), channel_id=1, source_target_pairs={{0,4},{4,0},{8,12},{12,8},{1,5},{5,1},{9,13},{13,9},{2,6},{6,2},{1... | collective-permute-start | bytes 294920 | tf_op jit(solution)/shard_map/ppermute | solution.py:462
  11.9 1.5 %select_cot.1.refs_5_.refs_0_.refs_1_.refs_2_.refs_6_ = bf16[32,1664]{1,0:T(8,128)(2,1)S(1)} custom-call(bf16[32,1536]{1,0:T(8,128)(2,1)S(1)} %collective-permute-done.1.after_ref.refs_2_, bf16[128,1536]{1,0:T(8,128)(2,1)} %cot_hbm.1, s32[2,128]{1,0:T(2,128)} %bitcast.13, s32[2,128]{1,0:T(2,128)} %bitcast.15), custom_call_target="tpu_custom_call" | custom-call | flops 7000000000 | bytes 1024 | tf_op jit(solution)/shard_map/select_cot/pallas_call | solution.py:122
  13.4 3.4 %collective-permute-start.8 = (bf16[32,1664]{1,0:T(8,128)(2,1)S(1)}, bf16[32,1664]{1,0:T(8,128)(2,1)S(1)}, u32[]{:S(2)}, u32[]{:S(2)}) collective-permute-start(bf16[32,1664]{1,0:T(8,128)(2,1)S(1)} %select_cot.1.refs_5_.refs_0_.refs_1_.refs_2_.refs_6_), channel_id=1, source_target_pairs={{0,8},{4,12},{8,0},{12,4},{1,9},{5,13},{9,1},{13,5},{2,10},{6,14},... | collective-permute-start | bytes 319496 | tf_op jit(solution)/shard_map/ppermute | solution.py:462
  16.8 0.0 collective-permute-start.7
  16.9 1.1 %project.6.refs_5_ = bf16[128,1024]{1,0:T(8,128)(2,1)S(1)} custom-call(s32[1]{0:T(128)} %bitcast.1.other_ref.first_ref, bf16[32,1536]{1,0:T(8,128)(2,1)S(1)} %select.3.refs_0_, bf16[32,1536]{1,0:T(8,128)(2,1)S(1)} %collective-permute-done.refs_1_, bf16[32,1536]{1,0:T(8,128)(2,1)S(1)} %collective-permute-done.1.after_ref.refs_2_, ...), custom_call_target="tpu_custom_call" | custom-call | flops 7000000000 | bytes 1024 | tf_op jit(solution)/shard_map/project/pallas_call | solution.py:153
  18.0 0.1 collective-permute-start.3
  18.1 1.1 %project.7 = f32[128,1024]{1,0:T(8,128)S(1)} custom-call(s32[1]{0:T(128)} %bitcast.2.own_ref.first_ref, bf16[32,1536]{1,0:T(8,128)(2,1)S(1)} %select.3.refs_0_, bf16[32,1536]{1,0:T(8,128)(2,1)S(1)} %collective-permute-done.refs_1_, bf16[32,1536]{1,0:T(8,128)(2,1)S(1)} %collective-permute-done.1.after_ref.refs_2_, ...), custom_call_target="tpu_custom_call" | custom-call | flops 7000000000 | bytes 1024 | tf_op jit(solution)/shard_map/project/pallas_call | solution.py:153
  19.3 0.4 collective-permute-done.3
  19.6 0.1 add_convert_fusion.2.refs_5_.refs_0_
  19.7 1.6 %collective-permute-start.4 = (bf16[128,1024]{1,0:T(8,128)(2,1)S(1)}, bf16[128,1024]{1,0:T(8,128)(2,1)S(1)}, u32[]{:S(2)}, u32[]{:S(2)}) collective-permute-start(bf16[128,1024]{1,0:T(8,128)(2,1)S(1)} %add_convert_fusion.2.refs_5_.refs_0_), channel_id=1, source_target_pairs={{0,2},{1,3},{2,0},{3,1},{4,6},{5,7},{6,4},{7,5},{8,10},{9,11},{10,... | collective-permute-start | bytes 786440 | tf_op jit(solution)/shard_map/ppermute | solution.py:462
  21.3 1.1 %project.8.refs_5_.after_ref = bf16[128,1024]{1,0:T(8,128)(2,1)S(1)} custom-call(s32[1]{0:T(128)} %bitcast.1.other_ref.first_ref, bf16[32,1536]{1,0:T(8,128)(2,1)S(1)} %select.3.refs_0_, bf16[32,1536]{1,0:T(8,128)(2,1)S(1)} %collective-permute-done.refs_1_, bf16[32,1536]{1,0:T(8,128)(2,1)S(1)} %collective-permute-done.1.after_ref.refs_2_, ...), custom_call_target="tpu_custom_call" | custom-call | flops 7000000000 | bytes 1024 | tf_op jit(solution)/shard_map/project/pallas_call | solution.py:153
  22.4 0.1 collective-permute-start.5
  22.5 0.0 slice-start.3
  22.5 0.0 slice-start.4
  22.5 2.1 %collective-permute-start.9 = (bf16[32,1664]{1,0:T(8,128)(2,1)S(1)}, bf16[32,1664]{1,0:T(8,128)(2,1)S(1)}, u32[]{:S(2)}, u32[]{:S(2)}) collective-permute-start(bf16[32,1664]{1,0:T(8,128)(2,1)S(1)} %relay.1), channel_id=1, source_target_pairs={{0,4},{4,0},{8,12},{12,8},{1,5},{5,1},{9,13},{13,9},{2,6},{6,2},{1... | collective-permute-start | bytes 319496 | tf_op jit(solution)/shard_map/ppermute | solution.py:462
  24.6 1.1 %project.9 = f32[128,1024]{1,0:T(8,128)S(1)} custom-call(s32[1]{0:T(128)} %bitcast.2.own_ref.first_ref, bf16[32,1536]{1,0:T(8,128)(2,1)S(1)} %select.3.refs_0_, bf16[32,1536]{1,0:T(8,128)(2,1)S(1)} %collective-permute-done.refs_1_, bf16[32,1536]{1,0:T(8,128)(2,1)S(1)} %collective-permute-done.1.after_ref.refs_2_, ...), custom_call_target="tpu_custom_call" | custom-call | flops 7000000000 | bytes 1024 | tf_op jit(solution)/shard_map/project/pallas_call | solution.py:153
  25.7 0.1 add_convert_fusion.1.refs_5_.refs_0_.refs_2_
  25.8 0.6 %collective-permute-start.6 = (bf16[128,1024]{1,0:T(8,128)(2,1)S(1)}, bf16[128,1024]{1,0:T(8,128)(2,1)S(1)}, u32[]{:S(2)}, u32[]{:S(2)}) collective-permute-start(bf16[128,1024]{1,0:T(8,128)(2,1)S(1)} %add_convert_fusion.1.refs_5_.refs_0_.refs_2_), channel_id=1, source_target_pairs={{0,2},{1,3},{2,0},{3,1},{4,6},{5,7},{6,4},{7,5},{8,10},{9,11},{10,... | collective-permute-start | bytes 786440 | tf_op jit(solution)/shard_map/ppermute | solution.py:462
  26.4 1.8 %collective-permute-done.9.refs_3_.refs_4_.refs_5_.refs_9_ = bf16[32,1664]{1,0:T(8,128)(2,1)S(1)} collective-permute-done((bf16[32,1664]{1,0:T(8,128)(2,1)S(1)}, bf16[32,1664]{1,0:T(8,128)(2,1)S(1)}, u32[]{:S(2)}, u32[]{:S(2)}) %collective-permute-start.9) | collective-permute-done | bytes 106528 | tf_op jit(solution)/shard_map/ppermute | solution.py:462
  28.2 1.1 %project.10.refs_5_ = bf16[128,1024]{1,0:T(8,128)(2,1)S(1)} custom-call(s32[1]{0:T(128)} %bitcast.1.other_ref.first_ref, bf16[32,1664]{1,0:T(8,128)(2,1)S(1)} %select_cot.1.refs_5_.refs_0_.refs_1_.refs_2_.refs_6_, bf16[32,1664]{1,0:T(8,128)(2,1)S(1)} %collective-permute-done.7.refs_1_.refs_2_.refs_3_.refs_7_, ...), custom_call_target="tpu_custom_call" | custom-call | flops 7000000000 | bytes 1024 | tf_op jit(solution)/shard_map/project/pallas_call | solution.py:153
  29.4 0.1 collective-permute-start.10
  29.4 1.1 %project.11 = f32[128,1024]{1,0:T(8,128)S(1)} custom-call(s32[1]{0:T(128)} %bitcast.2.own_ref.first_ref, bf16[32,1664]{1,0:T(8,128)(2,1)S(1)} %select_cot.1.refs_5_.refs_0_.refs_1_.refs_2_.refs_6_, bf16[32,1664]{1,0:T(8,128)(2,1)S(1)} %collective-permute-done.7.refs_1_.refs_2_.refs_3_.refs_7_, ...), custom_call_target="tpu_custom_call" | custom-call | flops 7000000000 | bytes 1024 | tf_op jit(solution)/shard_map/project/pallas_call | solution.py:153
  30.6 0.4 collective-permute-done.10
  31.0 0.1 add_convert_fusion.refs_2_.refs_4_
  31.0 0.6 %collective-permute-start.11 = (bf16[128,1024]{1,0:T(8,128)(2,1)S(1)}, bf16[128,1024]{1,0:T(8,128)(2,1)S(1)}, u32[]{:S(2)}, u32[]{:S(2)}) collective-permute-start(bf16[128,1024]{1,0:T(8,128)(2,1)S(1)} %add_convert_fusion.refs_2_.refs_4_), channel_id=1, source_target_pairs={{0,2},{1,3},{2,0},{3,1},{4,6},{5,7},{6,4},{7,5},{8,10},{9,11},{10,... | collective-permute-start | bytes 786440 | tf_op jit(solution)/shard_map/ppermute | solution.py:462
  31.6 0.1 hidden.2.refs_0_
  31.7 0.1 collective-permute-start.13
  31.8 2.1 %grad_out.3 = (f32[2048,1536]{1,0:T(8,128)}, f32[8,128]{1,0:T(8,128)S(1)}) custom-call(s32[1]{0:T(128)} %bitcast.2.own_ref.first_ref, s32[1]{0:T(128)} %bitcast.1.other_ref.first_ref, bf16[128,512]{1,0:T(8,128)(2,1)S(1)} %hidden.2.refs_0_, bf16[32,1664]{1,0:T(8,128)(2,1)S(1)} %select_cot.1.refs_5_.refs_0_.refs_1_.refs_2_.refs_6_, ...), custom_call_target="tpu_custom_call" | custom-call | flops 7000000000 | bytes 1024 | tf_op jit(solution)/shard_map/grad_out/pallas_call | solution.py:350
  33.9 0.7 %collective-permute-done.6.refs_1_.refs_3_ = bf16[128,1024]{1,0:T(8,128)(2,1)S(1)} collective-permute-done((bf16[128,1024]{1,0:T(8,128)(2,1)S(1)}, bf16[128,1024]{1,0:T(8,128)(2,1)S(1)}, u32[]{:S(2)}, u32[]{:S(2)}) %collective-permute-start.6) | collective-permute-done | bytes 262176 | tf_op jit(solution)/shard_map/ppermute | solution.py:462
  34.7 0.1 hidden.3.refs_1_
  34.8 0.1 collective-permute-start.12
  34.8 3.2 %grad_out.4 = (f32[2048,1536]{1,0:T(8,128)}, f32[8,128]{1,0:T(8,128)S(1)}) custom-call(s32[1]{0:T(128)} %bitcast.2.own_ref.first_ref, s32[1]{0:T(128)} %bitcast.1.other_ref.first_ref, bf16[128,512]{1,0:T(8,128)(2,1)S(1)} %collective-permute-done.13.refs_0_, bf16[128,512]{1,0:T(8,128)(2,1)S(1)} %hidden.3.refs_1_, ...), custom_call_target="tpu_custom_call", output_to_operand_aliasing={{0}: (8, {})} | custom-call | flops 7000000000 | bytes 1024 | tf_op jit(solution)/shard_map/grad_out/pallas_call | solution.py:350
  38.1 2.1 %grad_out.5 = (f32[2048,1536]{1,0:T(8,128)}, f32[8,128]{1,0:T(8,128)S(1)}) custom-call(s32[1]{0:T(128)} %bitcast.2.own_ref.first_ref, s32[1]{0:T(128)} %bitcast.1.other_ref.first_ref, bf16[128,512]{1,0:T(8,128)(2,1)S(1)} %collective-permute-done.12.refs_0_, ...), custom_call_target="tpu_custom_call", output_to_operand_aliasing={{0}: (8, {})} | custom-call | flops 7000000000 | bytes 1024 | tf_op jit(solution)/shard_map/grad_out/pallas_call | solution.py:350
  40.2 0.6 pre.1.pre_ref.mine_ref
  40.8 0.6 collective-permute-start.14
  41.3 1.0 %row_own.1.own_ref = f32[128,1536]{1,0:T(8,128)S(1)} custom-call(s32[1]{0:T(128)} %bitcast.2.own_ref.first_ref, bf16[128,2176]{1,0:T(8,128)(2,1)S(1)} %pre.1.pre_ref.mine_ref, bf16[2,2048,1536]{2,1,0:T(8,128)(2,1)S(1)} %bitcast.7), custom_call_target="tpu_custom_call" | custom-call | flops 7000000000 | bytes 1024 | tf_op jit(solution)/shard_map/row_own/pallas_call | solution.py:247
  42.3 0.6 %collective-permute-done.14.pre_ref.peer_ref = bf16[128,2176]{1,0:T(8,128)(2,1)S(1)} collective-permute-done((bf16[128,2176]{1,0:T(8,128)(2,1)S(1)}, bf16[128,2176]{1,0:T(8,128)(2,1)S(1)}, u32[]{:S(2)}, u32[]{:S(2)}) %collective-permute-start.14) | collective-permute-done | bytes 557088 | tf_op jit(solution)/shard_map/ppermute | solution.py:462
  42.9 1.0 %row_rest.1 = (f32[32,1664]{1,0:T(8,128)S(1)}, bf16[32,1664]{1,0:T(8,128)(2,1)S(1)}, bf16[32,1664]{1,0:T(8,128)(2,1)S(1)}, bf16[32,1664]{1,0:T(8,128)(2,1)S(1)}) custom-call(s32[1]{0:T(128)} %bitcast.1.other_ref.first_ref, f32[128,1536]{1,0:T(8,128)S(1)} %row_own.1.own_ref, bf16[128,2176]{1,0:T(8,128)(2,1)S(1)} %pre.1.pre_ref.mine_ref, ...), custom_call_target="tpu_custom_call" | custom-call | flops 7000000000 | bytes 1024 | tf_op jit(solution)/shard_map/row_rest/pallas_call | solution.py:286
  43.9 1.5 %collective-permute-start.15 = (bf16[32,1664]{1,0:T(8,128)(2,1)S(1)}, bf16[32,1664]{1,0:T(8,128)(2,1)S(1)}, u32[]{:S(2)}, u32[]{:S(2)}) collective-permute-start(bf16[32,1664]{1,0:T(8,128)(2,1)S(1)} %get-tuple-element.22), channel_id=1, source_target_pairs={{0,4},{4,0},{8,12},{12,8},{1,5},{5,1},{9,13},{13,9},{2,6},{6,2},{1... | collective-permute-start | bytes 319496 | tf_op jit(solution)/shard_map/ppermute | solution.py:462
  45.4 1.6 %collective-permute-start.16 = (bf16[32,1664]{1,0:T(8,128)(2,1)S(1)}, bf16[32,1664]{1,0:T(8,128)(2,1)S(1)}, u32[]{:S(2)}, u32[]{:S(2)}) collective-permute-start(bf16[32,1664]{1,0:T(8,128)(2,1)S(1)} %get-tuple-element.23), channel_id=1, source_target_pairs={{0,8},{4,12},{8,0},{12,4},{1,9},{5,13},{9,1},{13,5},{2,10},{6,14},... | collective-permute-start | bytes 319496 | tf_op jit(solution)/shard_map/ppermute | solution.py:462
  47.0 1.4 %collective-permute-start.17 = (bf16[32,1664]{1,0:T(8,128)(2,1)S(1)}, bf16[32,1664]{1,0:T(8,128)(2,1)S(1)}, u32[]{:S(2)}, u32[]{:S(2)}) collective-permute-start(bf16[32,1664]{1,0:T(8,128)(2,1)S(1)} %get-tuple-element.24), channel_id=1, source_target_pairs={{0,12},{4,8},{8,4},{12,0},{1,13},{5,9},{9,5},{13,1},{2,14},{6,10},... | collective-permute-start | bytes 319496 | tf_op jit(solution)/shard_map/ppermute | solution.py:462
  48.4 8.8 %grad_in.1 = f32[2,2048,1536]{2,1,0:T(8,128)} custom-call(s32[1]{0:T(128)} %bitcast.2.own_ref.first_ref, s32[1]{0:T(128)} %bitcast.1.other_ref.first_ref, bf16[128,2176]{1,0:T(8,128)(2,1)S(1)} %pre.1.pre_ref.mine_ref, bf16[128,2176]{1,0:T(8,128)(2,1)S(1)} %collective-permute-done.14.pre_ref.peer_ref, bf16[32,1536]{1,0:T(8,128)(2,1)S(1)} %select.3.refs_0_, ...), custom_call_target="tpu_custom_call" | custom-call | flops 7000000000 | bytes 1024 | tf_op jit(solution)/shard_map/grad_in/pallas_call | solution.py:408
  57.3 1.2 %place.1 = (bf16[128,1536]{1,0:T(8,128)(2,1)}, bf16[2,128]{1,0:T(2,128)(2,1)}) custom-call(s32[2,128]{1,0:T(2,128)S(1)} %bitcast.14, f32[32,1664]{1,0:T(8,128)S(1)} %get-tuple-element.21.refs_0_, bf16[32,1664]{1,0:T(8,128)(2,1)S(1)} %collective-permute-done.15.refs_1_, bf16[32,1664]{1,0:T(8,128)(2,1)S(1)} %collective-permute-done.16.refs_2_, ...), custom_call_target="tpu_custom_call" | custom-call | flops 7000000000 | bytes 1024 | tf_op jit(solution)/shard_map/place/pallas_call | solution.py:447
  (24 shorter events, 0.1 us)
Async XLA Ops:
  0.6 16.2 %slice-start = ((s8[12582912]{0:T(1024)(128)(4,1)}), s8[4194304]{0:T(1024)(128)(4,1)S(1)}, s32[]{:S(2)}) async-start(s8[12582912]{0:T(1024)(128)(4,1)} %bitcast.6), calls=%async_computation | async-start | bytes 8388608
  0.6 16.2 %slice-start.1 = ((s8[12582912]{0:T(1024)(128)(4,1)}), s8[4194304]{0:T(1024)(128)(4,1)S(1)}, s32[]{:S(2)}) async-start(s8[12582912]{0:T(1024)(128)(4,1)} %bitcast.6), calls=%async_computation.1 | async-start | bytes 8388608
  2.2 8.9 %collective-permute-start.1 = (bf16[32,1536]{1,0:T(8,128)(2,1)S(1)}, bf16[32,1536]{1,0:T(8,128)(2,1)S(1)}, u32[]{:S(2)}, u32[]{:S(2)}) collective-permute-start(bf16[32,1536]{1,0:T(8,128)(2,1)S(1)} %select.3.refs_0_), channel_id=1, source_target_pairs={{0,8},{4,12},{8,0},{12,4},{1,9},{5,13},{9,1},{13,5},{2,10},{6,14},... | collective-permute-start | bytes 294920 | tf_op jit(solution)/shard_map/ppermute | solution.py:462
  6.3 10.6 %collective-permute-start = (bf16[32,1536]{1,0:T(8,128)(2,1)S(1)}, bf16[32,1536]{1,0:T(8,128)(2,1)S(1)}, u32[]{:S(2)}, u32[]{:S(2)}) collective-permute-start(bf16[32,1536]{1,0:T(8,128)(2,1)S(1)} %select.3.refs_0_), channel_id=1, source_target_pairs={{0,4},{4,0},{8,12},{12,8},{1,5},{5,1},{9,13},{13,9},{2,6},{6,2},{1... | collective-permute-start | bytes 294920 | tf_op jit(solution)/shard_map/ppermute | solution.py:462
  11.0 5.8 %collective-permute-start.2 = (bf16[32,1536]{1,0:T(8,128)(2,1)S(1)}, bf16[32,1536]{1,0:T(8,128)(2,1)S(1)}, u32[]{:S(2)}, u32[]{:S(2)}) collective-permute-start(bf16[32,1536]{1,0:T(8,128)(2,1)S(1)} %collective-permute-done.1.after_ref.refs_2_), channel_id=1, source_target_pairs={{0,4},{4,0},{8,12},{12,8},{1,5},{5,1},{9,13},{13,9},{2,6},{6,2},{1... | collective-permute-start | bytes 294920 | tf_op jit(solution)/shard_map/ppermute | solution.py:462
  11.9 5.0 %slice-start.2 = ((s8[12582912]{0:T(1024)(128)(4,1)}), s8[4194304]{0:T(1024)(128)(4,1)S(1)}, s32[]{:S(2)}) async-start(s8[12582912]{0:T(1024)(128)(4,1)} %bitcast.6), calls=%async_computation.2 | async-start | bytes 8388608
  13.4 9.1 %collective-permute-start.8 = (bf16[32,1664]{1,0:T(8,128)(2,1)S(1)}, bf16[32,1664]{1,0:T(8,128)(2,1)S(1)}, u32[]{:S(2)}, u32[]{:S(2)}) collective-permute-start(bf16[32,1664]{1,0:T(8,128)(2,1)S(1)} %select_cot.1.refs_5_.refs_0_.refs_1_.refs_2_.refs_6_), channel_id=1, source_target_pairs={{0,8},{4,12},{8,0},{12,4},{1,9},{5,13},{9,1},{13,5},{2,10},{6,14},... | collective-permute-start | bytes 319496 | tf_op jit(solution)/shard_map/ppermute | solution.py:462
  16.8 9.6 %collective-permute-start.7 = (bf16[32,1664]{1,0:T(8,128)(2,1)S(1)}, bf16[32,1664]{1,0:T(8,128)(2,1)S(1)}, u32[]{:S(2)}, u32[]{:S(2)}) collective-permute-start(bf16[32,1664]{1,0:T(8,128)(2,1)S(1)} %select_cot.1.refs_5_.refs_0_.refs_1_.refs_2_.refs_6_), channel_id=1, source_target_pairs={{0,4},{4,0},{8,12},{12,8},{1,5},{5,1},{9,13},{13,9},{2,6},{6,2},{1... | collective-permute-start | bytes 319496 | tf_op jit(solution)/shard_map/ppermute | solution.py:462
  18.0 1.6 %collective-permute-start.3 = (bf16[128,1024]{1,0:T(8,128)(2,1)S(1)}, bf16[128,1024]{1,0:T(8,128)(2,1)S(1)}, u32[]{:S(2)}, u32[]{:S(2)}) collective-permute-start(bf16[128,1024]{1,0:T(8,128)(2,1)S(1)} %project.6.refs_5_), channel_id=1, source_target_pairs={{0,1},{1,0},{2,3},{3,2},{4,5},{5,4},{6,7},{7,6},{8,9},{9,8},{10,11... | collective-permute-start | bytes 786440 | tf_op jit(solution)/shard_map/ppermute | solution.py:462
  19.7 11.9 %collective-permute-start.4 = (bf16[128,1024]{1,0:T(8,128)(2,1)S(1)}, bf16[128,1024]{1,0:T(8,128)(2,1)S(1)}, u32[]{:S(2)}, u32[]{:S(2)}) collective-permute-start(bf16[128,1024]{1,0:T(8,128)(2,1)S(1)} %add_convert_fusion.2.refs_5_.refs_0_), channel_id=1, source_target_pairs={{0,2},{1,3},{2,0},{3,1},{4,6},{5,7},{6,4},{7,5},{8,10},{9,11},{10,... | collective-permute-start | bytes 786440 | tf_op jit(solution)/shard_map/ppermute | solution.py:462
  22.4 3.3 %collective-permute-start.5 = (bf16[128,1024]{1,0:T(8,128)(2,1)S(1)}, bf16[128,1024]{1,0:T(8,128)(2,1)S(1)}, u32[]{:S(2)}, u32[]{:S(2)}) collective-permute-start(bf16[128,1024]{1,0:T(8,128)(2,1)S(1)} %project.8.refs_5_.after_ref), channel_id=1, source_target_pairs={{0,1},{1,0},{2,3},{3,2},{4,5},{5,4},{6,7},{7,6},{8,9},{9,8},{10,11... | collective-permute-start | bytes 786440 | tf_op jit(solution)/shard_map/ppermute | solution.py:462
  22.5 5.7 %slice-start.3 = ((s8[6291456]{0:T(1024)(128)(4,1)}), s8[4194304]{0:T(1024)(128)(4,1)S(1)}, s32[]{:S(2)}) async-start(s8[6291456]{0:T(1024)(128)(4,1)} %bitcast.8), calls=%async_computation.3 | async-start | bytes 8388608
  22.5 5.7 %slice-start.4 = ((s8[6291456]{0:T(1024)(128)(4,1)}), s8[2097152]{0:T(1024)(128)(4,1)S(1)}, s32[]{:S(2)}) async-start(s8[6291456]{0:T(1024)(128)(4,1)} %bitcast.8), calls=%async_computation.4 | async-start | bytes 4194304
  22.5 5.7 %collective-permute-start.9 = (bf16[32,1664]{1,0:T(8,128)(2,1)S(1)}, bf16[32,1664]{1,0:T(8,128)(2,1)S(1)}, u32[]{:S(2)}, u32[]{:S(2)}) collective-permute-start(bf16[32,1664]{1,0:T(8,128)(2,1)S(1)} %relay.1), channel_id=1, source_target_pairs={{0,4},{4,0},{8,12},{12,8},{1,5},{5,1},{9,13},{13,9},{2,6},{6,2},{1... | collective-permute-start | bytes 319496 | tf_op jit(solution)/shard_map/ppermute | solution.py:462
  25.8 8.8 %collective-permute-start.6 = (bf16[128,1024]{1,0:T(8,128)(2,1)S(1)}, bf16[128,1024]{1,0:T(8,128)(2,1)S(1)}, u32[]{:S(2)}, u32[]{:S(2)}) collective-permute-start(bf16[128,1024]{1,0:T(8,128)(2,1)S(1)} %add_convert_fusion.1.refs_5_.refs_0_.refs_2_), channel_id=1, source_target_pairs={{0,2},{1,3},{2,0},{3,1},{4,6},{5,7},{6,4},{7,5},{8,10},{9,11},{10,... | collective-permute-start | bytes 786440 | tf_op jit(solution)/shard_map/ppermute | solution.py:462
  29.4 1.6 %collective-permute-start.10 = (bf16[128,1024]{1,0:T(8,128)(2,1)S(1)}, bf16[128,1024]{1,0:T(8,128)(2,1)S(1)}, u32[]{:S(2)}, u32[]{:S(2)}) collective-permute-start(bf16[128,1024]{1,0:T(8,128)(2,1)S(1)} %project.10.refs_5_), channel_id=1, source_target_pairs={{0,1},{1,0},{2,3},{3,2},{4,5},{5,4},{6,7},{7,6},{8,9},{9,8},{10,11... | collective-permute-start | bytes 786440 | tf_op jit(solution)/shard_map/ppermute | solution.py:462
  31.0 9.2 %collective-permute-start.11 = (bf16[128,1024]{1,0:T(8,128)(2,1)S(1)}, bf16[128,1024]{1,0:T(8,128)(2,1)S(1)}, u32[]{:S(2)}, u32[]{:S(2)}) collective-permute-start(bf16[128,1024]{1,0:T(8,128)(2,1)S(1)} %add_convert_fusion.refs_2_.refs_4_), channel_id=1, source_target_pairs={{0,2},{1,3},{2,0},{3,1},{4,6},{5,7},{6,4},{7,5},{8,10},{9,11},{10,... | collective-permute-start | bytes 786440 | tf_op jit(solution)/shard_map/ppermute | solution.py:462
  31.7 3.1 %collective-permute-start.13 = (bf16[128,512]{1,0:T(8,128)(2,1)S(1)}, bf16[128,512]{1,0:T(8,128)(2,1)S(1)}, u32[]{:S(2)}, u32[]{:S(2)}) collective-permute-start(bf16[128,512]{1,0:T(8,128)(2,1)S(1)} %hidden.2.refs_0_), channel_id=1, source_target_pairs={{0,1},{1,0},{2,3},{3,2},{4,5},{5,4},{6,7},{7,6},{8,9},{9,8},{10,11... | collective-permute-start | bytes 393224 | tf_op jit(solution)/shard_map/ppermute | solution.py:462
  34.8 3.3 %collective-permute-start.12 = (bf16[128,512]{1,0:T(8,128)(2,1)S(1)}, bf16[128,512]{1,0:T(8,128)(2,1)S(1)}, u32[]{:S(2)}, u32[]{:S(2)}) collective-permute-start(bf16[128,512]{1,0:T(8,128)(2,1)S(1)} %hidden.3.refs_1_), channel_id=1, source_target_pairs={{0,1},{1,0},{2,3},{3,2},{4,5},{5,4},{6,7},{7,6},{8,9},{9,8},{10,11... | collective-permute-start | bytes 393224 | tf_op jit(solution)/shard_map/ppermute | solution.py:462
  40.8 2.1 %collective-permute-start.14 = (bf16[128,2176]{1,0:T(8,128)(2,1)S(1)}, bf16[128,2176]{1,0:T(8,128)(2,1)S(1)}, u32[]{:S(2)}, u32[]{:S(2)}) collective-permute-start(bf16[128,2176]{1,0:T(8,128)(2,1)S(1)} %pre.1.pre_ref.mine_ref), channel_id=1, source_target_pairs={{0,1},{1,0},{2,3},{3,2},{4,5},{5,4},{6,7},{7,6},{8,9},{9,8},{10,11... | collective-permute-start | bytes 1671176 | tf_op jit(solution)/shard_map/ppermute | solution.py:462
  43.9 13.3 %collective-permute-start.15 = (bf16[32,1664]{1,0:T(8,128)(2,1)S(1)}, bf16[32,1664]{1,0:T(8,128)(2,1)S(1)}, u32[]{:S(2)}, u32[]{:S(2)}) collective-permute-start(bf16[32,1664]{1,0:T(8,128)(2,1)S(1)} %get-tuple-element.22), channel_id=1, source_target_pairs={{0,4},{4,0},{8,12},{12,8},{1,5},{5,1},{9,13},{13,9},{2,6},{6,2},{1... | collective-permute-start | bytes 319496 | tf_op jit(solution)/shard_map/ppermute | solution.py:462
  45.4 11.8 %collective-permute-start.16 = (bf16[32,1664]{1,0:T(8,128)(2,1)S(1)}, bf16[32,1664]{1,0:T(8,128)(2,1)S(1)}, u32[]{:S(2)}, u32[]{:S(2)}) collective-permute-start(bf16[32,1664]{1,0:T(8,128)(2,1)S(1)} %get-tuple-element.23), channel_id=1, source_target_pairs={{0,8},{4,12},{8,0},{12,4},{1,9},{5,13},{9,1},{13,5},{2,10},{6,14},... | collective-permute-start | bytes 319496 | tf_op jit(solution)/shard_map/ppermute | solution.py:462
  47.0 10.3 %copy-start = (s32[128,2]{0,1:T(2,128)S(1)}, s32[128,2]{0,1:T(2,128)}, u32[]{:S(2)}) copy-start(s32[128,2]{0,1:T(2,128)} %param.8) | copy-start | bytes 3076
  47.0 10.3 %collective-permute-start.17 = (bf16[32,1664]{1,0:T(8,128)(2,1)S(1)}, bf16[32,1664]{1,0:T(8,128)(2,1)S(1)}, u32[]{:S(2)}, u32[]{:S(2)}) collective-permute-start(bf16[32,1664]{1,0:T(8,128)(2,1)S(1)} %get-tuple-element.24), channel_id=1, source_target_pairs={{0,12},{4,8},{8,4},{12,0},{1,13},{5,9},{9,5},{13,1},{2,14},{6,10},... | collective-permute-start | bytes 319496 | tf_op jit(solution)/shard_map/ppermute | solution.py:462

commit v3 on v0

v3 whole, which is shorter than its diff:
```python
import functools

import jax
import jax.numpy as jnp
from jax import lax
from jax.experimental import pallas as pl
from jax.experimental.pallas import tpu as pltpu
from jax.sharding import PartitionSpec as P

F32 = jnp.float32
BF16 = jnp.bfloat16
VMEM = pl.BlockSpec(memory_space=pltpu.VMEM)
SMEM = pl.BlockSpec(memory_space=pltpu.SMEM)
ANY = pl.BlockSpec(memory_space=pl.ANY)
HBM = pl.BlockSpec(memory_space=pltpu.HBM)
LANES = 128
MIB = 2**20

NT = (((1,), (1,)), ((), ()))
TN = (((0,), (0,)), ((), ()))


def params(mib):
    return pltpu.CompilerParams(vmem_limit_bytes=mib * MIB)


def in_hbm(array):
    return pltpu.with_memory_space_constraint(array, pltpu.HBM)


def in_vmem(array):
    return pltpu.with_memory_space_constraint(array, pltpu.VMEM)


STEP = pl.CostEstimate(flops=7 * 10**9, bytes_accessed=1024, transcendentals=0)
FIRST = pl.CostEstimate(flops=12 * 10**9, bytes_accessed=1024, transcendentals=0)


def fetch(pairs, sems):
    copies = [pltpu.make_async_copy(a, b, sems.at[i]) for i, (a, b) in enumerate(pairs)]
    for copy in copies:
        copy.start()
    for copy in copies:
        copy.wait()


def slot_picker(ids, capacity):
    tok_rows = ids.shape[1]
    routed = jnp.logical_or(ids[0:1] == 0, ids[1:2] == 0)
    row = lax.broadcasted_iota(jnp.int32, (tok_rows, tok_rows), 0)
    col = lax.broadcasted_iota(jnp.int32, (tok_rows, tok_rows), 1)
    before = jnp.where(row < col, 1.0, 0.0).astype(BF16)
    flags = jnp.broadcast_to(jnp.where(routed, 1.0, 0.0), (capacity, tok_rows))
    position = jnp.dot(flags.astype(BF16), before, preferred_element_type=F32)
    slot = lax.broadcasted_iota(jnp.int32, (capacity, tok_rows), 0).astype(F32)
    return jnp.where(position == slot, flags, 0.0).astype(BF16)


def select_kernel(own_ref, other_ref, *refs):
    del own_ref, other_ref
    sources, (in_ref, grad_ref, picker_ref), scratch, sems = refs[:4], refs[4:7], refs[7:11], refs[11]
    fetch(zip(sources, scratch), sems)
    tok_ref, cot_ref, ids_ref, quant_ref = scratch
    capacity, width = in_ref.shape
    ids = ids_ref[...]
    picker = slot_picker(ids, capacity)
    picker_ref[...] = picker
    in_ref[...] = jnp.dot(picker, tok_ref[...], preferred_element_type=F32).astype(BF16)
    scaled = quant_ref[...].astype(F32)
    total = scaled[0:1] + scaled[1:2]
    routing = (scaled / total).astype(BF16).astype(F32)
    weight = jnp.where(ids == 0, routing, 0.0)
    rate = jnp.broadcast_to(weight[0:1] + weight[1:2], (LANES, ids.shape[1])).astype(BF16)
    grad_ref[:, :width] = jnp.dot(picker, cot_ref[...], preferred_element_type=F32).astype(BF16)
    grad_ref[:, width:] = lax.dot_general(picker, rate, NT, preferred_element_type=F32).astype(BF16)


def select(firsts, *arrays):
    tok_rows, width = arrays[0].shape
    capacity = tok_rows // 4
    return pl.pallas_call(
        select_kernel,
        in_specs=[SMEM] * 2 + [HBM] * 4,
        out_specs=[VMEM] * 3,
        out_shape=[
            jax.ShapeDtypeStruct((capacity, width), BF16),
            jax.ShapeDtypeStruct((capacity, width + LANES), BF16),
            jax.ShapeDtypeStruct((capacity, tok_rows), BF16),
        ],
        scratch_shapes=[pltpu.VMEM(a.shape, a.dtype) for a in arrays]
        + [pltpu.SemaphoreType.DMA((4,))],
        compiler_params=params(8),
        cost_estimate=FIRST,
        name="select",
    )(*firsts, *(in_hbm(a) for a in arrays))


def project_kernel(nblocks, width, units, first_ref, *refs):
    blocks, w_ref, out_ref = refs[:nblocks], refs[nblocks], refs[-1]
    kinds = w_ref.shape[0]
    half = out_ref.shape[1] // kinds
    rows = jnp.concatenate([b[:, :width] for b in blocks], axis=0)
    start = pl.multiple_of(first_ref[0], half)
    step = min(units, 512)
    at = 0
    for piece in range(0, half, units):
        for kind in range(kinds):
            for j in range(piece, piece + units, step):
                out_ref[:, at : at + step] = lax.dot_general(
                    rows, w_ref[kind, pl.ds(start + j, step), :], NT, preferred_element_type=F32
                ).astype(out_ref.dtype)
                at += step


def project(blocks, weight, first, units, out_type, after):
    kinds, hidden, width = weight.shape
    rows = sum(b.shape[0] for b in blocks)
    return pl.pallas_call(
        functools.partial(project_kernel, len(blocks), width, units),
        in_specs=[SMEM] + [VMEM] * (len(blocks) + 1) + [ANY] * len(after),
        out_specs=VMEM,
        out_shape=jax.ShapeDtypeStruct((rows, kinds * hidden // 2), out_type),
        compiler_params=params(24),
        cost_estimate=STEP,
        name="project",
    )(first, *blocks, in_vmem(weight), *after)


def add_kernel(mine_ref, arrived_ref, *out_refs):
    at = 0
    for out in out_refs:
        cut = slice(at, at + out.shape[1])
        out[...] = (mine_ref[:, cut] + arrived_ref[:, cut].astype(F32)).astype(BF16)
        at = cut.stop


def add(mine, arrived, cuts):
    rows, columns = mine.shape
    return pl.pallas_call(
        add_kernel,
        in_specs=[VMEM] * 2,
        out_specs=[VMEM] * cuts,
        out_shape=[jax.ShapeDtypeStruct((rows, columns // cuts), BF16)] * cuts,
        compiler_params=params(16),
        cost_estimate=STEP,
        name="add",
    )(mine, arrived)


def gate_up(refs, layout, units):
    at = 0
    for nparts, column in layout:
        parts, refs = refs[:nparts], refs[nparts:]
        sums = sum(p[:, column : column + 2 * units].astype(F32) for p in parts)
        yield slice(at, at + sums.shape[0]), sums[:, :units], sums[:, units:]
        at += sums.shape[0]


def hidden_kernel(layout, *refs):
    out_ref = refs[-1]
    for here, gate, up in gate_up(refs, layout, out_ref.shape[1]):
        out_ref[here, :] = (gate * jax.nn.sigmoid(gate) * up).astype(BF16)


def hidden_units(groups, units, after):
    flat = [p for parts, _ in groups for p in parts]
    rows = sum(parts[0].shape[0] for parts, _ in groups)
    return pl.pallas_call(
        functools.partial(hidden_kernel, [(len(parts), column) for parts, column in groups]),
        in_specs=[VMEM] * len(flat) + [ANY] * len(after),
        out_specs=VMEM,
        out_shape=jax.ShapeDtypeStruct((rows, units), BF16),
        compiler_params=params(16),
        cost_estimate=STEP,
        name="hidden",
    )(*flat, *after)


def pre_kernel(layouts, nback, nblocks, width, *refs):
    nsums = sum(n for layout in layouts for n, _ in layout)
    back_parts = refs[nsums : nsums + nback]
    blocks = refs[nsums + nback :][:nblocks]
    out_ref = refs[-1]
    half = back_parts[0].shape[1]
    units = half // len(layouts)
    rates = jnp.concatenate([b[:, width : width + 1].astype(F32) for b in blocks], axis=0)
    routes = {}
    for i, layout in enumerate(layouts):
        first, second = slice(i * units, (i + 1) * units), slice(half + i * units, half + (i + 1) * units)
        for here, gate, up in gate_up(refs, layout, units):
            s = jax.nn.sigmoid(gate)
            back = sum(p[here, first].astype(F32) for p in back_parts)
            hidden = (gate * s * up).astype(BF16).astype(F32)
            route = jnp.sum(hidden * back, axis=1, keepdims=True)
            routes[here.start] = routes[here.start] + route if i else route
            grad = rates[here] * back
            out_ref[here, first] = (grad * up * s * (1.0 + gate * (1.0 - s))).astype(BF16)
            out_ref[here, second] = (grad * gate * s).astype(BF16)
            if i == len(layouts) - 1:
                out_ref[here, 2 * half :] = high_low(routes[here.start])
        refs = refs[sum(n for n, _ in layout) :]


def high_low(value):
    high = value.astype(BF16).astype(F32)
    low = value - high
    lane = lax.broadcasted_iota(jnp.int32, (value.shape[0], LANES), 1)
    return jnp.where(lane == 0, high, jnp.where(lane == 1, low, 0.0)).astype(BF16)


def pre_grads(chunks, back_parts, blocks, width, after):
    half = back_parts[0].shape[1]
    rows = back_parts[0].shape[0]
    flat = [p for groups in chunks for parts, _ in groups for p in parts]
    layouts = [[(len(parts), column) for parts, column in groups] for groups in chunks]
    return pl.pallas_call(
        functools.partial(pre_kernel, layouts, len(back_parts), len(blocks), width),
        in_specs=[VMEM] * (len(flat) + len(back_parts) + len(blocks)) + [ANY] * len(after),
        out_specs=VMEM,
        out_shape=jax.ShapeDtypeStruct((rows, 2 * half + LANES), BF16),
        compiler_params=params(16),
        cost_estimate=STEP,
        name="pre",
    )(*flat, *back_parts, *blocks, *after)


def row_part(pre_ref, w_ref, start):
    half = (pre_ref.shape[1] - LANES) // 2
    return sum(
        jnp.dot(
            pre_ref[:, k * half : (k + 1) * half],
            w_ref[k, pl.ds(start, half), :],
            preferred_element_type=F32,
        )
        for k in range(2)
    )


def row_rest_kernel(first_ref, own_ref, mine_ref, pre_ref, w_ref, *out_refs):
    half = (pre_ref.shape[1] - LANES) // 2
    width = own_ref.shape[1]
    start = pl.multiple_of(first_ref[0], half)
    total = (
        own_ref[...]
        + jnp.dot(pre_ref[:, :half], w_ref[0, pl.ds(start, half), :], preferred_element_type=F32)
        + jnp.dot(
            pre_ref[:, half : 2 * half], w_ref[1, pl.ds(start, half), :], preferred_element_type=F32
        )
    )
    lanes = mine_ref[:, 2 * half :].astype(F32) + pre_ref[:, 2 * half :].astype(F32)
    route = lanes[:, 0:1] + lanes[:, 1:2]
    at = 0
    for out in out_refs:
        rows = out.shape[0]
        out[:, :width] = total[at : at + rows].astype(out.dtype)
        if out.dtype == F32:
            out[:, width:] = jnp.broadcast_to(route[at : at + rows], (rows, LANES)) * jnp.where(
                lax.broadcasted_iota(jnp.int32, (rows, LANES), 1) == 0, 1.0, 0.0
            )
        else:
            out[:, width:] = high_low(route[at : at + rows])
        at += rows


def row_rest(own, mine, pre, weight, first, outs):
    rows, width = own.shape
    return pl.pallas_call(
        row_rest_kernel,
        in_specs=[SMEM] + [VMEM] * 4,
        out_specs=[VMEM] * len(outs),
        out_shape=[jax.ShapeDtypeStruct((n, width + LANES), kind) for n, kind in outs],
        compiler_params=params(24),
        cost_estimate=STEP,
        name="row_rest",
    )(first, own, mine, pre, in_vmem(weight))


def grads_kernel(outs, nin, ntok, ncot, nrows, nafter, nbefore, own_ref, other_ref, *refs):
    out_sources, refs = refs[: len(outs)], refs[len(outs) :]
    in_sources, refs = refs[:nin], refs[nin:]
    toks, refs = refs[:ntok], refs[ntok:]
    cots, refs = refs[:ncot], refs[ncot:]
    summed, refs = refs[:nrows], refs[nrows:]
    refs = refs[nafter + nbefore :]
    out_ref, *extra, rows_of, buf, sem = refs
    hidden, width = out_ref.shape[-2:]
    half = hidden // 2
    ring, step = buf.shape[:2]
    at = 0
    for t in toks:
        rows_of[at : at + t.shape[0], :] = t[...]
        at += t.shape[0]
    for c in cots:
        rows_of[at : at + c.shape[0], :] = (
            c[:, width : width + 1].astype(F32) * c[:, :width].astype(F32)
        ).astype(BF16)
        at += c.shape[0]
    starts = [pl.multiple_of(ref[0], half) for ref in (own_ref, other_ref)]
    tiles = []
    for source, (side, offset) in zip(out_sources, outs):
        for j in range(0, source.shape[1], step):
            tiles.append((source, j, out_ref.at[pl.ds(starts[side] + offset + j, step)]))
    for side, source in enumerate(in_sources):
        for kind in range(2):
            for j in range(0, half, step):
                target = out_ref.at[kind, pl.ds(starts[side] + j, step)]
                tiles.append((source, kind * half + j, target))
    copies = []
    for i, (source, column, target) in enumerate(tiles):
        if i >= ring:
            copies[i - ring].wait()
        buf[i % ring] = lax.dot_general(
            source[:, column : column + step], rows_of[...], TN, preferred_element_type=F32
        )
        copies.append(pltpu.make_async_copy(buf.at[i % ring], target, sem.at[i % ring]))
        copies[-1].start()
    for more in extra:
        more[...] = row_part(*summed, starts[0]) if summed else jnp.zeros_like(more)
    for copy in copies[max(0, len(copies) - ring) :]:
        copy.wait()


def grads(outs, ins, tok_blocks, cot_blocks, firsts, hidden, so_far, after=(), extra=None):
    width = tok_blocks[0].shape[1] if ins else cot_blocks[0].shape[1] - LANES
    sources = [piece[0] for piece in outs]
    places = [piece[1:] for piece in outs]
    rows = (sources + list(ins))[0].shape[0]
    units = [source.shape[1] for source in sources] + [hidden // 2 for _ in ins]
    step = min(units + [256])
    ring = min(8, (sum(units) + sum(units[len(sources) :])) // step)
    before = [] if so_far is None else [in_hbm(so_far)]
    toks = tok_blocks if ins else []
    shape = (2, hidden, width) if ins else (hidden, width)
    out_shape = [pltpu.HBM(shape, F32)]
    summed = []
    if extra == ():
        out_shape.append(jax.ShapeDtypeStruct((8, LANES), F32))
    elif extra:
        out_shape.append(jax.ShapeDtypeStruct((rows, width), F32))
        summed = [extra[0], in_vmem(extra[1])]
    operands = [*sources, *ins, *toks, *cot_blocks, *summed]
    sizes = (len(ins), len(toks), len(cot_blocks), len(summed), len(after), len(before))
    return pl.pallas_call(
        functools.partial(grads_kernel, places, *sizes),
        in_specs=[SMEM] * 2 + [VMEM] * len(operands) + [ANY] * len(after) + [HBM] * len(before),
        out_specs=[HBM] + [VMEM] * (len(out_shape) - 1),
        out_shape=out_shape,
        scratch_shapes=[
            pltpu.VMEM((rows, width), BF16),
            pltpu.VMEM((ring, step, width), F32),
            pltpu.SemaphoreType.DMA((ring,)),
        ],
        input_output_aliases=(
            {2 + len(operands) + len(after): 0} if before else {}
        ),
        compiler_params=params(28),
        cost_estimate=STEP,
        name="grads",
    )(*firsts, *operands, *after, *before)


def place_kernel(ids_ref, picker_ref, *refs):
    blocks, (in_ref, weight_ref) = refs[:-2], refs[-2:]
    width = in_ref.shape[1]
    capacity = picker_ref.shape[0]
    picker = picker_ref[...]
    total = sum(b[:, :width].astype(F32) for b in blocks)
    lanes = sum(b[:, width:].astype(F32) for b in blocks)
    in_ref[...] = lax.dot_general(
        picker, total.astype(BF16), TN, preferred_element_type=F32
    ).astype(BF16)
    route = jnp.broadcast_to(lanes[:, 0:1] + lanes[:, 1:2], (capacity, LANES))
    high = route.astype(BF16)
    low = (route - high.astype(F32)).astype(BF16)
    spread = lax.dot_general(high, picker, TN, preferred_element_type=F32) + lax.dot_general(
        low, picker, TN, preferred_element_type=F32
    )
    ids = ids_ref[...]
    weight_ref[...] = jnp.where(ids == 0, spread[: ids.shape[0]], 0.0).astype(BF16)


def place(expert_ids, picker, blocks):
    width = blocks[0].shape[1] - LANES
    return pl.pallas_call(
        place_kernel,
        in_specs=[VMEM] * (2 + len(blocks)),
        out_specs=[VMEM] * 2,
        out_shape=[
            jax.ShapeDtypeStruct((picker.shape[1], width), BF16),
            jax.ShapeDtypeStruct(expert_ids.shape, BF16),
        ],
        compiler_params=params(8),
        cost_estimate=STEP,
        name="place",
    )(expert_ids, picker, *blocks)


def swap(array, axis, size, distance):
    return lax.ppermute(array, axis, [(i, i ^ distance) for i in range(size)])


def relay_kernel(nblocks, *refs):
    blocks, out_ref = refs[:nblocks], refs[-1]
    at = 0
    for b in blocks:
        out_ref[at : at + b.shape[0], :] = b[...]
        at += b.shape[0]


def relay(blocks, after):
    rows = sum(b.shape[0] for b in blocks)
    return pl.pallas_call(
        functools.partial(relay_kernel, len(blocks)),
        in_specs=[VMEM] * len(blocks) + [ANY],
        out_specs=VMEM,
        out_shape=jax.ShapeDtypeStruct((rows, blocks[0].shape[1]), blocks[0].dtype),
        compiler_params=params(8),
        cost_estimate=STEP,
        name="relay",
    )(*blocks, after)


def per_device(dp, chips, tokens, cotangent, expert_ids, quantized, weight_in, weight_out):
    experts = 2 * chips
    width = tokens.shape[1]
    hidden = weight_in.shape[1]
    half = hidden // 2
    core = lax.rem(lax.axis_index("expert"), 2)
    firsts = [(c * half).astype(jnp.int32).reshape(1) for c in (core, 1 - core)]
    direct = dp == 4

    expert_ids, quantized = expert_ids.T, quantized.T
    weight_out = weight_out.reshape((1,) + weight_out.shape)
    send_in, send_grad, picker = select(firsts, tokens, cotangent, expert_ids, quantized)
    if direct:
        tok_blocks = [send_in] + [swap(send_in, "dp", dp, d) for d in range(1, dp)]
        cot_blocks = [send_grad] + [swap(send_grad, "dp", dp, d) for d in (1, 2)]
        groups = [tok_blocks[:2], tok_blocks[2:]]
    else:
        tok_blocks = [lax.all_gather(send_in, "dp", axis=0, tiled=True)]
        cot_blocks = [lax.all_gather(send_grad, "dp", axis=0, tiled=True)]
        groups = [tok_blocks]

    pieces, units = 1, half

    def chip_sums(blocks, weight, last, cuts=1, meanwhile=None):
        theirs = project(blocks, weight, firsts[1], units, BF16, [last])
        arrived = swap(theirs, "expert", experts, 1)
        last = meanwhile(theirs) if meanwhile is not None else theirs
        mine = project(blocks, weight, firsts[0], units, F32, [last])
        return add(mine, arrived, cuts)

    def all_chips(chip):
        return [chip] + [swap(chip, "expert", experts, 2 * k) for k in range(1, chips)]

    def pass_on(after):
        block = relay([send_grad], after)
        cot_blocks.append(swap(block, "dp", dp, 3))
        return block

    chunks, last = [[] for _ in range(pieces)], send_grad
    for blocks in groups[:-1]:
        (last,) = chip_sums(blocks, weight_in, last)
        parts = all_chips(last)
        for i, groups_of in enumerate(chunks):
            groups_of.append((parts, i * 2 * units))
    if direct:
        last = pass_on(last)
    cuts = chip_sums(groups[-1], weight_in, last, pieces)
    for groups_of, cut in zip(chunks, cuts):
        groups_of.append((all_chips(cut), 0))
    back = all_chips(*chip_sums(cot_blocks, weight_out, cuts[-1]))

    mine = hidden_units(chunks[0], units, [back[0]])
    peer = swap(mine, "expert", experts, 1)
    grad_weight_out, last = grads(
        [(mine, 0, 0)], [], [], cot_blocks, firsts, hidden, None, extra=()
    )
    pre = pre_grads(chunks, back, cot_blocks, width, [last])
    pre_peer = swap(pre, "expert", experts, 1)
    grad_weight_out, part = grads(
        [(peer, 1, 0)],
        [],
        [],
        cot_blocks,
        firsts,
        hidden,
        grad_weight_out,
        extra=(pre, weight_in),
    )
    if direct:
        cap = send_in.shape[0]
        outs = [(cap, F32)] + [(cap, BF16)] * (dp - 1)
        sent = row_rest(part, pre, pre_peer, weight_in, firsts[1], outs)
        arrived = [sent[0]] + [swap(sent[d], "dp", dp, d) for d in (2, 3, 1)]
    else:
        sent = row_rest(part, pre, pre_peer, weight_in, firsts[1], [(part.shape[0], F32)])
        arrived = [lax.psum_scatter(sent[0], "dp", scatter_dimension=0, tiled=True)]
    (grad_weight_in,) = grads(
        [],
        [pre, pre_peer],
        tok_blocks,
        [],
        firsts,
        hidden,
        None,
        [sent[0]],
    )
    input_grad, weight_grad = place(expert_ids, picker, arrived)
    return (input_grad, weight_grad.T, grad_weight_in, grad_weight_out)


def solution(mesh):
    return jax.shard_map(
        functools.partial(per_device, mesh.shape["dp"], mesh.shape["expert"] // 2),
        mesh=mesh,
        in_specs=(
            P(("group", "dp"), "expert"),
            P(("group", "dp"), "expert"),
            P(("group", "dp"), None),
            P(("group", "dp"), None),
            P(None, "dp", "expert"),
            P("dp", "expert"),
        ),
        out_specs=(
            P(("group", "dp"), "expert"),
            P(("group", "dp"), None),
            P("group", "dp", "expert"),
            P(("group", "dp"), "expert"),
        ),
        check_vma=False,
    )
```

time: 188 us -> 57.1 us (0.30)
  waiting for transfers between devices: 71.7 us -> 4.95 us
  blocking collectives: 51.8 us -> 0 us
  matrix products: 41.1 us -> 0 us
  Pallas kernels: 0 us -> 30.2 us
  starting transfers between devices: 0.08 us -> 20.9 us
  between operations: 15.4 us -> 0.88 us
  other arithmetic: 6.5 us -> 0.01 us
    psum x1 -> x0, waiting for transfers between devices: 67.4 us -> none  [per_device(): projected, back_hidden = lax.psum((part_proj, part_back), 'expert')]
    dot_general x8 -> x0, matrix products: 41.1 us -> none  [the longest x1 10.7 us: per_device(): jnp.einsum('rkh,rd->khd', pre_grad, rows_in, preferred_element_type=jnp.f...]
    all_gather x2 -> x0, blocking collectives: 31.7 us -> none  [the longest x1 16.2 us: per_device(): lax.all_gather(send_in, 'dp', axis=0, tiled=True)]
    pallas_call x0 -> x18, Pallas kernels: none -> 30.2 us  [the longest x3 15.2 us: grads(): pl.pallas_call(functools.partial(grads_kernel, places, *sizes), in_specs=...]
    ppermute x0 -> x17, starting transfers between devices: none -> 20.9 us  [swap(): return lax.ppermute(array, axis, [(i, i ^ distance) for i in range(size)])]
    unnamed x2 -> x0, blocking collectives: 20.1 us -> none
    ppermute x0 -> x17, waiting for transfers between devices: none -> 4.95 us  [swap(): return lax.ppermute(array, axis, [(i, i ^ distance) for i in range(size)])]
    reduce_scatter x1 -> x0, waiting for transfers between devices: 4.27 us -> none  [per_device(): lax.psum_scatter(row_part, 'dp', scatter_dimension=0, tiled=True)]
  transfers between devices with their start and end apart: 2 -> 17, of which waited for: 2 -> 3; matrix products, arithmetic and copies ran while one was open for 10% -> 0% of each run, Pallas kernels for 0% -> 46%
where the time goes in v3:
time: 57.1 us; the launch traced here: 57 us
  Pallas kernels  30.2 us (53%)
  starting transfers between devices  20.9 us (37%)
  waiting for transfers between devices  4.95 us (9%)
  between operations  0.88 us (2%)
    ppermute x17, starting transfers between devices, swap(): return lax.ppermute(array, axis, [(i, i ^ distance) for i in range(size)])  20.9 us
    pallas_call x3, Pallas kernels, grads(): pl.pallas_call(functools.partial(grads_kernel, places, *sizes), in_specs=...  15.2 us
    pallas_call x6, Pallas kernels, project(): pl.pallas_call(functools.partial(project_kernel, len(blocks), width, unit...  10.3 us
    ppermute x17, waiting for transfers between devices, swap(): return lax.ppermute(array, axis, [(i, i ^ distance) for i in range(size)])  4.95 us
    pallas_call x1, Pallas kernels, select(): pl.pallas_call(select_kernel, in_specs=[SMEM] * 2 + [HBM] * 4, out_specs=...  1.69 us
  transfers between devices with their start and end apart: 17, of which 3 were waited for; matrix products, arithmetic and copies ran while one was open for 0% of the time, Pallas kernels for 46%

profile of v3, /device:TPU:0, one launch (start us, length us, event | category | flops | bytes accessed | tf_op | source)
XLA Modules:
  0.0 57.0 jit_solution(18133848800798637285)
XLA Ops:
  0.6 1.7 %select.3 = (bf16[32,1536]{1,0:T(8,128)(2,1)S(1)}, bf16[32,1664]{1,0:T(8,128)(2,1)S(1)}, bf16[32,128]{1,0:T(8,128)(2,1)S(1)}) custom-call(s32[1]{0:T(128)} %bitcast.1.own_ref.first_ref, s32[1]{0:T(128)} %bitcast.2.other_ref.first_ref, bf16[128,1536]{1,0:T(8,128)(2,1)} %refs_0_.1, bf16[128,1536]{1,0:T(8,128)(2,1)} %refs_1_.1, s32[2,128]{1,0:T(2,128)} %bitcast.10, ...), custom_call_target="tpu_custom_call" | custom-call | flops 12000000000 | bytes 1024 | tf_op jit(solution)/shard_map/select/pallas_call | solution.py:81
  2.3 3.1 %collective-permute-start = (bf16[32,1536]{1,0:T(8,128)(2,1)S(1)}, bf16[32,1536]{1,0:T(8,128)(2,1)S(1)}, u32[]{:S(2)}, u32[]{:S(2)}) collective-permute-start(bf16[32,1536]{1,0:T(8,128)(2,1)S(1)} %get-tuple-element.18.refs_0_.refs_2_), channel_id=1, source_target_pairs={{0,4},{4,0},{8,12},{12,8},{1,5},{5,1},{9,13},{13,9},{2,6},{6,2},{1... | collective-permute-start | bytes 294920 | tf_op jit(solution)/shard_map/ppermute | solution.py:399
  5.4 2.6 %collective-permute-start.3 = (bf16[32,1536]{1,0:T(8,128)(2,1)S(1)}, bf16[32,1536]{1,0:T(8,128)(2,1)S(1)}, u32[]{:S(2)}, u32[]{:S(2)}) collective-permute-start(bf16[32,1536]{1,0:T(8,128)(2,1)S(1)} %get-tuple-element.18.refs_0_.refs_2_), channel_id=1, source_target_pairs={{0,8},{4,12},{8,0},{12,4},{1,9},{5,13},{9,1},{13,5},{2,10},{6,14},... | collective-permute-start | bytes 294920 | tf_op jit(solution)/shard_map/ppermute | solution.py:399
  8.0 0.0 collective-permute-start.4
  8.0 0.9 %collective-permute-start.7 = (bf16[32,1664]{1,0:T(8,128)(2,1)S(1)}, bf16[32,1664]{1,0:T(8,128)(2,1)S(1)}, u32[]{:S(2)}, u32[]{:S(2)}) collective-permute-start(bf16[32,1664]{1,0:T(8,128)(2,1)S(1)} %get-tuple-element.19.refs_3_.refs_0_.refs_1_.refs_6_), channel_id=1, source_target_pairs={{0,4},{4,0},{8,12},{12,8},{1,5},{5,1},{9,13},{13,9},{2,6},{6,2},{1... | collective-permute-start | bytes 319496 | tf_op jit(solution)/shard_map/ppermute | solution.py:399
  8.9 3.5 %collective-permute-start.8 = (bf16[32,1664]{1,0:T(8,128)(2,1)S(1)}, bf16[32,1664]{1,0:T(8,128)(2,1)S(1)}, u32[]{:S(2)}, u32[]{:S(2)}) collective-permute-start(bf16[32,1664]{1,0:T(8,128)(2,1)S(1)} %get-tuple-element.19.refs_3_.refs_0_.refs_1_.refs_6_), channel_id=1, source_target_pairs={{0,8},{4,12},{8,0},{12,4},{1,9},{5,13},{9,1},{13,5},{2,10},{6,14},... | collective-permute-start | bytes 319496 | tf_op jit(solution)/shard_map/ppermute | solution.py:399
  12.4 0.0 collective-permute-done.refs_1_.refs_3_
  12.4 2.0 %project.6.refs_3_ = bf16[64,2048]{1,0:T(8,128)(2,1)S(1)} custom-call(s32[1]{0:T(128)} %bitcast.2.other_ref.first_ref, bf16[32,1536]{1,0:T(8,128)(2,1)S(1)} %get-tuple-element.18.refs_0_.refs_2_, bf16[32,1536]{1,0:T(8,128)(2,1)S(1)} %collective-permute-done.refs_1_.refs_3_, bf16[2,2048,1536]{2,1,0:T(8,128)(2,1)S(1)} %copy-done, ...), custom_call_target="tpu_custom_call" | custom-call | flops 7000000000 | bytes 1024 | tf_op jit(solution)/shard_map/project/pallas_call | solution.py:118
  14.4 0.1 collective-permute-start.1
  14.5 2.0 %project.7.mine_ref = f32[64,2048]{1,0:T(8,128)S(1)} custom-call(s32[1]{0:T(128)} %bitcast.1.own_ref.first_ref, bf16[32,1536]{1,0:T(8,128)(2,1)S(1)} %get-tuple-element.18.refs_0_.refs_2_, bf16[32,1536]{1,0:T(8,128)(2,1)S(1)} %collective-permute-done.refs_1_.refs_3_, bf16[2,2048,1536]{2,1,0:T(8,128)(2,1)S(1)} %copy-done, bf16[64,2048]{1,0:T(8,128)(2,1)S(1)} %project.6.refs_3_), custom_call_target="tpu_custom_call" | custom-call | flops 7000000000 | bytes 1024 | tf_op jit(solution)/shard_map/project/pallas_call | solution.py:118
  16.5 0.0 collective-permute-done.1.arrived_ref
  16.5 0.1 add.3.refs_1_.refs_0_
  16.6 1.6 %collective-permute-start.2 = (bf16[64,2048]{1,0:T(8,128)(2,1)S(1)}, bf16[64,2048]{1,0:T(8,128)(2,1)S(1)}, u32[]{:S(2)}, u32[]{:S(2)}) collective-permute-start(bf16[64,2048]{1,0:T(8,128)(2,1)S(1)} %add.3.refs_1_.refs_0_), channel_id=1, source_target_pairs={{0,2},{1,3},{2,0},{3,1},{4,6},{5,7},{6,4},{7,5},{8,10},{9,11},{10,... | collective-permute-start | bytes 786440 | tf_op jit(solution)/shard_map/ppermute | solution.py:399
  18.2 0.0 collective-permute-done.3.refs_0_.refs_4_
  18.2 1.4 %collective-permute-start.9 = (bf16[32,1664]{1,0:T(8,128)(2,1)S(1)}, bf16[32,1664]{1,0:T(8,128)(2,1)S(1)}, u32[]{:S(2)}, u32[]{:S(2)}) collective-permute-start(bf16[32,1664]{1,0:T(8,128)(2,1)S(1)} %relay.1.refs_3_), channel_id=1, source_target_pairs={{0,12},{4,8},{8,4},{12,0},{1,13},{5,9},{9,5},{13,1},{2,14},{6,10},... | collective-permute-start | bytes 319496 | tf_op jit(solution)/shard_map/ppermute | solution.py:399
  19.6 0.0 collective-permute-done.4.refs_1_.refs_5_
  19.6 2.0 %project.8.refs_3_ = bf16[64,2048]{1,0:T(8,128)(2,1)S(1)} custom-call(s32[1]{0:T(128)} %bitcast.2.other_ref.first_ref, bf16[32,1536]{1,0:T(8,128)(2,1)S(1)} %collective-permute-done.3.refs_0_.refs_4_, bf16[32,1536]{1,0:T(8,128)(2,1)S(1)} %collective-permute-done.4.refs_1_.refs_5_, bf16[2,2048,1536]{2,1,0:T(8,128)(2,1)S(1)} %copy-done, ...), custom_call_target="tpu_custom_call" | custom-call | flops 7000000000 | bytes 1024 | tf_op jit(solution)/shard_map/project/pallas_call | solution.py:118
  21.6 0.1 collective-permute-start.5
  21.7 0.0 slice-start
  21.7 2.0 %project.9.mine_ref = f32[64,2048]{1,0:T(8,128)S(1)} custom-call(s32[1]{0:T(128)} %bitcast.1.own_ref.first_ref, bf16[32,1536]{1,0:T(8,128)(2,1)S(1)} %collective-permute-done.3.refs_0_.refs_4_, bf16[32,1536]{1,0:T(8,128)(2,1)S(1)} %collective-permute-done.4.refs_1_.refs_5_, bf16[2,2048,1536]{2,1,0:T(8,128)(2,1)S(1)} %copy-done, ...), custom_call_target="tpu_custom_call" | custom-call | flops 7000000000 | bytes 1024 | tf_op jit(solution)/shard_map/project/pallas_call | solution.py:118
  23.7 0.0 slice-start.1
  23.7 0.1 add.4.refs_5_.refs_2_
  23.8 1.6 %collective-permute-start.6 = (bf16[64,2048]{1,0:T(8,128)(2,1)S(1)}, bf16[64,2048]{1,0:T(8,128)(2,1)S(1)}, u32[]{:S(2)}, u32[]{:S(2)}) collective-permute-start(bf16[64,2048]{1,0:T(8,128)(2,1)S(1)} %add.4.refs_5_.refs_2_), channel_id=1, source_target_pairs={{0,2},{1,3},{2,0},{3,1},{4,6},{5,7},{6,4},{7,5},{8,10},{9,11},{10,... | collective-permute-start | bytes 786440 | tf_op jit(solution)/shard_map/ppermute | solution.py:399
  25.4 1.2 %project.10.refs_5_ = bf16[128,1024]{1,0:T(8,128)(2,1)S(1)} custom-call(s32[1]{0:T(128)} %bitcast.2.other_ref.first_ref, bf16[32,1664]{1,0:T(8,128)(2,1)S(1)} %get-tuple-element.19.refs_3_.refs_0_.refs_1_.refs_6_, bf16[32,1664]{1,0:T(8,128)(2,1)S(1)} %collective-permute-done.7.refs_1_.refs_2_.refs_7_, ...), custom_call_target="tpu_custom_call" | custom-call | flops 7000000000 | bytes 1024 | tf_op jit(solution)/shard_map/project/pallas_call | solution.py:118
  26.5 0.5 collective-permute-start.10
  27.0 1.1 %project.11.mine_ref = f32[128,1024]{1,0:T(8,128)S(1)} custom-call(s32[1]{0:T(128)} %bitcast.1.own_ref.first_ref, bf16[32,1664]{1,0:T(8,128)(2,1)S(1)} %get-tuple-element.19.refs_3_.refs_0_.refs_1_.refs_6_, bf16[32,1664]{1,0:T(8,128)(2,1)S(1)} %collective-permute-done.7.refs_1_.refs_2_.refs_7_, ...), custom_call_target="tpu_custom_call" | custom-call | flops 7000000000 | bytes 1024 | tf_op jit(solution)/shard_map/project/pallas_call | solution.py:118
  28.2 0.0 collective-permute-done.10.arrived_ref
  28.2 0.1 add.5.refs_4_
  28.3 1.6 %collective-permute-start.12 = (bf16[128,1024]{1,0:T(8,128)(2,1)S(1)}, bf16[128,1024]{1,0:T(8,128)(2,1)S(1)}, u32[]{:S(2)}, u32[]{:S(2)}) collective-permute-start(bf16[128,1024]{1,0:T(8,128)(2,1)S(1)} %add.5.refs_4_), channel_id=1, source_target_pairs={{0,2},{1,3},{2,0},{3,1},{4,6},{5,7},{6,4},{7,5},{8,10},{9,11},{10,... | collective-permute-start | bytes 786440 | tf_op jit(solution)/shard_map/ppermute | solution.py:399
  29.9 0.0 collective-permute-done.2.refs_1_
  29.9 3.1 %collective-permute-done.6.refs_3_ = bf16[64,2048]{1,0:T(8,128)(2,1)S(1)} collective-permute-done((bf16[64,2048]{1,0:T(8,128)(2,1)S(1)}, bf16[64,2048]{1,0:T(8,128)(2,1)S(1)}, u32[]{:S(2)}, u32[]{:S(2)}) %collective-permute-start.6) | collective-permute-done | bytes 262176 | tf_op jit(solution)/shard_map/ppermute | solution.py:399
  33.0 0.2 hidden.1.refs_0_
  33.1 0.1 collective-permute-start.11
  33.2 3.2 %grads.3 = (f32[2048,1536]{1,0:T(8,128)}, f32[8,128]{1,0:T(8,128)S(1)}) custom-call(s32[1]{0:T(128)} %bitcast.1.own_ref.first_ref, s32[1]{0:T(128)} %bitcast.2.other_ref.first_ref, bf16[128,1024]{1,0:T(8,128)(2,1)S(1)} %hidden.1.refs_0_, bf16[32,1664]{1,0:T(8,128)(2,1)S(1)} %get-tuple-element.19.refs_3_.refs_0_.refs_1_.refs_6_, ...), custom_call_target="tpu_custom_call" | custom-call | flops 7000000000 | bytes 1024 | tf_op jit(solution)/shard_map/grads/pallas_call | solution.py:343
  36.4 1.7 %collective-permute-done.12.refs_5_ = bf16[128,1024]{1,0:T(8,128)(2,1)S(1)} collective-permute-done((bf16[128,1024]{1,0:T(8,128)(2,1)S(1)}, bf16[128,1024]{1,0:T(8,128)(2,1)S(1)}, u32[]{:S(2)}, u32[]{:S(2)}) %collective-permute-start.12) | collective-permute-done | bytes 262176 | tf_op jit(solution)/shard_map/ppermute | solution.py:399
  38.2 0.6 %pre.1.refs_5_.mine_ref.refs_0_ = bf16[128,2176]{1,0:T(8,128)(2,1)S(1)} custom-call(bf16[64,2048]{1,0:T(8,128)(2,1)S(1)} %add.3.refs_1_.refs_0_, bf16[64,2048]{1,0:T(8,128)(2,1)S(1)} %collective-permute-done.2.refs_1_, bf16[64,2048]{1,0:T(8,128)(2,1)S(1)} %add.4.refs_5_.refs_2_, bf16[64,2048]{1,0:T(8,128)(2,1)S(1)} %collective-permute-done.6.refs_3_, ...), custom_call_target="tpu_custom_call" | custom-call | flops 7000000000 | bytes 1024 | tf_op jit(solution)/shard_map/pre/pallas_call | solution.py:216
  38.7 0.1 collective-permute-start.13
  38.8 0.0 collective-permute-done.11.refs_0_
  38.8 3.2 %grads.4 = (f32[2048,1536]{1,0:T(8,128)}, f32[128,1536]{1,0:T(8,128)S(1)}) custom-call(s32[1]{0:T(128)} %bitcast.1.own_ref.first_ref, s32[1]{0:T(128)} %bitcast.2.other_ref.first_ref, bf16[128,1024]{1,0:T(8,128)(2,1)S(1)} %collective-permute-done.11.refs_0_, ...), custom_call_target="tpu_custom_call", output_to_operand_aliasing={{0}: (9, {})} | custom-call | flops 7000000000 | bytes 1024 | tf_op jit(solution)/shard_map/grads/pallas_call | solution.py:343
  42.0 0.0 collective-permute-done.13.pre_ref.refs_1_
  42.0 1.0 %row_rest.1 = (f32[32,1664]{1,0:T(8,128)S(1)}, bf16[32,1664]{1,0:T(8,128)(2,1)S(1)}, bf16[32,1664]{1,0:T(8,128)(2,1)S(1)}, bf16[32,1664]{1,0:T(8,128)(2,1)S(1)}) custom-call(s32[1]{0:T(128)} %bitcast.2.other_ref.first_ref, f32[128,1536]{1,0:T(8,128)S(1)} %get-tuple-element.22.own_ref, bf16[128,2176]{1,0:T(8,128)(2,1)S(1)} %pre.1.refs_5_.mine_ref.refs_0_, ...), custom_call_target="tpu_custom_call" | custom-call | flops 7000000000 | bytes 1024 | tf_op jit(solution)/shard_map/row_rest/pallas_call | solution.py:267
  43.0 3.3 %collective-permute-start.14 = (bf16[32,1664]{1,0:T(8,128)(2,1)S(1)}, bf16[32,1664]{1,0:T(8,128)(2,1)S(1)}, u32[]{:S(2)}, u32[]{:S(2)}) collective-permute-start(bf16[32,1664]{1,0:T(8,128)(2,1)S(1)} %get-tuple-element.24), channel_id=1, source_target_pairs={{0,8},{4,12},{8,0},{12,4},{1,9},{5,13},{9,1},{13,5},{2,10},{6,14},... | collective-permute-start | bytes 319496 | tf_op jit(solution)/shard_map/ppermute | solution.py:399
  46.3 0.4 collective-permute-start.15
  46.8 0.2 collective-permute-start.16
  47.0 8.8 %grads.5 = f32[2,2048,1536]{2,1,0:T(8,128)} custom-call(s32[1]{0:T(128)} %bitcast.1.own_ref.first_ref, s32[1]{0:T(128)} %bitcast.2.other_ref.first_ref, bf16[128,2176]{1,0:T(8,128)(2,1)S(1)} %pre.1.refs_5_.mine_ref.refs_0_, bf16[128,2176]{1,0:T(8,128)(2,1)S(1)} %collective-permute-done.13.pre_ref.refs_1_, ...), custom_call_target="tpu_custom_call" | custom-call | flops 7000000000 | bytes 1024 | tf_op jit(solution)/shard_map/grads/pallas_call | solution.py:343
  55.8 0.0 collective-permute-done.15.refs_2_
  55.8 0.1 collective-permute-done.16.refs_3_
  55.9 1.1 %place.1 = (bf16[128,1536]{1,0:T(8,128)(2,1)}, bf16[2,128]{1,0:T(2,128)(2,1)}) custom-call(s32[2,128]{1,0:T(2,128)S(1)} %bitcast.11, bf16[32,128]{1,0:T(8,128)(2,1)S(1)} %get-tuple-element.17.picker_ref, f32[32,1664]{1,0:T(8,128)S(1)} %get-tuple-element.23.refs_0_.refs_6_, bf16[32,1664]{1,0:T(8,128)(2,1)S(1)} %collective-permute-done.14.refs_1_, ...), custom_call_target="tpu_custom_call" | custom-call | flops 7000000000 | bytes 1024 | tf_op jit(solution)/shard_map/place/pallas_call | solution.py:384
  (13 shorter events, 0.0 us)
Async XLA Ops:
  0.6 11.8 %copy-start = (bf16[2,2048,1536]{2,1,0:T(8,128)(2,1)S(1)}, bf16[2,2048,1536]{2,1,0:T(8,128)(2,1)}, u32[]{:S(2)}) copy-start(bf16[2,2048,1536]{2,1,0:T(8,128)(2,1)} %w_ref.1) | copy-start | bytes 37748740
  2.3 10.1 %collective-permute-start = (bf16[32,1536]{1,0:T(8,128)(2,1)S(1)}, bf16[32,1536]{1,0:T(8,128)(2,1)S(1)}, u32[]{:S(2)}, u32[]{:S(2)}) collective-permute-start(bf16[32,1536]{1,0:T(8,128)(2,1)S(1)} %get-tuple-element.18.refs_0_.refs_2_), channel_id=1, source_target_pairs={{0,4},{4,0},{8,12},{12,8},{1,5},{5,1},{9,13},{13,9},{2,6},{6,2},{1... | collective-permute-start | bytes 294920 | tf_op jit(solution)/shard_map/ppermute | solution.py:399
  5.4 12.7 %collective-permute-start.3 = (bf16[32,1536]{1,0:T(8,128)(2,1)S(1)}, bf16[32,1536]{1,0:T(8,128)(2,1)S(1)}, u32[]{:S(2)}, u32[]{:S(2)}) collective-permute-start(bf16[32,1536]{1,0:T(8,128)(2,1)S(1)} %get-tuple-element.18.refs_0_.refs_2_), channel_id=1, source_target_pairs={{0,8},{4,12},{8,0},{12,4},{1,9},{5,13},{9,1},{13,5},{2,10},{6,14},... | collective-permute-start | bytes 294920 | tf_op jit(solution)/shard_map/ppermute | solution.py:399
  8.0 11.6 %collective-permute-start.4 = (bf16[32,1536]{1,0:T(8,128)(2,1)S(1)}, bf16[32,1536]{1,0:T(8,128)(2,1)S(1)}, u32[]{:S(2)}, u32[]{:S(2)}) collective-permute-start(bf16[32,1536]{1,0:T(8,128)(2,1)S(1)} %get-tuple-element.18.refs_0_.refs_2_), channel_id=1, source_target_pairs={{0,12},{4,8},{8,4},{12,0},{1,13},{5,9},{9,5},{13,1},{2,14},{6,10},... | collective-permute-start | bytes 294920 | tf_op jit(solution)/shard_map/ppermute | solution.py:399
  8.0 17.3 %collective-permute-start.7 = (bf16[32,1664]{1,0:T(8,128)(2,1)S(1)}, bf16[32,1664]{1,0:T(8,128)(2,1)S(1)}, u32[]{:S(2)}, u32[]{:S(2)}) collective-permute-start(bf16[32,1664]{1,0:T(8,128)(2,1)S(1)} %get-tuple-element.19.refs_3_.refs_0_.refs_1_.refs_6_), channel_id=1, source_target_pairs={{0,4},{4,0},{8,12},{12,8},{1,5},{5,1},{9,13},{13,9},{2,6},{6,2},{1... | collective-permute-start | bytes 319496 | tf_op jit(solution)/shard_map/ppermute | solution.py:399
  8.9 16.4 %collective-permute-start.8 = (bf16[32,1664]{1,0:T(8,128)(2,1)S(1)}, bf16[32,1664]{1,0:T(8,128)(2,1)S(1)}, u32[]{:S(2)}, u32[]{:S(2)}) collective-permute-start(bf16[32,1664]{1,0:T(8,128)(2,1)S(1)} %get-tuple-element.19.refs_3_.refs_0_.refs_1_.refs_6_), channel_id=1, source_target_pairs={{0,8},{4,12},{8,0},{12,4},{1,9},{5,13},{9,1},{13,5},{2,10},{6,14},... | collective-permute-start | bytes 319496 | tf_op jit(solution)/shard_map/ppermute | solution.py:399
  14.4 2.1 %collective-permute-start.1 = (bf16[64,2048]{1,0:T(8,128)(2,1)S(1)}, bf16[64,2048]{1,0:T(8,128)(2,1)S(1)}, u32[]{:S(2)}, u32[]{:S(2)}) collective-permute-start(bf16[64,2048]{1,0:T(8,128)(2,1)S(1)} %project.6.refs_3_), channel_id=1, source_target_pairs={{0,1},{1,0},{2,3},{3,2},{4,5},{5,4},{6,7},{7,6},{8,9},{9,8},{10,11... | collective-permute-start | bytes 786440 | tf_op jit(solution)/shard_map/ppermute | solution.py:399
  16.6 13.2 %collective-permute-start.2 = (bf16[64,2048]{1,0:T(8,128)(2,1)S(1)}, bf16[64,2048]{1,0:T(8,128)(2,1)S(1)}, u32[]{:S(2)}, u32[]{:S(2)}) collective-permute-start(bf16[64,2048]{1,0:T(8,128)(2,1)S(1)} %add.3.refs_1_.refs_0_), channel_id=1, source_target_pairs={{0,2},{1,3},{2,0},{3,1},{4,6},{5,7},{6,4},{7,5},{8,10},{9,11},{10,... | collective-permute-start | bytes 786440 | tf_op jit(solution)/shard_map/ppermute | solution.py:399
  18.2 7.2 %collective-permute-start.9 = (bf16[32,1664]{1,0:T(8,128)(2,1)S(1)}, bf16[32,1664]{1,0:T(8,128)(2,1)S(1)}, u32[]{:S(2)}, u32[]{:S(2)}) collective-permute-start(bf16[32,1664]{1,0:T(8,128)(2,1)S(1)} %relay.1.refs_3_), channel_id=1, source_target_pairs={{0,12},{4,8},{8,4},{12,0},{1,13},{5,9},{9,5},{13,1},{2,14},{6,10},... | collective-permute-start | bytes 319496 | tf_op jit(solution)/shard_map/ppermute | solution.py:399
  21.6 2.1 %collective-permute-start.5 = (bf16[64,2048]{1,0:T(8,128)(2,1)S(1)}, bf16[64,2048]{1,0:T(8,128)(2,1)S(1)}, u32[]{:S(2)}, u32[]{:S(2)}) collective-permute-start(bf16[64,2048]{1,0:T(8,128)(2,1)S(1)} %project.8.refs_3_), channel_id=1, source_target_pairs={{0,1},{1,0},{2,3},{3,2},{4,5},{5,4},{6,7},{7,6},{8,9},{9,8},{10,11... | collective-permute-start | bytes 786440 | tf_op jit(solution)/shard_map/ppermute | solution.py:399
  21.7 3.7 %slice-start = ((s8[6291456]{0:T(1024)(128)(4,1)}), s8[4194304]{0:T(1024)(128)(4,1)S(1)}, s32[]{:S(2)}) async-start(s8[6291456]{0:T(1024)(128)(4,1)} %bitcast.6), calls=%async_computation | async-start | bytes 8388608
  23.7 1.7 %slice-start.1 = ((s8[6291456]{0:T(1024)(128)(4,1)}), s8[2097152]{0:T(1024)(128)(4,1)S(1)}, s32[]{:S(2)}) async-start(s8[6291456]{0:T(1024)(128)(4,1)} %bitcast.6), calls=%async_computation.1 | async-start | bytes 4194304
  23.8 9.2 %collective-permute-start.6 = (bf16[64,2048]{1,0:T(8,128)(2,1)S(1)}, bf16[64,2048]{1,0:T(8,128)(2,1)S(1)}, u32[]{:S(2)}, u32[]{:S(2)}) collective-permute-start(bf16[64,2048]{1,0:T(8,128)(2,1)S(1)} %add.4.refs_5_.refs_2_), channel_id=1, source_target_pairs={{0,2},{1,3},{2,0},{3,1},{4,6},{5,7},{6,4},{7,5},{8,10},{9,11},{10,... | collective-permute-start | bytes 786440 | tf_op jit(solution)/shard_map/ppermute | solution.py:399
  26.5 1.7 %collective-permute-start.10 = (bf16[128,1024]{1,0:T(8,128)(2,1)S(1)}, bf16[128,1024]{1,0:T(8,128)(2,1)S(1)}, u32[]{:S(2)}, u32[]{:S(2)}) collective-permute-start(bf16[128,1024]{1,0:T(8,128)(2,1)S(1)} %project.10.refs_5_), channel_id=1, source_target_pairs={{0,1},{1,0},{2,3},{3,2},{4,5},{5,4},{6,7},{7,6},{8,9},{9,8},{10,11... | collective-permute-start | bytes 786440 | tf_op jit(solution)/shard_map/ppermute | solution.py:399
  28.3 9.9 %collective-permute-start.12 = (bf16[128,1024]{1,0:T(8,128)(2,1)S(1)}, bf16[128,1024]{1,0:T(8,128)(2,1)S(1)}, u32[]{:S(2)}, u32[]{:S(2)}) collective-permute-start(bf16[128,1024]{1,0:T(8,128)(2,1)S(1)} %add.5.refs_4_), channel_id=1, source_target_pairs={{0,2},{1,3},{2,0},{3,1},{4,6},{5,7},{6,4},{7,5},{8,10},{9,11},{10,... | collective-permute-start | bytes 786440 | tf_op jit(solution)/shard_map/ppermute | solution.py:399
  33.1 5.7 %collective-permute-start.11 = (bf16[128,1024]{1,0:T(8,128)(2,1)S(1)}, bf16[128,1024]{1,0:T(8,128)(2,1)S(1)}, u32[]{:S(2)}, u32[]{:S(2)}) collective-permute-start(bf16[128,1024]{1,0:T(8,128)(2,1)S(1)} %hidden.1.refs_0_), channel_id=1, source_target_pairs={{0,1},{1,0},{2,3},{3,2},{4,5},{5,4},{6,7},{7,6},{8,9},{9,8},{10,11... | collective-permute-start | bytes 786440 | tf_op jit(solution)/shard_map/ppermute | solution.py:399
  38.7 3.3 %collective-permute-start.13 = (bf16[128,2176]{1,0:T(8,128)(2,1)S(1)}, bf16[128,2176]{1,0:T(8,128)(2,1)S(1)}, u32[]{:S(2)}, u32[]{:S(2)}) collective-permute-start(bf16[128,2176]{1,0:T(8,128)(2,1)S(1)} %pre.1.refs_5_.mine_ref.refs_0_), channel_id=1, source_target_pairs={{0,1},{1,0},{2,3},{3,2},{4,5},{5,4},{6,7},{7,6},{8,9},{9,8},{10,11... | collective-permute-start | bytes 1671176 | tf_op jit(solution)/shard_map/ppermute | solution.py:399
  43.0 12.8 %collective-permute-start.14 = (bf16[32,1664]{1,0:T(8,128)(2,1)S(1)}, bf16[32,1664]{1,0:T(8,128)(2,1)S(1)}, u32[]{:S(2)}, u32[]{:S(2)}) collective-permute-start(bf16[32,1664]{1,0:T(8,128)(2,1)S(1)} %get-tuple-element.24), channel_id=1, source_target_pairs={{0,8},{4,12},{8,0},{12,4},{1,9},{5,13},{9,1},{13,5},{2,10},{6,14},... | collective-permute-start | bytes 319496 | tf_op jit(solution)/shard_map/ppermute | solution.py:399
  46.3 9.5 %collective-permute-start.15 = (bf16[32,1664]{1,0:T(8,128)(2,1)S(1)}, bf16[32,1664]{1,0:T(8,128)(2,1)S(1)}, u32[]{:S(2)}, u32[]{:S(2)}) collective-permute-start(bf16[32,1664]{1,0:T(8,128)(2,1)S(1)} %get-tuple-element.25), channel_id=1, source_target_pairs={{0,12},{4,8},{8,4},{12,0},{1,13},{5,9},{9,5},{13,1},{2,14},{6,10},... | collective-permute-start | bytes 319496 | tf_op jit(solution)/shard_map/ppermute | solution.py:399
  46.8 9.1 %collective-permute-start.16 = (bf16[32,1664]{1,0:T(8,128)(2,1)S(1)}, bf16[32,1664]{1,0:T(8,128)(2,1)S(1)}, u32[]{:S(2)}, u32[]{:S(2)}) collective-permute-start(bf16[32,1664]{1,0:T(8,128)(2,1)S(1)} %get-tuple-element.26), channel_id=1, source_target_pairs={{0,4},{4,0},{8,12},{12,8},{1,5},{5,1},{9,13},{13,9},{2,6},{6,2},{1... | collective-permute-start | bytes 319496 | tf_op jit(solution)/shard_map/ppermute | solution.py:399
  47.0 8.9 %copy-start.1 = (s32[128,2]{0,1:T(2,128)S(1)}, s32[128,2]{0,1:T(2,128)}, u32[]{:S(2)}) copy-start(s32[128,2]{0,1:T(2,128)} %param.8) | copy-start | bytes 3076

commit v4 on v3

--- a/solution.py
+++ b/solution.py
@@ -32,16 +32,8 @@
     return pltpu.with_memory_space_constraint(array, pltpu.VMEM)
 
 
-STEP = pl.CostEstimate(flops=7 * 10**9, bytes_accessed=1024, transcendentals=0)
-FIRST = pl.CostEstimate(flops=12 * 10**9, bytes_accessed=1024, transcendentals=0)
-
-
-def fetch(pairs, sems):
-    copies = [pltpu.make_async_copy(a, b, sems.at[i]) for i, (a, b) in enumerate(pairs)]
-    for copy in copies:
-        copy.start()
-    for copy in copies:
-        copy.wait()
+STEP = pl.CostEstimate(flops=16 * 10**9, bytes_accessed=1024, transcendentals=0)
+FIRST = pl.CostEstimate(flops=18 * 10**9, bytes_accessed=1024, transcendentals=0)
 
 
 def slot_picker(ids, capacity):
@@ -59,20 +51,28 @@
 def select_kernel(own_ref, other_ref, *refs):
     del own_ref, other_ref
     sources, (in_ref, grad_ref, picker_ref), scratch, sems = refs[:4], refs[4:7], refs[7:11], refs[11]
-    fetch(zip(sources, scratch), sems)
+    copies = [
+        pltpu.make_async_copy(a, b, sems.at[i]) for i, (a, b) in enumerate(zip(sources, scratch))
+    ]
+    for copy in reversed(copies):
+        copy.start()
     tok_ref, cot_ref, ids_ref, quant_ref = scratch
+    copies[2].wait()
+    copies[3].wait()
     capacity, width = in_ref.shape
     ids = ids_ref[...]
     picker = slot_picker(ids, capacity)
     picker_ref[...] = picker
-    in_ref[...] = jnp.dot(picker, tok_ref[...], preferred_element_type=F32).astype(BF16)
     scaled = quant_ref[...].astype(F32)
     total = scaled[0:1] + scaled[1:2]
     routing = (scaled / total).astype(BF16).astype(F32)
     weight = jnp.where(ids == 0, routing, 0.0)
     rate = jnp.broadcast_to(weight[0:1] + weight[1:2], (LANES, ids.shape[1])).astype(BF16)
+    grad_ref[:, width:] = lax.dot_general(picker, rate, NT, preferred_element_type=F32).astype(BF16)
+    copies[0].wait()
+    in_ref[...] = jnp.dot(picker, tok_ref[...], preferred_element_type=F32).astype(BF16)
+    copies[1].wait()
     grad_ref[:, :width] = jnp.dot(picker, cot_ref[...], preferred_element_type=F32).astype(BF16)
-    grad_ref[:, width:] = lax.dot_general(picker, rate, NT, preferred_element_type=F32).astype(BF16)
 
 
 def select(firsts, *arrays):
@@ -297,9 +297,9 @@
         at += c.shape[0]
     starts = [pl.multiple_of(ref[0], half) for ref in (own_ref, other_ref)]
     tiles = []
-    for source, (side, offset) in zip(out_sources, outs):
-        for j in range(0, source.shape[1], step):
-            tiles.append((source, j, out_ref.at[pl.ds(starts[side] + offset + j, step)]))
+    for source, (side, first, end) in zip(out_sources, outs):
+        for j in range(first, end, step):
+            tiles.append((source, j, out_ref.at[pl.ds(starts[side] + j, step)]))
     for side, source in enumerate(in_sources):
         for kind in range(2):
             for j in range(0, half, step):
@@ -325,9 +325,8 @@
     sources = [piece[0] for piece in outs]
     places = [piece[1:] for piece in outs]
     rows = (sources + list(ins))[0].shape[0]
-    units = [source.shape[1] for source in sources] + [hidden // 2 for _ in ins]
-    step = min(units + [256])
-    ring = min(8, (sum(units) + sum(units[len(sources) :])) // step)
+    step = min(hidden // 2, 256)
+    ring = min(8, (sum(end - first for _, first, end in places) + len(ins) * hidden) // step)
     before = [] if so_far is None else [in_hbm(so_far)]
     toks = tok_blocks if ins else []
     shape = (2, hidden, width) if ins else (hidden, width)
@@ -473,13 +472,25 @@
 
     mine = hidden_units(chunks[0], units, [back[0]])
     peer = swap(mine, "expert", experts, 1)
-    grad_weight_out, last = grads(
-        [(mine, 0, 0)], [], [], cot_blocks, firsts, hidden, None, extra=()
-    )
-    pre = pre_grads(chunks, back, cot_blocks, width, [last])
+    middle = half // 2 if half % 512 == 0 else 0
+    grad_weight_out, *mark = grads(
+        [(mine, 0, 0, half)],
+        [],
+        [],
+        cot_blocks,
+        firsts,
+        hidden,
+        None,
+        extra=None if middle else (),
+    )
+    if middle:
+        grad_weight_out, *mark = grads(
+            [(peer, 1, 0, middle)], [], [], cot_blocks, firsts, hidden, grad_weight_out, extra=()
+        )
+    pre = pre_grads(chunks, back, cot_blocks, width, mark)
     pre_peer = swap(pre, "expert", experts, 1)
     grad_weight_out, part = grads(
-        [(peer, 1, 0)],
+        [(peer, 1, middle, half)],
         [],
         [],
         cot_blocks,

time: 57.1 us -> 57 us (level)
  waiting for transfers between devices: 4.95 us -> 3.18 us
  Pallas kernels: 30.2 us -> 31.3 us
    ppermute x17, waiting for transfers between devices: 4.95 us -> 3.18 us  [swap(): return lax.ppermute(array, axis, [(i, i ^ distance) for i in range(size)])]
    pallas_call x3 -> x4, Pallas kernels: 15.2 us -> 16.3 us  [grads(): pl.pallas_call(functools.partial(grads_kernel, places, *sizes), in_specs=...]
  transfers between devices with their start and end apart: 17 -> 17, of which waited for: 3 -> 1; matrix products, arithmetic and copies ran while one was open for 0% -> 0% of each run, Pallas kernels for 46% -> 48%
where the time goes in v4:
time: 57 us; the launch traced here: 56.7 us
  Pallas kernels  31.3 us (55%)
  starting transfers between devices  21.1 us (37%)
  waiting for transfers between devices  3.18 us (6%)
  between operations  1 us (2%)
    ppermute x17, starting transfers between devices, swap(): return lax.ppermute(array, axis, [(i, i ^ distance) for i in range(size)])  21.1 us
    pallas_call x4, Pallas kernels, grads(): pl.pallas_call(functools.partial(grads_kernel, places, *sizes), in_specs=...  16.3 us
    pallas_call x6, Pallas kernels, project(): pl.pallas_call(functools.partial(project_kernel, len(blocks), width, unit...  10.3 us
    ppermute x17, waiting for transfers between devices, swap(): return lax.ppermute(array, axis, [(i, i ^ distance) for i in range(size)])  3.18 us
    pallas_call x1, Pallas kernels, select(): pl.pallas_call(select_kernel, in_specs=[SMEM] * 2 + [HBM] * 4, out_specs=...  1.73 us
  transfers between devices with their start and end apart: 17, of which 1 were waited for; matrix products, arithmetic and copies ran while one was open for 0% of the time, Pallas kernels for 48%

profile of v4, /device:TPU:0, one launch (start us, length us, event | category | flops | bytes accessed | tf_op | source)
XLA Modules:
  0.0 56.7 jit_solution(14774149185290671018)
XLA Ops:
  0.6 1.7 %select.3 = (bf16[32,1536]{1,0:T(8,128)(2,1)S(1)}, bf16[32,1664]{1,0:T(8,128)(2,1)S(1)}, bf16[32,128]{1,0:T(8,128)(2,1)S(1)}) custom-call(s32[1]{0:T(128)} %bitcast.1.own_ref.first_ref, s32[1]{0:T(128)} %bitcast.2.other_ref.first_ref, bf16[128,1536]{1,0:T(8,128)(2,1)} %refs_0_.1, bf16[128,1536]{1,0:T(8,128)(2,1)} %refs_1_.1, s32[2,128]{1,0:T(2,128)} %bitcast.10, ...), custom_call_target="tpu_custom_call" | custom-call | flops 17999998976 | bytes 1024 | tf_op jit(solution)/shard_map/select/pallas_call | solution.py:81
  2.4 0.0 copy-start.1
  2.4 3.1 %collective-permute-start = (bf16[32,1536]{1,0:T(8,128)(2,1)S(1)}, bf16[32,1536]{1,0:T(8,128)(2,1)S(1)}, u32[]{:S(2)}, u32[]{:S(2)}) collective-permute-start(bf16[32,1536]{1,0:T(8,128)(2,1)S(1)} %get-tuple-element.18.refs_0_.refs_2_), channel_id=1, source_target_pairs={{0,4},{4,0},{8,12},{12,8},{1,5},{5,1},{9,13},{13,9},{2,6},{6,2},{1... | collective-permute-start | bytes 294920 | tf_op jit(solution)/shard_map/ppermute | solution.py:398
  5.5 2.6 %collective-permute-start.3 = (bf16[32,1536]{1,0:T(8,128)(2,1)S(1)}, bf16[32,1536]{1,0:T(8,128)(2,1)S(1)}, u32[]{:S(2)}, u32[]{:S(2)}) collective-permute-start(bf16[32,1536]{1,0:T(8,128)(2,1)S(1)} %get-tuple-element.18.refs_0_.refs_2_), channel_id=1, source_target_pairs={{0,8},{4,12},{8,0},{12,4},{1,9},{5,13},{9,1},{13,5},{2,10},{6,14},... | collective-permute-start | bytes 294920 | tf_op jit(solution)/shard_map/ppermute | solution.py:398
  8.1 0.0 collective-permute-start.4
  8.1 0.9 %collective-permute-start.7 = (bf16[32,1664]{1,0:T(8,128)(2,1)S(1)}, bf16[32,1664]{1,0:T(8,128)(2,1)S(1)}, u32[]{:S(2)}, u32[]{:S(2)}) collective-permute-start(bf16[32,1664]{1,0:T(8,128)(2,1)S(1)} %get-tuple-element.19.refs_3_.refs_0_.refs_1_.refs_6_), channel_id=1, source_target_pairs={{0,4},{4,0},{8,12},{12,8},{1,5},{5,1},{9,13},{13,9},{2,6},{6,2},{1... | collective-permute-start | bytes 319496 | tf_op jit(solution)/shard_map/ppermute | solution.py:398
  9.0 3.5 %collective-permute-start.8 = (bf16[32,1664]{1,0:T(8,128)(2,1)S(1)}, bf16[32,1664]{1,0:T(8,128)(2,1)S(1)}, u32[]{:S(2)}, u32[]{:S(2)}) collective-permute-start(bf16[32,1664]{1,0:T(8,128)(2,1)S(1)} %get-tuple-element.19.refs_3_.refs_0_.refs_1_.refs_6_), channel_id=1, source_target_pairs={{0,8},{4,12},{8,0},{12,4},{1,9},{5,13},{9,1},{13,5},{2,10},{6,14},... | collective-permute-start | bytes 319496 | tf_op jit(solution)/shard_map/ppermute | solution.py:398
  12.5 2.0 %project.6.refs_3_ = bf16[64,2048]{1,0:T(8,128)(2,1)S(1)} custom-call(s32[1]{0:T(128)} %bitcast.2.other_ref.first_ref, bf16[32,1536]{1,0:T(8,128)(2,1)S(1)} %get-tuple-element.18.refs_0_.refs_2_, bf16[32,1536]{1,0:T(8,128)(2,1)S(1)} %collective-permute-done.refs_1_.refs_3_, bf16[2,2048,1536]{2,1,0:T(8,128)(2,1)S(1)} %copy-done, ...), custom_call_target="tpu_custom_call" | custom-call | flops 16000000000 | bytes 1024 | tf_op jit(solution)/shard_map/project/pallas_call | solution.py:118
  14.5 0.1 collective-permute-start.1
  14.6 2.0 %project.7.mine_ref = f32[64,2048]{1,0:T(8,128)S(1)} custom-call(s32[1]{0:T(128)} %bitcast.1.own_ref.first_ref, bf16[32,1536]{1,0:T(8,128)(2,1)S(1)} %get-tuple-element.18.refs_0_.refs_2_, bf16[32,1536]{1,0:T(8,128)(2,1)S(1)} %collective-permute-done.refs_1_.refs_3_, bf16[2,2048,1536]{2,1,0:T(8,128)(2,1)S(1)} %copy-done, bf16[64,2048]{1,0:T(8,128)(2,1)S(1)} %project.6.refs_3_), custom_call_target="tpu_custom_call" | custom-call | flops 16000000000 | bytes 1024 | tf_op jit(solution)/shard_map/project/pallas_call | solution.py:118
  16.6 0.1 add.3.refs_1_.refs_0_
  16.7 1.6 %collective-permute-start.2 = (bf16[64,2048]{1,0:T(8,128)(2,1)S(1)}, bf16[64,2048]{1,0:T(8,128)(2,1)S(1)}, u32[]{:S(2)}, u32[]{:S(2)}) collective-permute-start(bf16[64,2048]{1,0:T(8,128)(2,1)S(1)} %add.3.refs_1_.refs_0_), channel_id=1, source_target_pairs={{0,2},{1,3},{2,0},{3,1},{4,6},{5,7},{6,4},{7,5},{8,10},{9,11},{10,... | collective-permute-start | bytes 786440 | tf_op jit(solution)/shard_map/ppermute | solution.py:398
  18.2 0.0 collective-permute-done.3.refs_0_.refs_4_
  18.2 1.4 %collective-permute-start.9 = (bf16[32,1664]{1,0:T(8,128)(2,1)S(1)}, bf16[32,1664]{1,0:T(8,128)(2,1)S(1)}, u32[]{:S(2)}, u32[]{:S(2)}) collective-permute-start(bf16[32,1664]{1,0:T(8,128)(2,1)S(1)} %relay.1.refs_3_), channel_id=1, source_target_pairs={{0,12},{4,8},{8,4},{12,0},{1,13},{5,9},{9,5},{13,1},{2,14},{6,10},... | collective-permute-start | bytes 319496 | tf_op jit(solution)/shard_map/ppermute | solution.py:398
  19.6 0.0 collective-permute-done.4.refs_1_.refs_5_
  19.6 2.0 %project.8.refs_3_ = bf16[64,2048]{1,0:T(8,128)(2,1)S(1)} custom-call(s32[1]{0:T(128)} %bitcast.2.other_ref.first_ref, bf16[32,1536]{1,0:T(8,128)(2,1)S(1)} %collective-permute-done.3.refs_0_.refs_4_, bf16[32,1536]{1,0:T(8,128)(2,1)S(1)} %collective-permute-done.4.refs_1_.refs_5_, bf16[2,2048,1536]{2,1,0:T(8,128)(2,1)S(1)} %copy-done, ...), custom_call_target="tpu_custom_call" | custom-call | flops 16000000000 | bytes 1024 | tf_op jit(solution)/shard_map/project/pallas_call | solution.py:118
  21.6 0.1 collective-permute-start.5
  21.7 0.0 slice-start
  21.8 2.0 %project.9.mine_ref = f32[64,2048]{1,0:T(8,128)S(1)} custom-call(s32[1]{0:T(128)} %bitcast.1.own_ref.first_ref, bf16[32,1536]{1,0:T(8,128)(2,1)S(1)} %collective-permute-done.3.refs_0_.refs_4_, bf16[32,1536]{1,0:T(8,128)(2,1)S(1)} %collective-permute-done.4.refs_1_.refs_5_, bf16[2,2048,1536]{2,1,0:T(8,128)(2,1)S(1)} %copy-done, ...), custom_call_target="tpu_custom_call" | custom-call | flops 16000000000 | bytes 1024 | tf_op jit(solution)/shard_map/project/pallas_call | solution.py:118
  23.8 0.0 slice-start.1
  23.8 0.1 add.4.refs_5_.refs_2_
  23.9 1.6 %collective-permute-start.6 = (bf16[64,2048]{1,0:T(8,128)(2,1)S(1)}, bf16[64,2048]{1,0:T(8,128)(2,1)S(1)}, u32[]{:S(2)}, u32[]{:S(2)}) collective-permute-start(bf16[64,2048]{1,0:T(8,128)(2,1)S(1)} %add.4.refs_5_.refs_2_), channel_id=1, source_target_pairs={{0,2},{1,3},{2,0},{3,1},{4,6},{5,7},{6,4},{7,5},{8,10},{9,11},{10,... | collective-permute-start | bytes 786440 | tf_op jit(solution)/shard_map/ppermute | solution.py:398
  25.4 1.2 %project.10.refs_5_ = bf16[128,1024]{1,0:T(8,128)(2,1)S(1)} custom-call(s32[1]{0:T(128)} %bitcast.2.other_ref.first_ref, bf16[32,1664]{1,0:T(8,128)(2,1)S(1)} %get-tuple-element.19.refs_3_.refs_0_.refs_1_.refs_6_, bf16[32,1664]{1,0:T(8,128)(2,1)S(1)} %collective-permute-done.7.refs_1_.refs_2_.refs_7_, ...), custom_call_target="tpu_custom_call" | custom-call | flops 16000000000 | bytes 1024 | tf_op jit(solution)/shard_map/project/pallas_call | solution.py:118
  26.6 0.5 collective-permute-start.10
  27.1 1.1 %project.11.mine_ref = f32[128,1024]{1,0:T(8,128)S(1)} custom-call(s32[1]{0:T(128)} %bitcast.1.own_ref.first_ref, bf16[32,1664]{1,0:T(8,128)(2,1)S(1)} %get-tuple-element.19.refs_3_.refs_0_.refs_1_.refs_6_, bf16[32,1664]{1,0:T(8,128)(2,1)S(1)} %collective-permute-done.7.refs_1_.refs_2_.refs_7_, ...), custom_call_target="tpu_custom_call" | custom-call | flops 16000000000 | bytes 1024 | tf_op jit(solution)/shard_map/project/pallas_call | solution.py:118
  28.2 0.0 collective-permute-done.10.arrived_ref
  28.3 0.1 add.5.refs_4_
  28.3 1.6 %collective-permute-start.12 = (bf16[128,1024]{1,0:T(8,128)(2,1)S(1)}, bf16[128,1024]{1,0:T(8,128)(2,1)S(1)}, u32[]{:S(2)}, u32[]{:S(2)}) collective-permute-start(bf16[128,1024]{1,0:T(8,128)(2,1)S(1)} %add.5.refs_4_), channel_id=1, source_target_pairs={{0,2},{1,3},{2,0},{3,1},{4,6},{5,7},{6,4},{7,5},{8,10},{9,11},{10,... | collective-permute-start | bytes 786440 | tf_op jit(solution)/shard_map/ppermute | solution.py:398
  29.9 0.0 collective-permute-done.2.refs_1_
  29.9 3.1 %collective-permute-done.6.refs_3_ = bf16[64,2048]{1,0:T(8,128)(2,1)S(1)} collective-permute-done((bf16[64,2048]{1,0:T(8,128)(2,1)S(1)}, bf16[64,2048]{1,0:T(8,128)(2,1)S(1)}, u32[]{:S(2)}, u32[]{:S(2)}) %collective-permute-start.6) | collective-permute-done | bytes 262176 | tf_op jit(solution)/shard_map/ppermute | solution.py:398
  33.0 0.2 hidden.1.refs_0_
  33.2 0.1 collective-permute-start.11
  33.3 3.2 %grads.4.refs_5_ = f32[2048,1536]{1,0:T(8,128)} custom-call(s32[1]{0:T(128)} %bitcast.1.own_ref.first_ref, s32[1]{0:T(128)} %bitcast.2.other_ref.first_ref, bf16[128,1024]{1,0:T(8,128)(2,1)S(1)} %hidden.1.refs_0_, bf16[32,1664]{1,0:T(8,128)(2,1)S(1)} %get-tuple-element.19.refs_3_.refs_0_.refs_1_.refs_6_, ...), custom_call_target="tpu_custom_call" | custom-call | flops 16000000000 | bytes 1024 | tf_op jit(solution)/shard_map/grads/pallas_call | solution.py:342
  36.5 0.0 collective-permute-done.11.refs_0_
  36.5 2.1 %grads.5 = (f32[2048,1536]{1,0:T(8,128)}, f32[8,128]{1,0:T(8,128)S(1)}) custom-call(s32[1]{0:T(128)} %bitcast.1.own_ref.first_ref, s32[1]{0:T(128)} %bitcast.2.other_ref.first_ref, bf16[128,1024]{1,0:T(8,128)(2,1)S(1)} %collective-permute-done.11.refs_0_, ...), custom_call_target="tpu_custom_call", output_to_operand_aliasing={{0}: (7, {})} | custom-call | flops 16000000000 | bytes 1024 | tf_op jit(solution)/shard_map/grads/pallas_call | solution.py:342
  38.6 0.0 collective-permute-done.12.refs_5_
  38.7 0.6 %pre.1.refs_5_.mine_ref.refs_0_ = bf16[128,2176]{1,0:T(8,128)(2,1)S(1)} custom-call(bf16[64,2048]{1,0:T(8,128)(2,1)S(1)} %add.3.refs_1_.refs_0_, bf16[64,2048]{1,0:T(8,128)(2,1)S(1)} %collective-permute-done.2.refs_1_, bf16[64,2048]{1,0:T(8,128)(2,1)S(1)} %add.4.refs_5_.refs_2_, bf16[64,2048]{1,0:T(8,128)(2,1)S(1)} %collective-permute-done.6.refs_3_, ...), custom_call_target="tpu_custom_call" | custom-call | flops 16000000000 | bytes 1024 | tf_op jit(solution)/shard_map/pre/pallas_call | solution.py:216
  39.2 0.6 collective-permute-start.13
  39.8 2.1 %grads.6 = (f32[2048,1536]{1,0:T(8,128)}, f32[128,1536]{1,0:T(8,128)S(1)}) custom-call(s32[1]{0:T(128)} %bitcast.1.own_ref.first_ref, s32[1]{0:T(128)} %bitcast.2.other_ref.first_ref, bf16[128,1024]{1,0:T(8,128)(2,1)S(1)} %collective-permute-done.11.refs_0_, ...), custom_call_target="tpu_custom_call", output_to_operand_aliasing={{0}: (9, {})} | custom-call | flops 16000000000 | bytes 1024 | tf_op jit(solution)/shard_map/grads/pallas_call | solution.py:342
  41.9 0.0 copy-start.2
  42.0 0.0 copy-start.4
  42.0 1.0 %row_rest.1 = (f32[32,1664]{1,0:T(8,128)S(1)}, bf16[32,1664]{1,0:T(8,128)(2,1)S(1)}, bf16[32,1664]{1,0:T(8,128)(2,1)S(1)}, bf16[32,1664]{1,0:T(8,128)(2,1)S(1)}) custom-call(s32[1]{0:T(128)} %bitcast.2.other_ref.first_ref, f32[128,1536]{1,0:T(8,128)S(1)} %get-tuple-element.22.own_ref, bf16[128,2176]{1,0:T(8,128)(2,1)S(1)} %pre.1.refs_5_.mine_ref.refs_0_, ...), custom_call_target="tpu_custom_call" | custom-call | flops 16000000000 | bytes 1024 | tf_op jit(solution)/shard_map/row_rest/pallas_call | solution.py:267
  43.0 3.1 %collective-permute-start.14 = (bf16[32,1664]{1,0:T(8,128)(2,1)S(1)}, bf16[32,1664]{1,0:T(8,128)(2,1)S(1)}, u32[]{:S(2)}, u32[]{:S(2)}) collective-permute-start(bf16[32,1664]{1,0:T(8,128)(2,1)S(1)} %get-tuple-element.24), channel_id=1, source_target_pairs={{0,8},{4,12},{8,0},{12,4},{1,9},{5,13},{9,1},{13,5},{2,10},{6,14},... | collective-permute-start | bytes 319496 | tf_op jit(solution)/shard_map/ppermute | solution.py:398
  46.1 0.6 %collective-permute-start.15 = (bf16[32,1664]{1,0:T(8,128)(2,1)S(1)}, bf16[32,1664]{1,0:T(8,128)(2,1)S(1)}, u32[]{:S(2)}, u32[]{:S(2)}) collective-permute-start(bf16[32,1664]{1,0:T(8,128)(2,1)S(1)} %get-tuple-element.25), channel_id=1, source_target_pairs={{0,12},{4,8},{8,4},{12,0},{1,13},{5,9},{9,5},{13,1},{2,14},{6,10},... | collective-permute-start | bytes 319496 | tf_op jit(solution)/shard_map/ppermute | solution.py:398
  46.7 0.0 collective-permute-start.16
  46.7 0.0 copy-start.9
  46.8 8.8 %grads.7 = f32[2,2048,1536]{2,1,0:T(8,128)} custom-call(s32[1]{0:T(128)} %bitcast.1.own_ref.first_ref, s32[1]{0:T(128)} %bitcast.2.other_ref.first_ref, bf16[128,2176]{1,0:T(8,128)(2,1)S(1)} %pre.1.refs_5_.mine_ref.refs_0_, bf16[128,2176]{1,0:T(8,128)(2,1)S(1)} %collective-permute-done.13.pre_ref.refs_1_, bf16[32,1536]{1,0:T(8,128)(2,1)S(1)} %copy-done.2, ...), custom_call_target="tpu_custom_call" | custom-call | flops 16000000000 | bytes 1024 | tf_op jit(solution)/shard_map/grads/pallas_call | solution.py:342
  55.6 1.1 %place.1 = (bf16[128,1536]{1,0:T(8,128)(2,1)}, bf16[2,128]{1,0:T(2,128)(2,1)}) custom-call(s32[2,128]{1,0:T(2,128)S(1)} %bitcast.11, bf16[32,128]{1,0:T(8,128)(2,1)S(1)} %get-tuple-element.17.picker_ref, f32[32,1664]{1,0:T(8,128)S(1)} %get-tuple-element.23.refs_0_.refs_6_, bf16[32,1664]{1,0:T(8,128)(2,1)S(1)} %collective-permute-done.14.refs_1_, ...), custom_call_target="tpu_custom_call" | custom-call | flops 16000000000 | bytes 1024 | tf_op jit(solution)/shard_map/place/pallas_call | solution.py:383
  (30 shorter events, 0.1 us)
Async XLA Ops:
  0.6 11.8 %copy-start = (bf16[2,2048,1536]{2,1,0:T(8,128)(2,1)S(1)}, bf16[2,2048,1536]{2,1,0:T(8,128)(2,1)}, u32[]{:S(2)}) copy-start(bf16[2,2048,1536]{2,1,0:T(8,128)(2,1)} %w_ref.1) | copy-start | bytes 37748740
  2.4 12.2 %copy-start.1 = (bf16[32,1536]{1,0:T(8,128)(2,1)}, bf16[32,1536]{1,0:T(8,128)(2,1)S(1)}, u32[]{:S(2)}) copy-start(bf16[32,1536]{1,0:T(8,128)(2,1)S(1)} %get-tuple-element.18.refs_0_.refs_2_) | copy-start | bytes 294916
  2.4 10.1 %collective-permute-start = (bf16[32,1536]{1,0:T(8,128)(2,1)S(1)}, bf16[32,1536]{1,0:T(8,128)(2,1)S(1)}, u32[]{:S(2)}, u32[]{:S(2)}) collective-permute-start(bf16[32,1536]{1,0:T(8,128)(2,1)S(1)} %get-tuple-element.18.refs_0_.refs_2_), channel_id=1, source_target_pairs={{0,4},{4,0},{8,12},{12,8},{1,5},{5,1},{9,13},{13,9},{2,6},{6,2},{1... | collective-permute-start | bytes 294920 | tf_op jit(solution)/shard_map/ppermute | solution.py:398
  5.5 12.8 %collective-permute-start.3 = (bf16[32,1536]{1,0:T(8,128)(2,1)S(1)}, bf16[32,1536]{1,0:T(8,128)(2,1)S(1)}, u32[]{:S(2)}, u32[]{:S(2)}) collective-permute-start(bf16[32,1536]{1,0:T(8,128)(2,1)S(1)} %get-tuple-element.18.refs_0_.refs_2_), channel_id=1, source_target_pairs={{0,8},{4,12},{8,0},{12,4},{1,9},{5,13},{9,1},{13,5},{2,10},{6,14},... | collective-permute-start | bytes 294920 | tf_op jit(solution)/shard_map/ppermute | solution.py:398
  8.1 11.6 %collective-permute-start.4 = (bf16[32,1536]{1,0:T(8,128)(2,1)S(1)}, bf16[32,1536]{1,0:T(8,128)(2,1)S(1)}, u32[]{:S(2)}, u32[]{:S(2)}) collective-permute-start(bf16[32,1536]{1,0:T(8,128)(2,1)S(1)} %get-tuple-element.18.refs_0_.refs_2_), channel_id=1, source_target_pairs={{0,12},{4,8},{8,4},{12,0},{1,13},{5,9},{9,5},{13,1},{2,14},{6,10},... | collective-permute-start | bytes 294920 | tf_op jit(solution)/shard_map/ppermute | solution.py:398
  8.1 17.3 %collective-permute-start.7 = (bf16[32,1664]{1,0:T(8,128)(2,1)S(1)}, bf16[32,1664]{1,0:T(8,128)(2,1)S(1)}, u32[]{:S(2)}, u32[]{:S(2)}) collective-permute-start(bf16[32,1664]{1,0:T(8,128)(2,1)S(1)} %get-tuple-element.19.refs_3_.refs_0_.refs_1_.refs_6_), channel_id=1, source_target_pairs={{0,4},{4,0},{8,12},{12,8},{1,5},{5,1},{9,13},{13,9},{2,6},{6,2},{1... | collective-permute-start | bytes 319496 | tf_op jit(solution)/shard_map/ppermute | solution.py:398
  9.0 16.4 %collective-permute-start.8 = (bf16[32,1664]{1,0:T(8,128)(2,1)S(1)}, bf16[32,1664]{1,0:T(8,128)(2,1)S(1)}, u32[]{:S(2)}, u32[]{:S(2)}) collective-permute-start(bf16[32,1664]{1,0:T(8,128)(2,1)S(1)} %get-tuple-element.19.refs_3_.refs_0_.refs_1_.refs_6_), channel_id=1, source_target_pairs={{0,8},{4,12},{8,0},{12,4},{1,9},{5,13},{9,1},{13,5},{2,10},{6,14},... | collective-permute-start | bytes 319496 | tf_op jit(solution)/shard_map/ppermute | solution.py:398
  12.5 2.1 %copy-start.3 = (bf16[32,1536]{1,0:T(8,128)(2,1)}, bf16[32,1536]{1,0:T(8,128)(2,1)S(1)}, u32[]{:S(2)}) copy-start(bf16[32,1536]{1,0:T(8,128)(2,1)S(1)} %collective-permute-done.refs_1_.refs_3_) | copy-start | bytes 294916
  14.5 2.1 %collective-permute-start.1 = (bf16[64,2048]{1,0:T(8,128)(2,1)S(1)}, bf16[64,2048]{1,0:T(8,128)(2,1)S(1)}, u32[]{:S(2)}, u32[]{:S(2)}) collective-permute-start(bf16[64,2048]{1,0:T(8,128)(2,1)S(1)} %project.6.refs_3_), channel_id=1, source_target_pairs={{0,1},{1,0},{2,3},{3,2},{4,5},{5,4},{6,7},{7,6},{8,9},{9,8},{10,11... | collective-permute-start | bytes 786440 | tf_op jit(solution)/shard_map/ppermute | solution.py:398
  16.7 13.2 %collective-permute-start.2 = (bf16[64,2048]{1,0:T(8,128)(2,1)S(1)}, bf16[64,2048]{1,0:T(8,128)(2,1)S(1)}, u32[]{:S(2)}, u32[]{:S(2)}) collective-permute-start(bf16[64,2048]{1,0:T(8,128)(2,1)S(1)} %add.3.refs_1_.refs_0_), channel_id=1, source_target_pairs={{0,2},{1,3},{2,0},{3,1},{4,6},{5,7},{6,4},{7,5},{8,10},{9,11},{10,... | collective-permute-start | bytes 786440 | tf_op jit(solution)/shard_map/ppermute | solution.py:398
  18.2 3.5 %copy-start.5 = (bf16[32,1536]{1,0:T(8,128)(2,1)}, bf16[32,1536]{1,0:T(8,128)(2,1)S(1)}, u32[]{:S(2)}) copy-start(bf16[32,1536]{1,0:T(8,128)(2,1)S(1)} %collective-permute-done.3.refs_0_.refs_4_) | copy-start | bytes 294916
  18.2 7.2 %collective-permute-start.9 = (bf16[32,1664]{1,0:T(8,128)(2,1)S(1)}, bf16[32,1664]{1,0:T(8,128)(2,1)S(1)}, u32[]{:S(2)}, u32[]{:S(2)}) collective-permute-start(bf16[32,1664]{1,0:T(8,128)(2,1)S(1)} %relay.1.refs_3_), channel_id=1, source_target_pairs={{0,12},{4,8},{8,4},{12,0},{1,13},{5,9},{9,5},{13,1},{2,14},{6,10},... | collective-permute-start | bytes 319496 | tf_op jit(solution)/shard_map/ppermute | solution.py:398
  19.6 2.1 %copy-start.7 = (bf16[32,1536]{1,0:T(8,128)(2,1)}, bf16[32,1536]{1,0:T(8,128)(2,1)S(1)}, u32[]{:S(2)}) copy-start(bf16[32,1536]{1,0:T(8,128)(2,1)S(1)} %collective-permute-done.4.refs_1_.refs_5_) | copy-start | bytes 294916
  21.6 2.1 %collective-permute-start.5 = (bf16[64,2048]{1,0:T(8,128)(2,1)S(1)}, bf16[64,2048]{1,0:T(8,128)(2,1)S(1)}, u32[]{:S(2)}, u32[]{:S(2)}) collective-permute-start(bf16[64,2048]{1,0:T(8,128)(2,1)S(1)} %project.8.refs_3_), channel_id=1, source_target_pairs={{0,1},{1,0},{2,3},{3,2},{4,5},{5,4},{6,7},{7,6},{8,9},{9,8},{10,11... | collective-permute-start | bytes 786440 | tf_op jit(solution)/shard_map/ppermute | solution.py:398
  21.7 3.7 %slice-start = ((s8[6291456]{0:T(1024)(128)(4,1)}), s8[4194304]{0:T(1024)(128)(4,1)S(1)}, s32[]{:S(2)}) async-start(s8[6291456]{0:T(1024)(128)(4,1)} %bitcast.6), calls=%async_computation | async-start | bytes 8388608
  23.8 1.7 %slice-start.1 = ((s8[6291456]{0:T(1024)(128)(4,1)}), s8[2097152]{0:T(1024)(128)(4,1)S(1)}, s32[]{:S(2)}) async-start(s8[6291456]{0:T(1024)(128)(4,1)} %bitcast.6), calls=%async_computation.1 | async-start | bytes 4194304
  23.9 9.2 %collective-permute-start.6 = (bf16[64,2048]{1,0:T(8,128)(2,1)S(1)}, bf16[64,2048]{1,0:T(8,128)(2,1)S(1)}, u32[]{:S(2)}, u32[]{:S(2)}) collective-permute-start(bf16[64,2048]{1,0:T(8,128)(2,1)S(1)} %add.4.refs_5_.refs_2_), channel_id=1, source_target_pairs={{0,2},{1,3},{2,0},{3,1},{4,6},{5,7},{6,4},{7,5},{8,10},{9,11},{10,... | collective-permute-start | bytes 786440 | tf_op jit(solution)/shard_map/ppermute | solution.py:398
  26.6 1.6 %collective-permute-start.10 = (bf16[128,1024]{1,0:T(8,128)(2,1)S(1)}, bf16[128,1024]{1,0:T(8,128)(2,1)S(1)}, u32[]{:S(2)}, u32[]{:S(2)}) collective-permute-start(bf16[128,1024]{1,0:T(8,128)(2,1)S(1)} %project.10.refs_5_), channel_id=1, source_target_pairs={{0,1},{1,0},{2,3},{3,2},{4,5},{5,4},{6,7},{7,6},{8,9},{9,8},{10,11... | collective-permute-start | bytes 786440 | tf_op jit(solution)/shard_map/ppermute | solution.py:398
  28.3 10.3 %collective-permute-start.12 = (bf16[128,1024]{1,0:T(8,128)(2,1)S(1)}, bf16[128,1024]{1,0:T(8,128)(2,1)S(1)}, u32[]{:S(2)}, u32[]{:S(2)}) collective-permute-start(bf16[128,1024]{1,0:T(8,128)(2,1)S(1)} %add.5.refs_4_), channel_id=1, source_target_pairs={{0,2},{1,3},{2,0},{3,1},{4,6},{5,7},{6,4},{7,5},{8,10},{9,11},{10,... | collective-permute-start | bytes 786440 | tf_op jit(solution)/shard_map/ppermute | solution.py:398
  33.2 3.3 %collective-permute-start.11 = (bf16[128,1024]{1,0:T(8,128)(2,1)S(1)}, bf16[128,1024]{1,0:T(8,128)(2,1)S(1)}, u32[]{:S(2)}, u32[]{:S(2)}) collective-permute-start(bf16[128,1024]{1,0:T(8,128)(2,1)S(1)} %hidden.1.refs_0_), channel_id=1, source_target_pairs={{0,1},{1,0},{2,3},{3,2},{4,5},{5,4},{6,7},{7,6},{8,9},{9,8},{10,11... | collective-permute-start | bytes 786440 | tf_op jit(solution)/shard_map/ppermute | solution.py:398
  39.2 2.7 %collective-permute-start.13 = (bf16[128,2176]{1,0:T(8,128)(2,1)S(1)}, bf16[128,2176]{1,0:T(8,128)(2,1)S(1)}, u32[]{:S(2)}, u32[]{:S(2)}) collective-permute-start(bf16[128,2176]{1,0:T(8,128)(2,1)S(1)} %pre.1.refs_5_.mine_ref.refs_0_), channel_id=1, source_target_pairs={{0,1},{1,0},{2,3},{3,2},{4,5},{5,4},{6,7},{7,6},{8,9},{9,8},{10,11... | collective-permute-start | bytes 1671176 | tf_op jit(solution)/shard_map/ppermute | solution.py:398
  41.9 4.8 %copy-start.2 = (bf16[32,1536]{1,0:T(8,128)(2,1)S(1)}, bf16[32,1536]{1,0:T(8,128)(2,1)}, u32[]{:S(2)}) copy-start(bf16[32,1536]{1,0:T(8,128)(2,1)} %copy-done.1) | copy-start | bytes 294916
  42.0 4.8 %copy-start.4 = (bf16[32,1536]{1,0:T(8,128)(2,1)S(1)}, bf16[32,1536]{1,0:T(8,128)(2,1)}, u32[]{:S(2)}) copy-start(bf16[32,1536]{1,0:T(8,128)(2,1)} %copy-done.3) | copy-start | bytes 294916
  42.0 4.8 %copy-start.6 = (bf16[32,1536]{1,0:T(8,128)(2,1)S(1)}, bf16[32,1536]{1,0:T(8,128)(2,1)}, u32[]{:S(2)}) copy-start(bf16[32,1536]{1,0:T(8,128)(2,1)} %copy-done.5) | copy-start | bytes 294916
  42.0 4.8 %copy-start.8 = (bf16[32,1536]{1,0:T(8,128)(2,1)S(1)}, bf16[32,1536]{1,0:T(8,128)(2,1)}, u32[]{:S(2)}) copy-start(bf16[32,1536]{1,0:T(8,128)(2,1)} %copy-done.7) | copy-start | bytes 294916
  43.0 12.6 %collective-permute-start.14 = (bf16[32,1664]{1,0:T(8,128)(2,1)S(1)}, bf16[32,1664]{1,0:T(8,128)(2,1)S(1)}, u32[]{:S(2)}, u32[]{:S(2)}) collective-permute-start(bf16[32,1664]{1,0:T(8,128)(2,1)S(1)} %get-tuple-element.24), channel_id=1, source_target_pairs={{0,8},{4,12},{8,0},{12,4},{1,9},{5,13},{9,1},{13,5},{2,10},{6,14},... | collective-permute-start | bytes 319496 | tf_op jit(solution)/shard_map/ppermute | solution.py:398
  46.1 9.5 %collective-permute-start.15 = (bf16[32,1664]{1,0:T(8,128)(2,1)S(1)}, bf16[32,1664]{1,0:T(8,128)(2,1)S(1)}, u32[]{:S(2)}, u32[]{:S(2)}) collective-permute-start(bf16[32,1664]{1,0:T(8,128)(2,1)S(1)} %get-tuple-element.25), channel_id=1, source_target_pairs={{0,12},{4,8},{8,4},{12,0},{1,13},{5,9},{9,5},{13,1},{2,14},{6,10},... | collective-permute-start | bytes 319496 | tf_op jit(solution)/shard_map/ppermute | solution.py:398
  46.7 8.9 %collective-permute-start.16 = (bf16[32,1664]{1,0:T(8,128)(2,1)S(1)}, bf16[32,1664]{1,0:T(8,128)(2,1)S(1)}, u32[]{:S(2)}, u32[]{:S(2)}) collective-permute-start(bf16[32,1664]{1,0:T(8,128)(2,1)S(1)} %get-tuple-element.26), channel_id=1, source_target_pairs={{0,4},{4,0},{8,12},{12,8},{1,5},{5,1},{9,13},{13,9},{2,6},{6,2},{1... | collective-permute-start | bytes 319496 | tf_op jit(solution)/shard_map/ppermute | solution.py:398
  46.7 8.9 %copy-start.9 = (s32[128,2]{0,1:T(2,128)S(1)}, s32[128,2]{0,1:T(2,128)}, u32[]{:S(2)}) copy-start(s32[128,2]{0,1:T(2,128)} %param.8) | copy-start | bytes 3076

commit v5 on v4

--- a/solution.py
+++ b/solution.py
@@ -433,7 +433,7 @@
     send_in, send_grad, picker = select(firsts, tokens, cotangent, expert_ids, quantized)
     if direct:
         tok_blocks = [send_in] + [swap(send_in, "dp", dp, d) for d in range(1, dp)]
-        cot_blocks = [send_grad] + [swap(send_grad, "dp", dp, d) for d in (1, 2)]
+        cot_blocks = [send_grad, swap(send_grad, "dp", dp, 2)]
         groups = [tok_blocks[:2], tok_blocks[2:]]
     else:
         tok_blocks = [lax.all_gather(send_in, "dp", axis=0, tiled=True)]
@@ -454,6 +454,7 @@
 
     def pass_on(after):
         block = relay([send_grad], after)
+        cot_blocks.insert(1, swap(block, "dp", dp, 1))
         cot_blocks.append(swap(block, "dp", dp, 3))
         return block
 

time: 57 us -> 56.9 us (level)
  starting transfers between devices: 21.1 us -> 19 us
  waiting for transfers between devices: 3.18 us -> 4.78 us
  local copies, waits for them, and re-layouts: 0.06 us -> 0.68 us
    ppermute x17, starting transfers between devices: 21.1 us -> 19 us  [swap(): return lax.ppermute(array, axis, [(i, i ^ distance) for i in range(size)])]
    ppermute x17, waiting for transfers between devices: 3.18 us -> 4.78 us  [swap(): return lax.ppermute(array, axis, [(i, i ^ distance) for i in range(size)])]
    unnamed x24, local copies, waits for them, and re-layouts: 0.06 us -> 0.68 us
  transfers between devices with their start and end apart: 17 -> 17, of which waited for: 1 -> 4; matrix products, arithmetic and copies ran while one was open for 0% -> 0% of each run, Pallas kernels for 48% -> 47%
where the time goes in v5:
time: 56.9 us; the launch traced here: 56.8 us
  Pallas kernels  31.3 us (55%)
  starting transfers between devices  19 us (33%)
  waiting for transfers between devices  4.78 us (8%)
  between operations  0.96 us (2%)
  local copies, waits for them, and re-layouts  0.68 us (1%)
    ppermute x17, starting transfers between devices, swap(): return lax.ppermute(array, axis, [(i, i ^ distance) for i in range(size)])  19 us
    pallas_call x4, Pallas kernels, grads(): pl.pallas_call(functools.partial(grads_kernel, places, *sizes), in_specs=...  16.3 us
    pallas_call x6, Pallas kernels, project(): pl.pallas_call(functools.partial(project_kernel, len(blocks), width, unit...  10.3 us
    ppermute x17, waiting for transfers between devices, swap(): return lax.ppermute(array, axis, [(i, i ^ distance) for i in range(size)])  4.78 us
    pallas_call x1, Pallas kernels, select(): pl.pallas_call(select_kernel, in_specs=[SMEM] * 2 + [HBM] * 4, out_specs=...  1.73 us
  transfers between devices with their start and end apart: 17, of which 4 were waited for; matrix products, arithmetic and copies ran while one was open for 0% of the time, Pallas kernels for 47%

profile of v5, /device:TPU:0, one launch (start us, length us, event | category | flops | bytes accessed | tf_op | source)
XLA Modules:
  0.0 56.8 jit_solution(16798470190286140709)
XLA Ops:
  0.6 1.7 %select.3 = (bf16[32,1536]{1,0:T(8,128)(2,1)S(1)}, bf16[32,1664]{1,0:T(8,128)(2,1)S(1)}, bf16[32,128]{1,0:T(8,128)(2,1)S(1)}) custom-call(s32[1]{0:T(128)} %bitcast.1.own_ref.first_ref, s32[1]{0:T(128)} %bitcast.2.other_ref.first_ref, bf16[128,1536]{1,0:T(8,128)(2,1)} %refs_0_.1, bf16[128,1536]{1,0:T(8,128)(2,1)} %refs_1_.1, s32[2,128]{1,0:T(2,128)} %bitcast.10, ...), custom_call_target="tpu_custom_call" | custom-call | flops 17999998976 | bytes 1024 | tf_op jit(solution)/shard_map/select/pallas_call | solution.py:81
  2.4 0.0 copy-start.1
  2.4 3.1 %collective-permute-start = (bf16[32,1536]{1,0:T(8,128)(2,1)S(1)}, bf16[32,1536]{1,0:T(8,128)(2,1)S(1)}, u32[]{:S(2)}, u32[]{:S(2)}) collective-permute-start(bf16[32,1536]{1,0:T(8,128)(2,1)S(1)} %get-tuple-element.18.refs_0_.refs_2_), channel_id=1, source_target_pairs={{0,4},{4,0},{8,12},{12,8},{1,5},{5,1},{9,13},{13,9},{2,6},{6,2},{1... | collective-permute-start | bytes 294920 | tf_op jit(solution)/shard_map/ppermute | solution.py:398
  5.5 2.6 %collective-permute-start.3 = (bf16[32,1536]{1,0:T(8,128)(2,1)S(1)}, bf16[32,1536]{1,0:T(8,128)(2,1)S(1)}, u32[]{:S(2)}, u32[]{:S(2)}) collective-permute-start(bf16[32,1536]{1,0:T(8,128)(2,1)S(1)} %get-tuple-element.18.refs_0_.refs_2_), channel_id=1, source_target_pairs={{0,8},{4,12},{8,0},{12,4},{1,9},{5,13},{9,1},{13,5},{2,10},{6,14},... | collective-permute-start | bytes 294920 | tf_op jit(solution)/shard_map/ppermute | solution.py:398
  8.1 0.0 collective-permute-start.4
  8.1 1.9 %collective-permute-start.8 = (bf16[32,1664]{1,0:T(8,128)(2,1)S(1)}, bf16[32,1664]{1,0:T(8,128)(2,1)S(1)}, u32[]{:S(2)}, u32[]{:S(2)}) collective-permute-start(bf16[32,1664]{1,0:T(8,128)(2,1)S(1)} %get-tuple-element.19.refs_3_.refs_0_.refs_1_.refs_6_), channel_id=1, source_target_pairs={{0,8},{4,12},{8,0},{12,4},{1,9},{5,13},{9,1},{13,5},{2,10},{6,14},... | collective-permute-start | bytes 319496 | tf_op jit(solution)/shard_map/ppermute | solution.py:398
  10.0 2.0 %project.6.refs_3_ = bf16[64,2048]{1,0:T(8,128)(2,1)S(1)} custom-call(s32[1]{0:T(128)} %bitcast.2.other_ref.first_ref, bf16[32,1536]{1,0:T(8,128)(2,1)S(1)} %get-tuple-element.18.refs_0_.refs_2_, bf16[32,1536]{1,0:T(8,128)(2,1)S(1)} %collective-permute-done.refs_1_.refs_3_, bf16[2,2048,1536]{2,1,0:T(8,128)(2,1)S(1)} %copy-done, ...), custom_call_target="tpu_custom_call" | custom-call | flops 16000000000 | bytes 1024 | tf_op jit(solution)/shard_map/project/pallas_call | solution.py:118
  12.0 0.1 collective-permute-start.1
  12.1 2.0 %project.7.mine_ref = f32[64,2048]{1,0:T(8,128)S(1)} custom-call(s32[1]{0:T(128)} %bitcast.1.own_ref.first_ref, bf16[32,1536]{1,0:T(8,128)(2,1)S(1)} %get-tuple-element.18.refs_0_.refs_2_, bf16[32,1536]{1,0:T(8,128)(2,1)S(1)} %collective-permute-done.refs_1_.refs_3_, bf16[2,2048,1536]{2,1,0:T(8,128)(2,1)S(1)} %copy-done, bf16[64,2048]{1,0:T(8,128)(2,1)S(1)} %project.6.refs_3_), custom_call_target="tpu_custom_call" | custom-call | flops 16000000000 | bytes 1024 | tf_op jit(solution)/shard_map/project/pallas_call | solution.py:118
  14.1 0.0 collective-permute-done.1.arrived_ref
  14.1 0.1 add.3.refs_1_.refs_0_
  14.2 2.5 %collective-permute-start.7 = (bf16[32,1664]{1,0:T(8,128)(2,1)S(1)}, bf16[32,1664]{1,0:T(8,128)(2,1)S(1)}, u32[]{:S(2)}, u32[]{:S(2)}) collective-permute-start(bf16[32,1664]{1,0:T(8,128)(2,1)S(1)} %relay.1.refs_3_), channel_id=1, source_target_pairs={{0,4},{4,0},{8,12},{12,8},{1,5},{5,1},{9,13},{13,9},{2,6},{6,2},{1... | collective-permute-start | bytes 319496 | tf_op jit(solution)/shard_map/ppermute | solution.py:398
  16.7 1.1 %collective-permute-start.9 = (bf16[32,1664]{1,0:T(8,128)(2,1)S(1)}, bf16[32,1664]{1,0:T(8,128)(2,1)S(1)}, u32[]{:S(2)}, u32[]{:S(2)}) collective-permute-start(bf16[32,1664]{1,0:T(8,128)(2,1)S(1)} %relay.1.refs_3_), channel_id=1, source_target_pairs={{0,12},{4,8},{8,4},{12,0},{1,13},{5,9},{9,5},{13,1},{2,14},{6,10},... | collective-permute-start | bytes 319496 | tf_op jit(solution)/shard_map/ppermute | solution.py:398
  17.8 0.6 collective-permute-done.3.refs_0_.refs_4_
  18.4 1.5 %collective-permute-start.2 = (bf16[64,2048]{1,0:T(8,128)(2,1)S(1)}, bf16[64,2048]{1,0:T(8,128)(2,1)S(1)}, u32[]{:S(2)}, u32[]{:S(2)}) collective-permute-start(bf16[64,2048]{1,0:T(8,128)(2,1)S(1)} %add.3.refs_1_.refs_0_), channel_id=1, source_target_pairs={{0,2},{1,3},{2,0},{3,1},{4,6},{5,7},{6,4},{7,5},{8,10},{9,11},{10,... | collective-permute-start | bytes 786440 | tf_op jit(solution)/shard_map/ppermute | solution.py:398
  19.9 2.0 %project.8.refs_3_ = bf16[64,2048]{1,0:T(8,128)(2,1)S(1)} custom-call(s32[1]{0:T(128)} %bitcast.2.other_ref.first_ref, bf16[32,1536]{1,0:T(8,128)(2,1)S(1)} %collective-permute-done.3.refs_0_.refs_4_, bf16[32,1536]{1,0:T(8,128)(2,1)S(1)} %collective-permute-done.4.refs_1_.refs_5_, bf16[2,2048,1536]{2,1,0:T(8,128)(2,1)S(1)} %copy-done, ...), custom_call_target="tpu_custom_call" | custom-call | flops 16000000000 | bytes 1024 | tf_op jit(solution)/shard_map/project/pallas_call | solution.py:118
  21.9 0.1 collective-permute-start.5
  22.0 0.0 slice-start
  22.0 2.0 %project.9.mine_ref = f32[64,2048]{1,0:T(8,128)S(1)} custom-call(s32[1]{0:T(128)} %bitcast.1.own_ref.first_ref, bf16[32,1536]{1,0:T(8,128)(2,1)S(1)} %collective-permute-done.3.refs_0_.refs_4_, bf16[32,1536]{1,0:T(8,128)(2,1)S(1)} %collective-permute-done.4.refs_1_.refs_5_, bf16[2,2048,1536]{2,1,0:T(8,128)(2,1)S(1)} %copy-done, ...), custom_call_target="tpu_custom_call" | custom-call | flops 16000000000 | bytes 1024 | tf_op jit(solution)/shard_map/project/pallas_call | solution.py:118
  24.0 0.0 slice-start.1
  24.0 0.1 add.4.refs_5_.refs_2_
  24.1 0.6 %collective-permute-start.6 = (bf16[64,2048]{1,0:T(8,128)(2,1)S(1)}, bf16[64,2048]{1,0:T(8,128)(2,1)S(1)}, u32[]{:S(2)}, u32[]{:S(2)}) collective-permute-start(bf16[64,2048]{1,0:T(8,128)(2,1)S(1)} %add.4.refs_5_.refs_2_), channel_id=1, source_target_pairs={{0,2},{1,3},{2,0},{3,1},{4,6},{5,7},{6,4},{7,5},{8,10},{9,11},{10,... | collective-permute-start | bytes 786440 | tf_op jit(solution)/shard_map/ppermute | solution.py:398
  24.7 0.2 collective-permute-done.8.refs_2_.refs_3_.refs_8_
  24.9 0.1 collective-permute-done.7.refs_1_.refs_2_.refs_7_
  25.0 0.6 %slice-done.1 = s8[2097152]{0:T(1024)(128)(4,1)S(1)} async-done(((s8[6291456]{0:T(1024)(128)(4,1)}), s8[2097152]{0:T(1024)(128)(4,1)S(1)}, s32[]{:S(2)}) %slice-start.1) | async-done | bytes 2097176
  25.7 1.1 %project.10.refs_5_ = bf16[128,1024]{1,0:T(8,128)(2,1)S(1)} custom-call(s32[1]{0:T(128)} %bitcast.2.other_ref.first_ref, bf16[32,1664]{1,0:T(8,128)(2,1)S(1)} %get-tuple-element.19.refs_3_.refs_0_.refs_1_.refs_6_, bf16[32,1664]{1,0:T(8,128)(2,1)S(1)} %collective-permute-done.7.refs_1_.refs_2_.refs_7_, ...), custom_call_target="tpu_custom_call" | custom-call | flops 16000000000 | bytes 1024 | tf_op jit(solution)/shard_map/project/pallas_call | solution.py:118
  26.8 0.5 collective-permute-start.10
  27.3 1.1 %project.11.mine_ref = f32[128,1024]{1,0:T(8,128)S(1)} custom-call(s32[1]{0:T(128)} %bitcast.1.own_ref.first_ref, bf16[32,1664]{1,0:T(8,128)(2,1)S(1)} %get-tuple-element.19.refs_3_.refs_0_.refs_1_.refs_6_, bf16[32,1664]{1,0:T(8,128)(2,1)S(1)} %collective-permute-done.7.refs_1_.refs_2_.refs_7_, ...), custom_call_target="tpu_custom_call" | custom-call | flops 16000000000 | bytes 1024 | tf_op jit(solution)/shard_map/project/pallas_call | solution.py:118
  28.5 0.0 collective-permute-done.10.arrived_ref
  28.5 0.1 add.5.refs_4_
  28.6 0.9 %collective-permute-start.12 = (bf16[128,1024]{1,0:T(8,128)(2,1)S(1)}, bf16[128,1024]{1,0:T(8,128)(2,1)S(1)}, u32[]{:S(2)}, u32[]{:S(2)}) collective-permute-start(bf16[128,1024]{1,0:T(8,128)(2,1)S(1)} %add.5.refs_4_), channel_id=1, source_target_pairs={{0,2},{1,3},{2,0},{3,1},{4,6},{5,7},{6,4},{7,5},{8,10},{9,11},{10,... | collective-permute-start | bytes 786440 | tf_op jit(solution)/shard_map/ppermute | solution.py:398
  29.4 3.8 %collective-permute-done.6.refs_3_ = bf16[64,2048]{1,0:T(8,128)(2,1)S(1)} collective-permute-done((bf16[64,2048]{1,0:T(8,128)(2,1)S(1)}, bf16[64,2048]{1,0:T(8,128)(2,1)S(1)}, u32[]{:S(2)}, u32[]{:S(2)}) %collective-permute-start.6) | collective-permute-done | bytes 262176 | tf_op jit(solution)/shard_map/ppermute | solution.py:398
  33.3 0.2 hidden.1.refs_0_
  33.5 0.1 collective-permute-start.11
  33.5 3.2 %grads.4.refs_5_ = f32[2048,1536]{1,0:T(8,128)} custom-call(s32[1]{0:T(128)} %bitcast.1.own_ref.first_ref, s32[1]{0:T(128)} %bitcast.2.other_ref.first_ref, bf16[128,1024]{1,0:T(8,128)(2,1)S(1)} %hidden.1.refs_0_, bf16[32,1664]{1,0:T(8,128)(2,1)S(1)} %get-tuple-element.19.refs_3_.refs_0_.refs_1_.refs_6_, ...), custom_call_target="tpu_custom_call" | custom-call | flops 16000000000 | bytes 1024 | tf_op jit(solution)/shard_map/grads/pallas_call | solution.py:342
  36.7 2.1 %grads.5 = (f32[2048,1536]{1,0:T(8,128)}, f32[8,128]{1,0:T(8,128)S(1)}) custom-call(s32[1]{0:T(128)} %bitcast.1.own_ref.first_ref, s32[1]{0:T(128)} %bitcast.2.other_ref.first_ref, bf16[128,1024]{1,0:T(8,128)(2,1)S(1)} %collective-permute-done.11.refs_0_, ...), custom_call_target="tpu_custom_call", output_to_operand_aliasing={{0}: (7, {})} | custom-call | flops 16000000000 | bytes 1024 | tf_op jit(solution)/shard_map/grads/pallas_call | solution.py:342
  38.9 0.6 %pre.1.refs_5_.mine_ref.refs_0_ = bf16[128,2176]{1,0:T(8,128)(2,1)S(1)} custom-call(bf16[64,2048]{1,0:T(8,128)(2,1)S(1)} %add.3.refs_1_.refs_0_, bf16[64,2048]{1,0:T(8,128)(2,1)S(1)} %collective-permute-done.2.refs_1_, bf16[64,2048]{1,0:T(8,128)(2,1)S(1)} %add.4.refs_5_.refs_2_, bf16[64,2048]{1,0:T(8,128)(2,1)S(1)} %collective-permute-done.6.refs_3_, ...), custom_call_target="tpu_custom_call" | custom-call | flops 16000000000 | bytes 1024 | tf_op jit(solution)/shard_map/pre/pallas_call | solution.py:216
  39.5 0.6 collective-permute-start.13
  40.0 2.1 %grads.6 = (f32[2048,1536]{1,0:T(8,128)}, f32[128,1536]{1,0:T(8,128)S(1)}) custom-call(s32[1]{0:T(128)} %bitcast.1.own_ref.first_ref, s32[1]{0:T(128)} %bitcast.2.other_ref.first_ref, bf16[128,1024]{1,0:T(8,128)(2,1)S(1)} %collective-permute-done.11.refs_0_, ...), custom_call_target="tpu_custom_call", output_to_operand_aliasing={{0}: (9, {})} | custom-call | flops 16000000000 | bytes 1024 | tf_op jit(solution)/shard_map/grads/pallas_call | solution.py:342
  42.2 0.0 copy-start.2
  42.2 0.0 copy-start.4
  42.2 1.0 %row_rest.1 = (f32[32,1664]{1,0:T(8,128)S(1)}, bf16[32,1664]{1,0:T(8,128)(2,1)S(1)}, bf16[32,1664]{1,0:T(8,128)(2,1)S(1)}, bf16[32,1664]{1,0:T(8,128)(2,1)S(1)}) custom-call(s32[1]{0:T(128)} %bitcast.2.other_ref.first_ref, f32[128,1536]{1,0:T(8,128)S(1)} %get-tuple-element.22.own_ref, bf16[128,2176]{1,0:T(8,128)(2,1)S(1)} %pre.1.refs_5_.mine_ref.refs_0_, ...), custom_call_target="tpu_custom_call" | custom-call | flops 16000000000 | bytes 1024 | tf_op jit(solution)/shard_map/row_rest/pallas_call | solution.py:267
  43.2 2.2 %collective-permute-start.14 = (bf16[32,1664]{1,0:T(8,128)(2,1)S(1)}, bf16[32,1664]{1,0:T(8,128)(2,1)S(1)}, u32[]{:S(2)}, u32[]{:S(2)}) collective-permute-start(bf16[32,1664]{1,0:T(8,128)(2,1)S(1)} %get-tuple-element.24), channel_id=1, source_target_pairs={{0,8},{4,12},{8,0},{12,4},{1,9},{5,13},{9,1},{13,5},{2,10},{6,14},... | collective-permute-start | bytes 319496 | tf_op jit(solution)/shard_map/ppermute | solution.py:398
  45.4 1.3 %collective-permute-start.15 = (bf16[32,1664]{1,0:T(8,128)(2,1)S(1)}, bf16[32,1664]{1,0:T(8,128)(2,1)S(1)}, u32[]{:S(2)}, u32[]{:S(2)}) collective-permute-start(bf16[32,1664]{1,0:T(8,128)(2,1)S(1)} %get-tuple-element.25), channel_id=1, source_target_pairs={{0,12},{4,8},{8,4},{12,0},{1,13},{5,9},{9,5},{13,1},{2,14},{6,10},... | collective-permute-start | bytes 319496 | tf_op jit(solution)/shard_map/ppermute | solution.py:398
  46.7 0.1 collective-permute-start.16
  46.8 0.0 copy-start.9
  46.8 8.8 %grads.7 = f32[2,2048,1536]{2,1,0:T(8,128)} custom-call(s32[1]{0:T(128)} %bitcast.1.own_ref.first_ref, s32[1]{0:T(128)} %bitcast.2.other_ref.first_ref, bf16[128,2176]{1,0:T(8,128)(2,1)S(1)} %pre.1.refs_5_.mine_ref.refs_0_, bf16[128,2176]{1,0:T(8,128)(2,1)S(1)} %collective-permute-done.13.pre_ref.refs_1_, bf16[32,1536]{1,0:T(8,128)(2,1)S(1)} %copy-done.2, ...), custom_call_target="tpu_custom_call" | custom-call | flops 16000000000 | bytes 1024 | tf_op jit(solution)/shard_map/grads/pallas_call | solution.py:342
  55.7 1.1 %place.1 = (bf16[128,1536]{1,0:T(8,128)(2,1)}, bf16[2,128]{1,0:T(2,128)(2,1)}) custom-call(s32[2,128]{1,0:T(2,128)S(1)} %bitcast.11, bf16[32,128]{1,0:T(8,128)(2,1)S(1)} %get-tuple-element.17.picker_ref, f32[32,1664]{1,0:T(8,128)S(1)} %get-tuple-element.23.refs_0_.refs_6_, bf16[32,1664]{1,0:T(8,128)(2,1)S(1)} %collective-permute-done.14.refs_1_, ...), custom_call_target="tpu_custom_call" | custom-call | flops 16000000000 | bytes 1024 | tf_op jit(solution)/shard_map/place/pallas_call | solution.py:383
  (30 shorter events, 0.1 us)
Async XLA Ops:
  0.6 9.4 %copy-start = (bf16[2,2048,1536]{2,1,0:T(8,128)(2,1)S(1)}, bf16[2,2048,1536]{2,1,0:T(8,128)(2,1)}, u32[]{:S(2)}) copy-start(bf16[2,2048,1536]{2,1,0:T(8,128)(2,1)} %w_ref.1) | copy-start | bytes 37748740
  2.4 9.7 %copy-start.1 = (bf16[32,1536]{1,0:T(8,128)(2,1)}, bf16[32,1536]{1,0:T(8,128)(2,1)S(1)}, u32[]{:S(2)}) copy-start(bf16[32,1536]{1,0:T(8,128)(2,1)S(1)} %get-tuple-element.18.refs_0_.refs_2_) | copy-start | bytes 294916
  2.4 7.6 %collective-permute-start = (bf16[32,1536]{1,0:T(8,128)(2,1)S(1)}, bf16[32,1536]{1,0:T(8,128)(2,1)S(1)}, u32[]{:S(2)}, u32[]{:S(2)}) collective-permute-start(bf16[32,1536]{1,0:T(8,128)(2,1)S(1)} %get-tuple-element.18.refs_0_.refs_2_), channel_id=1, source_target_pairs={{0,4},{4,0},{8,12},{12,8},{1,5},{5,1},{9,13},{13,9},{2,6},{6,2},{1... | collective-permute-start | bytes 294920 | tf_op jit(solution)/shard_map/ppermute | solution.py:398
  5.5 12.9 %collective-permute-start.3 = (bf16[32,1536]{1,0:T(8,128)(2,1)S(1)}, bf16[32,1536]{1,0:T(8,128)(2,1)S(1)}, u32[]{:S(2)}, u32[]{:S(2)}) collective-permute-start(bf16[32,1536]{1,0:T(8,128)(2,1)S(1)} %get-tuple-element.18.refs_0_.refs_2_), channel_id=1, source_target_pairs={{0,8},{4,12},{8,0},{12,4},{1,9},{5,13},{9,1},{13,5},{2,10},{6,14},... | collective-permute-start | bytes 294920 | tf_op jit(solution)/shard_map/ppermute | solution.py:398
  8.1 11.8 %collective-permute-start.4 = (bf16[32,1536]{1,0:T(8,128)(2,1)S(1)}, bf16[32,1536]{1,0:T(8,128)(2,1)S(1)}, u32[]{:S(2)}, u32[]{:S(2)}) collective-permute-start(bf16[32,1536]{1,0:T(8,128)(2,1)S(1)} %get-tuple-element.18.refs_0_.refs_2_), channel_id=1, source_target_pairs={{0,12},{4,8},{8,4},{12,0},{1,13},{5,9},{9,5},{13,1},{2,14},{6,10},... | collective-permute-start | bytes 294920 | tf_op jit(solution)/shard_map/ppermute | solution.py:398
  8.1 16.9 %collective-permute-start.8 = (bf16[32,1664]{1,0:T(8,128)(2,1)S(1)}, bf16[32,1664]{1,0:T(8,128)(2,1)S(1)}, u32[]{:S(2)}, u32[]{:S(2)}) collective-permute-start(bf16[32,1664]{1,0:T(8,128)(2,1)S(1)} %get-tuple-element.19.refs_3_.refs_0_.refs_1_.refs_6_), channel_id=1, source_target_pairs={{0,8},{4,12},{8,0},{12,4},{1,9},{5,13},{9,1},{13,5},{2,10},{6,14},... | collective-permute-start | bytes 319496 | tf_op jit(solution)/shard_map/ppermute | solution.py:398
  10.0 2.1 %copy-start.3 = (bf16[32,1536]{1,0:T(8,128)(2,1)}, bf16[32,1536]{1,0:T(8,128)(2,1)S(1)}, u32[]{:S(2)}) copy-start(bf16[32,1536]{1,0:T(8,128)(2,1)S(1)} %collective-permute-done.refs_1_.refs_3_) | copy-start | bytes 294916
  12.0 2.1 %collective-permute-start.1 = (bf16[64,2048]{1,0:T(8,128)(2,1)S(1)}, bf16[64,2048]{1,0:T(8,128)(2,1)S(1)}, u32[]{:S(2)}, u32[]{:S(2)}) collective-permute-start(bf16[64,2048]{1,0:T(8,128)(2,1)S(1)} %project.6.refs_3_), channel_id=1, source_target_pairs={{0,1},{1,0},{2,3},{3,2},{4,5},{5,4},{6,7},{7,6},{8,9},{9,8},{10,11... | collective-permute-start | bytes 786440 | tf_op jit(solution)/shard_map/ppermute | solution.py:398
  14.2 10.8 %collective-permute-start.7 = (bf16[32,1664]{1,0:T(8,128)(2,1)S(1)}, bf16[32,1664]{1,0:T(8,128)(2,1)S(1)}, u32[]{:S(2)}, u32[]{:S(2)}) collective-permute-start(bf16[32,1664]{1,0:T(8,128)(2,1)S(1)} %relay.1.refs_3_), channel_id=1, source_target_pairs={{0,4},{4,0},{8,12},{12,8},{1,5},{5,1},{9,13},{13,9},{2,6},{6,2},{1... | collective-permute-start | bytes 319496 | tf_op jit(solution)/shard_map/ppermute | solution.py:398
  16.7 8.3 %collective-permute-start.9 = (bf16[32,1664]{1,0:T(8,128)(2,1)S(1)}, bf16[32,1664]{1,0:T(8,128)(2,1)S(1)}, u32[]{:S(2)}, u32[]{:S(2)}) collective-permute-start(bf16[32,1664]{1,0:T(8,128)(2,1)S(1)} %relay.1.refs_3_), channel_id=1, source_target_pairs={{0,12},{4,8},{8,4},{12,0},{1,13},{5,9},{9,5},{13,1},{2,14},{6,10},... | collective-permute-start | bytes 319496 | tf_op jit(solution)/shard_map/ppermute | solution.py:398
  18.4 3.6 %copy-start.5 = (bf16[32,1536]{1,0:T(8,128)(2,1)}, bf16[32,1536]{1,0:T(8,128)(2,1)S(1)}, u32[]{:S(2)}) copy-start(bf16[32,1536]{1,0:T(8,128)(2,1)S(1)} %collective-permute-done.3.refs_0_.refs_4_) | copy-start | bytes 294916
  18.4 11.0 %collective-permute-start.2 = (bf16[64,2048]{1,0:T(8,128)(2,1)S(1)}, bf16[64,2048]{1,0:T(8,128)(2,1)S(1)}, u32[]{:S(2)}, u32[]{:S(2)}) collective-permute-start(bf16[64,2048]{1,0:T(8,128)(2,1)S(1)} %add.3.refs_1_.refs_0_), channel_id=1, source_target_pairs={{0,2},{1,3},{2,0},{3,1},{4,6},{5,7},{6,4},{7,5},{8,10},{9,11},{10,... | collective-permute-start | bytes 786440 | tf_op jit(solution)/shard_map/ppermute | solution.py:398
  19.9 2.1 %copy-start.7 = (bf16[32,1536]{1,0:T(8,128)(2,1)}, bf16[32,1536]{1,0:T(8,128)(2,1)S(1)}, u32[]{:S(2)}) copy-start(bf16[32,1536]{1,0:T(8,128)(2,1)S(1)} %collective-permute-done.4.refs_1_.refs_5_) | copy-start | bytes 294916
  21.9 2.1 %collective-permute-start.5 = (bf16[64,2048]{1,0:T(8,128)(2,1)S(1)}, bf16[64,2048]{1,0:T(8,128)(2,1)S(1)}, u32[]{:S(2)}, u32[]{:S(2)}) collective-permute-start(bf16[64,2048]{1,0:T(8,128)(2,1)S(1)} %project.8.refs_3_), channel_id=1, source_target_pairs={{0,1},{1,0},{2,3},{3,2},{4,5},{5,4},{6,7},{7,6},{8,9},{9,8},{10,11... | collective-permute-start | bytes 786440 | tf_op jit(solution)/shard_map/ppermute | solution.py:398
  22.0 3.0 %slice-start = ((s8[6291456]{0:T(1024)(128)(4,1)}), s8[4194304]{0:T(1024)(128)(4,1)S(1)}, s32[]{:S(2)}) async-start(s8[6291456]{0:T(1024)(128)(4,1)} %bitcast.6), calls=%async_computation | async-start | bytes 8388608
  24.0 1.6 %slice-start.1 = ((s8[6291456]{0:T(1024)(128)(4,1)}), s8[2097152]{0:T(1024)(128)(4,1)S(1)}, s32[]{:S(2)}) async-start(s8[6291456]{0:T(1024)(128)(4,1)} %bitcast.6), calls=%async_computation.1 | async-start | bytes 4194304
  24.1 9.2 %collective-permute-start.6 = (bf16[64,2048]{1,0:T(8,128)(2,1)S(1)}, bf16[64,2048]{1,0:T(8,128)(2,1)S(1)}, u32[]{:S(2)}, u32[]{:S(2)}) collective-permute-start(bf16[64,2048]{1,0:T(8,128)(2,1)S(1)} %add.4.refs_5_.refs_2_), channel_id=1, source_target_pairs={{0,2},{1,3},{2,0},{3,1},{4,6},{5,7},{6,4},{7,5},{8,10},{9,11},{10,... | collective-permute-start | bytes 786440 | tf_op jit(solution)/shard_map/ppermute | solution.py:398
  26.8 1.7 %collective-permute-start.10 = (bf16[128,1024]{1,0:T(8,128)(2,1)S(1)}, bf16[128,1024]{1,0:T(8,128)(2,1)S(1)}, u32[]{:S(2)}, u32[]{:S(2)}) collective-permute-start(bf16[128,1024]{1,0:T(8,128)(2,1)S(1)} %project.10.refs_5_), channel_id=1, source_target_pairs={{0,1},{1,0},{2,3},{3,2},{4,5},{5,4},{6,7},{7,6},{8,9},{9,8},{10,11... | collective-permute-start | bytes 786440 | tf_op jit(solution)/shard_map/ppermute | solution.py:398
  28.6 10.3 %collective-permute-start.12 = (bf16[128,1024]{1,0:T(8,128)(2,1)S(1)}, bf16[128,1024]{1,0:T(8,128)(2,1)S(1)}, u32[]{:S(2)}, u32[]{:S(2)}) collective-permute-start(bf16[128,1024]{1,0:T(8,128)(2,1)S(1)} %add.5.refs_4_), channel_id=1, source_target_pairs={{0,2},{1,3},{2,0},{3,1},{4,6},{5,7},{6,4},{7,5},{8,10},{9,11},{10,... | collective-permute-start | bytes 786440 | tf_op jit(solution)/shard_map/ppermute | solution.py:398
  33.5 3.3 %collective-permute-start.11 = (bf16[128,1024]{1,0:T(8,128)(2,1)S(1)}, bf16[128,1024]{1,0:T(8,128)(2,1)S(1)}, u32[]{:S(2)}, u32[]{:S(2)}) collective-permute-start(bf16[128,1024]{1,0:T(8,128)(2,1)S(1)} %hidden.1.refs_0_), channel_id=1, source_target_pairs={{0,1},{1,0},{2,3},{3,2},{4,5},{5,4},{6,7},{7,6},{8,9},{9,8},{10,11... | collective-permute-start | bytes 786440 | tf_op jit(solution)/shard_map/ppermute | solution.py:398
  39.5 2.7 %collective-permute-start.13 = (bf16[128,2176]{1,0:T(8,128)(2,1)S(1)}, bf16[128,2176]{1,0:T(8,128)(2,1)S(1)}, u32[]{:S(2)}, u32[]{:S(2)}) collective-permute-start(bf16[128,2176]{1,0:T(8,128)(2,1)S(1)} %pre.1.refs_5_.mine_ref.refs_0_), channel_id=1, source_target_pairs={{0,1},{1,0},{2,3},{3,2},{4,5},{5,4},{6,7},{7,6},{8,9},{9,8},{10,11... | collective-permute-start | bytes 1671176 | tf_op jit(solution)/shard_map/ppermute | solution.py:398
  42.2 4.6 %copy-start.2 = (bf16[32,1536]{1,0:T(8,128)(2,1)S(1)}, bf16[32,1536]{1,0:T(8,128)(2,1)}, u32[]{:S(2)}) copy-start(bf16[32,1536]{1,0:T(8,128)(2,1)} %copy-done.1) | copy-start | bytes 294916
  42.2 4.6 %copy-start.4 = (bf16[32,1536]{1,0:T(8,128)(2,1)S(1)}, bf16[32,1536]{1,0:T(8,128)(2,1)}, u32[]{:S(2)}) copy-start(bf16[32,1536]{1,0:T(8,128)(2,1)} %copy-done.3) | copy-start | bytes 294916
  42.2 4.6 %copy-start.6 = (bf16[32,1536]{1,0:T(8,128)(2,1)S(1)}, bf16[32,1536]{1,0:T(8,128)(2,1)}, u32[]{:S(2)}) copy-start(bf16[32,1536]{1,0:T(8,128)(2,1)} %copy-done.5) | copy-start | bytes 294916
  42.2 4.6 %copy-start.8 = (bf16[32,1536]{1,0:T(8,128)(2,1)S(1)}, bf16[32,1536]{1,0:T(8,128)(2,1)}, u32[]{:S(2)}) copy-start(bf16[32,1536]{1,0:T(8,128)(2,1)} %copy-done.7) | copy-start | bytes 294916
  43.2 12.4 %collective-permute-start.14 = (bf16[32,1664]{1,0:T(8,128)(2,1)S(1)}, bf16[32,1664]{1,0:T(8,128)(2,1)S(1)}, u32[]{:S(2)}, u32[]{:S(2)}) collective-permute-start(bf16[32,1664]{1,0:T(8,128)(2,1)S(1)} %get-tuple-element.24), channel_id=1, source_target_pairs={{0,8},{4,12},{8,0},{12,4},{1,9},{5,13},{9,1},{13,5},{2,10},{6,14},... | collective-permute-start | bytes 319496 | tf_op jit(solution)/shard_map/ppermute | solution.py:398
  45.4 10.3 %collective-permute-start.15 = (bf16[32,1664]{1,0:T(8,128)(2,1)S(1)}, bf16[32,1664]{1,0:T(8,128)(2,1)S(1)}, u32[]{:S(2)}, u32[]{:S(2)}) collective-permute-start(bf16[32,1664]{1,0:T(8,128)(2,1)S(1)} %get-tuple-element.25), channel_id=1, source_target_pairs={{0,12},{4,8},{8,4},{12,0},{1,13},{5,9},{9,5},{13,1},{2,14},{6,10},... | collective-permute-start | bytes 319496 | tf_op jit(solution)/shard_map/ppermute | solution.py:398
  46.7 8.9 %collective-permute-start.16 = (bf16[32,1664]{1,0:T(8,128)(2,1)S(1)}, bf16[32,1664]{1,0:T(8,128)(2,1)S(1)}, u32[]{:S(2)}, u32[]{:S(2)}) collective-permute-start(bf16[32,1664]{1,0:T(8,128)(2,1)S(1)} %get-tuple-element.26), channel_id=1, source_target_pairs={{0,4},{4,0},{8,12},{12,8},{1,5},{5,1},{9,13},{13,9},{2,6},{6,2},{1... | collective-permute-start | bytes 319496 | tf_op jit(solution)/shard_map/ppermute | solution.py:398
  46.8 8.9 %copy-start.9 = (s32[128,2]{0,1:T(2,128)S(1)}, s32[128,2]{0,1:T(2,128)}, u32[]{:S(2)}) copy-start(s32[128,2]{0,1:T(2,128)} %param.8) | copy-start | bytes 3076

commit v6 on v5

--- a/solution.py
+++ b/solution.py
@@ -454,8 +454,8 @@
 
     def pass_on(after):
         block = relay([send_grad], after)
+        cot_blocks.append(swap(block, "dp", dp, 3))
         cot_blocks.insert(1, swap(block, "dp", dp, 1))
-        cot_blocks.append(swap(block, "dp", dp, 3))
         return block
 
     chunks, last = [[] for _ in range(pieces)], send_grad

time: 56.9 us -> 56.9 us (level)
  no operation moved by 1% of the time
where the time goes in v6:
time: 56.9 us; the launch traced here: 56.8 us
  Pallas kernels  31.3 us (55%)
  starting transfers between devices  19 us (33%)
  waiting for transfers between devices  4.78 us (8%)
  between operations  0.96 us (2%)
  local copies, waits for them, and re-layouts  0.68 us (1%)
    ppermute x17, starting transfers between devices, swap(): return lax.ppermute(array, axis, [(i, i ^ distance) for i in range(size)])  19 us
    pallas_call x4, Pallas kernels, grads(): pl.pallas_call(functools.partial(grads_kernel, places, *sizes), in_specs=...  16.3 us
    pallas_call x6, Pallas kernels, project(): pl.pallas_call(functools.partial(project_kernel, len(blocks), width, unit...  10.3 us
    ppermute x17, waiting for transfers between devices, swap(): return lax.ppermute(array, axis, [(i, i ^ distance) for i in range(size)])  4.78 us
    pallas_call x1, Pallas kernels, select(): pl.pallas_call(select_kernel, in_specs=[SMEM] * 2 + [HBM] * 4, out_specs=...  1.73 us
  transfers between devices with their start and end apart: 17, of which 4 were waited for; matrix products, arithmetic and copies ran while one was open for 0% of the time, Pallas kernels for 47%

profile of v6, /device:TPU:0, one launch (start us, length us, event | category | flops | bytes accessed | tf_op | source)
XLA Modules:
  0.0 56.8 jit_solution(16798470190286140709)
XLA Ops:
  0.6 1.7 %select.3 = (bf16[32,1536]{1,0:T(8,128)(2,1)S(1)}, bf16[32,1664]{1,0:T(8,128)(2,1)S(1)}, bf16[32,128]{1,0:T(8,128)(2,1)S(1)}) custom-call(s32[1]{0:T(128)} %bitcast.1.own_ref.first_ref, s32[1]{0:T(128)} %bitcast.2.other_ref.first_ref, bf16[128,1536]{1,0:T(8,128)(2,1)} %refs_0_.1, bf16[128,1536]{1,0:T(8,128)(2,1)} %refs_1_.1, s32[2,128]{1,0:T(2,128)} %bitcast.10, ...), custom_call_target="tpu_custom_call" | custom-call | flops 17999998976 | bytes 1024 | tf_op jit(solution)/shard_map/select/pallas_call | solution.py:81
  2.4 0.0 copy-start.1
  2.4 3.1 %collective-permute-start = (bf16[32,1536]{1,0:T(8,128)(2,1)S(1)}, bf16[32,1536]{1,0:T(8,128)(2,1)S(1)}, u32[]{:S(2)}, u32[]{:S(2)}) collective-permute-start(bf16[32,1536]{1,0:T(8,128)(2,1)S(1)} %get-tuple-element.18.refs_0_.refs_2_), channel_id=1, source_target_pairs={{0,4},{4,0},{8,12},{12,8},{1,5},{5,1},{9,13},{13,9},{2,6},{6,2},{1... | collective-permute-start | bytes 294920 | tf_op jit(solution)/shard_map/ppermute | solution.py:398
  5.5 2.6 %collective-permute-start.3 = (bf16[32,1536]{1,0:T(8,128)(2,1)S(1)}, bf16[32,1536]{1,0:T(8,128)(2,1)S(1)}, u32[]{:S(2)}, u32[]{:S(2)}) collective-permute-start(bf16[32,1536]{1,0:T(8,128)(2,1)S(1)} %get-tuple-element.18.refs_0_.refs_2_), channel_id=1, source_target_pairs={{0,8},{4,12},{8,0},{12,4},{1,9},{5,13},{9,1},{13,5},{2,10},{6,14},... | collective-permute-start | bytes 294920 | tf_op jit(solution)/shard_map/ppermute | solution.py:398
  8.1 0.0 collective-permute-start.4
  8.1 1.9 %collective-permute-start.8 = (bf16[32,1664]{1,0:T(8,128)(2,1)S(1)}, bf16[32,1664]{1,0:T(8,128)(2,1)S(1)}, u32[]{:S(2)}, u32[]{:S(2)}) collective-permute-start(bf16[32,1664]{1,0:T(8,128)(2,1)S(1)} %get-tuple-element.19.refs_3_.refs_0_.refs_1_.refs_6_), channel_id=1, source_target_pairs={{0,8},{4,12},{8,0},{12,4},{1,9},{5,13},{9,1},{13,5},{2,10},{6,14},... | collective-permute-start | bytes 319496 | tf_op jit(solution)/shard_map/ppermute | solution.py:398
  10.0 2.0 %project.6.refs_3_ = bf16[64,2048]{1,0:T(8,128)(2,1)S(1)} custom-call(s32[1]{0:T(128)} %bitcast.2.other_ref.first_ref, bf16[32,1536]{1,0:T(8,128)(2,1)S(1)} %get-tuple-element.18.refs_0_.refs_2_, bf16[32,1536]{1,0:T(8,128)(2,1)S(1)} %collective-permute-done.refs_1_.refs_3_, bf16[2,2048,1536]{2,1,0:T(8,128)(2,1)S(1)} %copy-done, ...), custom_call_target="tpu_custom_call" | custom-call | flops 16000000000 | bytes 1024 | tf_op jit(solution)/shard_map/project/pallas_call | solution.py:118
  12.0 0.1 collective-permute-start.1
  12.1 2.0 %project.7.mine_ref = f32[64,2048]{1,0:T(8,128)S(1)} custom-call(s32[1]{0:T(128)} %bitcast.1.own_ref.first_ref, bf16[32,1536]{1,0:T(8,128)(2,1)S(1)} %get-tuple-element.18.refs_0_.refs_2_, bf16[32,1536]{1,0:T(8,128)(2,1)S(1)} %collective-permute-done.refs_1_.refs_3_, bf16[2,2048,1536]{2,1,0:T(8,128)(2,1)S(1)} %copy-done, bf16[64,2048]{1,0:T(8,128)(2,1)S(1)} %project.6.refs_3_), custom_call_target="tpu_custom_call" | custom-call | flops 16000000000 | bytes 1024 | tf_op jit(solution)/shard_map/project/pallas_call | solution.py:118
  14.1 0.0 collective-permute-done.1.arrived_ref
  14.1 0.1 add.3.refs_1_.refs_0_
  14.2 2.5 %collective-permute-start.7 = (bf16[32,1664]{1,0:T(8,128)(2,1)S(1)}, bf16[32,1664]{1,0:T(8,128)(2,1)S(1)}, u32[]{:S(2)}, u32[]{:S(2)}) collective-permute-start(bf16[32,1664]{1,0:T(8,128)(2,1)S(1)} %relay.1.refs_3_), channel_id=1, source_target_pairs={{0,4},{4,0},{8,12},{12,8},{1,5},{5,1},{9,13},{13,9},{2,6},{6,2},{1... | collective-permute-start | bytes 319496 | tf_op jit(solution)/shard_map/ppermute | solution.py:398
  16.7 1.1 %collective-permute-start.9 = (bf16[32,1664]{1,0:T(8,128)(2,1)S(1)}, bf16[32,1664]{1,0:T(8,128)(2,1)S(1)}, u32[]{:S(2)}, u32[]{:S(2)}) collective-permute-start(bf16[32,1664]{1,0:T(8,128)(2,1)S(1)} %relay.1.refs_3_), channel_id=1, source_target_pairs={{0,12},{4,8},{8,4},{12,0},{1,13},{5,9},{9,5},{13,1},{2,14},{6,10},... | collective-permute-start | bytes 319496 | tf_op jit(solution)/shard_map/ppermute | solution.py:398
  17.8 0.6 collective-permute-done.3.refs_0_.refs_4_
  18.4 1.5 %collective-permute-start.2 = (bf16[64,2048]{1,0:T(8,128)(2,1)S(1)}, bf16[64,2048]{1,0:T(8,128)(2,1)S(1)}, u32[]{:S(2)}, u32[]{:S(2)}) collective-permute-start(bf16[64,2048]{1,0:T(8,128)(2,1)S(1)} %add.3.refs_1_.refs_0_), channel_id=1, source_target_pairs={{0,2},{1,3},{2,0},{3,1},{4,6},{5,7},{6,4},{7,5},{8,10},{9,11},{10,... | collective-permute-start | bytes 786440 | tf_op jit(solution)/shard_map/ppermute | solution.py:398
  19.9 2.0 %project.8.refs_3_ = bf16[64,2048]{1,0:T(8,128)(2,1)S(1)} custom-call(s32[1]{0:T(128)} %bitcast.2.other_ref.first_ref, bf16[32,1536]{1,0:T(8,128)(2,1)S(1)} %collective-permute-done.3.refs_0_.refs_4_, bf16[32,1536]{1,0:T(8,128)(2,1)S(1)} %collective-permute-done.4.refs_1_.refs_5_, bf16[2,2048,1536]{2,1,0:T(8,128)(2,1)S(1)} %copy-done, ...), custom_call_target="tpu_custom_call" | custom-call | flops 16000000000 | bytes 1024 | tf_op jit(solution)/shard_map/project/pallas_call | solution.py:118
  21.9 0.1 collective-permute-start.5
  22.0 0.0 slice-start
  22.0 2.0 %project.9.mine_ref = f32[64,2048]{1,0:T(8,128)S(1)} custom-call(s32[1]{0:T(128)} %bitcast.1.own_ref.first_ref, bf16[32,1536]{1,0:T(8,128)(2,1)S(1)} %collective-permute-done.3.refs_0_.refs_4_, bf16[32,1536]{1,0:T(8,128)(2,1)S(1)} %collective-permute-done.4.refs_1_.refs_5_, bf16[2,2048,1536]{2,1,0:T(8,128)(2,1)S(1)} %copy-done, ...), custom_call_target="tpu_custom_call" | custom-call | flops 16000000000 | bytes 1024 | tf_op jit(solution)/shard_map/project/pallas_call | solution.py:118
  24.0 0.0 slice-start.1
  24.0 0.1 add.4.refs_5_.refs_2_
  24.1 0.6 %collective-permute-start.6 = (bf16[64,2048]{1,0:T(8,128)(2,1)S(1)}, bf16[64,2048]{1,0:T(8,128)(2,1)S(1)}, u32[]{:S(2)}, u32[]{:S(2)}) collective-permute-start(bf16[64,2048]{1,0:T(8,128)(2,1)S(1)} %add.4.refs_5_.refs_2_), channel_id=1, source_target_pairs={{0,2},{1,3},{2,0},{3,1},{4,6},{5,7},{6,4},{7,5},{8,10},{9,11},{10,... | collective-permute-start | bytes 786440 | tf_op jit(solution)/shard_map/ppermute | solution.py:398
  24.7 0.2 collective-permute-done.8.refs_2_.refs_3_.refs_8_
  24.9 0.1 collective-permute-done.7.refs_1_.refs_2_.refs_7_
  25.0 0.6 %slice-done.1 = s8[2097152]{0:T(1024)(128)(4,1)S(1)} async-done(((s8[6291456]{0:T(1024)(128)(4,1)}), s8[2097152]{0:T(1024)(128)(4,1)S(1)}, s32[]{:S(2)}) %slice-start.1) | async-done | bytes 2097176
  25.7 1.1 %project.10.refs_5_ = bf16[128,1024]{1,0:T(8,128)(2,1)S(1)} custom-call(s32[1]{0:T(128)} %bitcast.2.other_ref.first_ref, bf16[32,1664]{1,0:T(8,128)(2,1)S(1)} %get-tuple-element.19.refs_3_.refs_0_.refs_1_.refs_6_, bf16[32,1664]{1,0:T(8,128)(2,1)S(1)} %collective-permute-done.7.refs_1_.refs_2_.refs_7_, ...), custom_call_target="tpu_custom_call" | custom-call | flops 16000000000 | bytes 1024 | tf_op jit(solution)/shard_map/project/pallas_call | solution.py:118
  26.8 0.5 collective-permute-start.10
  27.3 1.1 %project.11.mine_ref = f32[128,1024]{1,0:T(8,128)S(1)} custom-call(s32[1]{0:T(128)} %bitcast.1.own_ref.first_ref, bf16[32,1664]{1,0:T(8,128)(2,1)S(1)} %get-tuple-element.19.refs_3_.refs_0_.refs_1_.refs_6_, bf16[32,1664]{1,0:T(8,128)(2,1)S(1)} %collective-permute-done.7.refs_1_.refs_2_.refs_7_, ...), custom_call_target="tpu_custom_call" | custom-call | flops 16000000000 | bytes 1024 | tf_op jit(solution)/shard_map/project/pallas_call | solution.py:118
  28.5 0.0 collective-permute-done.10.arrived_ref
  28.5 0.1 add.5.refs_4_
  28.6 0.9 %collective-permute-start.12 = (bf16[128,1024]{1,0:T(8,128)(2,1)S(1)}, bf16[128,1024]{1,0:T(8,128)(2,1)S(1)}, u32[]{:S(2)}, u32[]{:S(2)}) collective-permute-start(bf16[128,1024]{1,0:T(8,128)(2,1)S(1)} %add.5.refs_4_), channel_id=1, source_target_pairs={{0,2},{1,3},{2,0},{3,1},{4,6},{5,7},{6,4},{7,5},{8,10},{9,11},{10,... | collective-permute-start | bytes 786440 | tf_op jit(solution)/shard_map/ppermute | solution.py:398
  29.4 3.8 %collective-permute-done.6.refs_3_ = bf16[64,2048]{1,0:T(8,128)(2,1)S(1)} collective-permute-done((bf16[64,2048]{1,0:T(8,128)(2,1)S(1)}, bf16[64,2048]{1,0:T(8,128)(2,1)S(1)}, u32[]{:S(2)}, u32[]{:S(2)}) %collective-permute-start.6) | collective-permute-done | bytes 262176 | tf_op jit(solution)/shard_map/ppermute | solution.py:398
  33.3 0.2 hidden.1.refs_0_
  33.5 0.1 collective-permute-start.11
  33.5 3.2 %grads.4.refs_5_ = f32[2048,1536]{1,0:T(8,128)} custom-call(s32[1]{0:T(128)} %bitcast.1.own_ref.first_ref, s32[1]{0:T(128)} %bitcast.2.other_ref.first_ref, bf16[128,1024]{1,0:T(8,128)(2,1)S(1)} %hidden.1.refs_0_, bf16[32,1664]{1,0:T(8,128)(2,1)S(1)} %get-tuple-element.19.refs_3_.refs_0_.refs_1_.refs_6_, ...), custom_call_target="tpu_custom_call" | custom-call | flops 16000000000 | bytes 1024 | tf_op jit(solution)/shard_map/grads/pallas_call | solution.py:342
  36.7 2.1 %grads.5 = (f32[2048,1536]{1,0:T(8,128)}, f32[8,128]{1,0:T(8,128)S(1)}) custom-call(s32[1]{0:T(128)} %bitcast.1.own_ref.first_ref, s32[1]{0:T(128)} %bitcast.2.other_ref.first_ref, bf16[128,1024]{1,0:T(8,128)(2,1)S(1)} %collective-permute-done.11.refs_0_, ...), custom_call_target="tpu_custom_call", output_to_operand_aliasing={{0}: (7, {})} | custom-call | flops 16000000000 | bytes 1024 | tf_op jit(solution)/shard_map/grads/pallas_call | solution.py:342
  38.9 0.6 %pre.1.refs_5_.mine_ref.refs_0_ = bf16[128,2176]{1,0:T(8,128)(2,1)S(1)} custom-call(bf16[64,2048]{1,0:T(8,128)(2,1)S(1)} %add.3.refs_1_.refs_0_, bf16[64,2048]{1,0:T(8,128)(2,1)S(1)} %collective-permute-done.2.refs_1_, bf16[64,2048]{1,0:T(8,128)(2,1)S(1)} %add.4.refs_5_.refs_2_, bf16[64,2048]{1,0:T(8,128)(2,1)S(1)} %collective-permute-done.6.refs_3_, ...), custom_call_target="tpu_custom_call" | custom-call | flops 16000000000 | bytes 1024 | tf_op jit(solution)/shard_map/pre/pallas_call | solution.py:216
  39.5 0.6 collective-permute-start.13
  40.0 2.1 %grads.6 = (f32[2048,1536]{1,0:T(8,128)}, f32[128,1536]{1,0:T(8,128)S(1)}) custom-call(s32[1]{0:T(128)} %bitcast.1.own_ref.first_ref, s32[1]{0:T(128)} %bitcast.2.other_ref.first_ref, bf16[128,1024]{1,0:T(8,128)(2,1)S(1)} %collective-permute-done.11.refs_0_, ...), custom_call_target="tpu_custom_call", output_to_operand_aliasing={{0}: (9, {})} | custom-call | flops 16000000000 | bytes 1024 | tf_op jit(solution)/shard_map/grads/pallas_call | solution.py:342
  42.2 0.0 copy-start.2
  42.2 0.0 copy-start.4
  42.2 1.0 %row_rest.1 = (f32[32,1664]{1,0:T(8,128)S(1)}, bf16[32,1664]{1,0:T(8,128)(2,1)S(1)}, bf16[32,1664]{1,0:T(8,128)(2,1)S(1)}, bf16[32,1664]{1,0:T(8,128)(2,1)S(1)}) custom-call(s32[1]{0:T(128)} %bitcast.2.other_ref.first_ref, f32[128,1536]{1,0:T(8,128)S(1)} %get-tuple-element.22.own_ref, bf16[128,2176]{1,0:T(8,128)(2,1)S(1)} %pre.1.refs_5_.mine_ref.refs_0_, ...), custom_call_target="tpu_custom_call" | custom-call | flops 16000000000 | bytes 1024 | tf_op jit(solution)/shard_map/row_rest/pallas_call | solution.py:267
  43.2 2.2 %collective-permute-start.14 = (bf16[32,1664]{1,0:T(8,128)(2,1)S(1)}, bf16[32,1664]{1,0:T(8,128)(2,1)S(1)}, u32[]{:S(2)}, u32[]{:S(2)}) collective-permute-start(bf16[32,1664]{1,0:T(8,128)(2,1)S(1)} %get-tuple-element.24), channel_id=1, source_target_pairs={{0,8},{4,12},{8,0},{12,4},{1,9},{5,13},{9,1},{13,5},{2,10},{6,14},... | collective-permute-start | bytes 319496 | tf_op jit(solution)/shard_map/ppermute | solution.py:398
  45.4 1.3 %collective-permute-start.15 = (bf16[32,1664]{1,0:T(8,128)(2,1)S(1)}, bf16[32,1664]{1,0:T(8,128)(2,1)S(1)}, u32[]{:S(2)}, u32[]{:S(2)}) collective-permute-start(bf16[32,1664]{1,0:T(8,128)(2,1)S(1)} %get-tuple-element.25), channel_id=1, source_target_pairs={{0,12},{4,8},{8,4},{12,0},{1,13},{5,9},{9,5},{13,1},{2,14},{6,10},... | collective-permute-start | bytes 319496 | tf_op jit(solution)/shard_map/ppermute | solution.py:398
  46.7 0.1 collective-permute-start.16
  46.8 0.0 copy-start.9
  46.8 8.8 %grads.7 = f32[2,2048,1536]{2,1,0:T(8,128)} custom-call(s32[1]{0:T(128)} %bitcast.1.own_ref.first_ref, s32[1]{0:T(128)} %bitcast.2.other_ref.first_ref, bf16[128,2176]{1,0:T(8,128)(2,1)S(1)} %pre.1.refs_5_.mine_ref.refs_0_, bf16[128,2176]{1,0:T(8,128)(2,1)S(1)} %collective-permute-done.13.pre_ref.refs_1_, bf16[32,1536]{1,0:T(8,128)(2,1)S(1)} %copy-done.2, ...), custom_call_target="tpu_custom_call" | custom-call | flops 16000000000 | bytes 1024 | tf_op jit(solution)/shard_map/grads/pallas_call | solution.py:342
  55.7 1.1 %place.1 = (bf16[128,1536]{1,0:T(8,128)(2,1)}, bf16[2,128]{1,0:T(2,128)(2,1)}) custom-call(s32[2,128]{1,0:T(2,128)S(1)} %bitcast.11, bf16[32,128]{1,0:T(8,128)(2,1)S(1)} %get-tuple-element.17.picker_ref, f32[32,1664]{1,0:T(8,128)S(1)} %get-tuple-element.23.refs_0_.refs_6_, bf16[32,1664]{1,0:T(8,128)(2,1)S(1)} %collective-permute-done.14.refs_1_, ...), custom_call_target="tpu_custom_call" | custom-call | flops 16000000000 | bytes 1024 | tf_op jit(solution)/shard_map/place/pallas_call | solution.py:383
  (30 shorter events, 0.1 us)
Async XLA Ops:
  0.6 9.4 %copy-start = (bf16[2,2048,1536]{2,1,0:T(8,128)(2,1)S(1)}, bf16[2,2048,1536]{2,1,0:T(8,128)(2,1)}, u32[]{:S(2)}) copy-start(bf16[2,2048,1536]{2,1,0:T(8,128)(2,1)} %w_ref.1) | copy-start | bytes 37748740
  2.4 9.7 %copy-start.1 = (bf16[32,1536]{1,0:T(8,128)(2,1)}, bf16[32,1536]{1,0:T(8,128)(2,1)S(1)}, u32[]{:S(2)}) copy-start(bf16[32,1536]{1,0:T(8,128)(2,1)S(1)} %get-tuple-element.18.refs_0_.refs_2_) | copy-start | bytes 294916
  2.4 7.6 %collective-permute-start = (bf16[32,1536]{1,0:T(8,128)(2,1)S(1)}, bf16[32,1536]{1,0:T(8,128)(2,1)S(1)}, u32[]{:S(2)}, u32[]{:S(2)}) collective-permute-start(bf16[32,1536]{1,0:T(8,128)(2,1)S(1)} %get-tuple-element.18.refs_0_.refs_2_), channel_id=1, source_target_pairs={{0,4},{4,0},{8,12},{12,8},{1,5},{5,1},{9,13},{13,9},{2,6},{6,2},{1... | collective-permute-start | bytes 294920 | tf_op jit(solution)/shard_map/ppermute | solution.py:398
  5.5 12.9 %collective-permute-start.3 = (bf16[32,1536]{1,0:T(8,128)(2,1)S(1)}, bf16[32,1536]{1,0:T(8,128)(2,1)S(1)}, u32[]{:S(2)}, u32[]{:S(2)}) collective-permute-start(bf16[32,1536]{1,0:T(8,128)(2,1)S(1)} %get-tuple-element.18.refs_0_.refs_2_), channel_id=1, source_target_pairs={{0,8},{4,12},{8,0},{12,4},{1,9},{5,13},{9,1},{13,5},{2,10},{6,14},... | collective-permute-start | bytes 294920 | tf_op jit(solution)/shard_map/ppermute | solution.py:398
  8.1 11.8 %collective-permute-start.4 = (bf16[32,1536]{1,0:T(8,128)(2,1)S(1)}, bf16[32,1536]{1,0:T(8,128)(2,1)S(1)}, u32[]{:S(2)}, u32[]{:S(2)}) collective-permute-start(bf16[32,1536]{1,0:T(8,128)(2,1)S(1)} %get-tuple-element.18.refs_0_.refs_2_), channel_id=1, source_target_pairs={{0,12},{4,8},{8,4},{12,0},{1,13},{5,9},{9,5},{13,1},{2,14},{6,10},... | collective-permute-start | bytes 294920 | tf_op jit(solution)/shard_map/ppermute | solution.py:398
  8.1 16.9 %collective-permute-start.8 = (bf16[32,1664]{1,0:T(8,128)(2,1)S(1)}, bf16[32,1664]{1,0:T(8,128)(2,1)S(1)}, u32[]{:S(2)}, u32[]{:S(2)}) collective-permute-start(bf16[32,1664]{1,0:T(8,128)(2,1)S(1)} %get-tuple-element.19.refs_3_.refs_0_.refs_1_.refs_6_), channel_id=1, source_target_pairs={{0,8},{4,12},{8,0},{12,4},{1,9},{5,13},{9,1},{13,5},{2,10},{6,14},... | collective-permute-start | bytes 319496 | tf_op jit(solution)/shard_map/ppermute | solution.py:398
  10.0 2.1 %copy-start.3 = (bf16[32,1536]{1,0:T(8,128)(2,1)}, bf16[32,1536]{1,0:T(8,128)(2,1)S(1)}, u32[]{:S(2)}) copy-start(bf16[32,1536]{1,0:T(8,128)(2,1)S(1)} %collective-permute-done.refs_1_.refs_3_) | copy-start | bytes 294916
  12.0 2.1 %collective-permute-start.1 = (bf16[64,2048]{1,0:T(8,128)(2,1)S(1)}, bf16[64,2048]{1,0:T(8,128)(2,1)S(1)}, u32[]{:S(2)}, u32[]{:S(2)}) collective-permute-start(bf16[64,2048]{1,0:T(8,128)(2,1)S(1)} %project.6.refs_3_), channel_id=1, source_target_pairs={{0,1},{1,0},{2,3},{3,2},{4,5},{5,4},{6,7},{7,6},{8,9},{9,8},{10,11... | collective-permute-start | bytes 786440 | tf_op jit(solution)/shard_map/ppermute | solution.py:398
  14.2 10.8 %collective-permute-start.7 = (bf16[32,1664]{1,0:T(8,128)(2,1)S(1)}, bf16[32,1664]{1,0:T(8,128)(2,1)S(1)}, u32[]{:S(2)}, u32[]{:S(2)}) collective-permute-start(bf16[32,1664]{1,0:T(8,128)(2,1)S(1)} %relay.1.refs_3_), channel_id=1, source_target_pairs={{0,4},{4,0},{8,12},{12,8},{1,5},{5,1},{9,13},{13,9},{2,6},{6,2},{1... | collective-permute-start | bytes 319496 | tf_op jit(solution)/shard_map/ppermute | solution.py:398
  16.7 8.3 %collective-permute-start.9 = (bf16[32,1664]{1,0:T(8,128)(2,1)S(1)}, bf16[32,1664]{1,0:T(8,128)(2,1)S(1)}, u32[]{:S(2)}, u32[]{:S(2)}) collective-permute-start(bf16[32,1664]{1,0:T(8,128)(2,1)S(1)} %relay.1.refs_3_), channel_id=1, source_target_pairs={{0,12},{4,8},{8,4},{12,0},{1,13},{5,9},{9,5},{13,1},{2,14},{6,10},... | collective-permute-start | bytes 319496 | tf_op jit(solution)/shard_map/ppermute | solution.py:398
  18.4 3.6 %copy-start.5 = (bf16[32,1536]{1,0:T(8,128)(2,1)}, bf16[32,1536]{1,0:T(8,128)(2,1)S(1)}, u32[]{:S(2)}) copy-start(bf16[32,1536]{1,0:T(8,128)(2,1)S(1)} %collective-permute-done.3.refs_0_.refs_4_) | copy-start | bytes 294916
  18.4 11.0 %collective-permute-start.2 = (bf16[64,2048]{1,0:T(8,128)(2,1)S(1)}, bf16[64,2048]{1,0:T(8,128)(2,1)S(1)}, u32[]{:S(2)}, u32[]{:S(2)}) collective-permute-start(bf16[64,2048]{1,0:T(8,128)(2,1)S(1)} %add.3.refs_1_.refs_0_), channel_id=1, source_target_pairs={{0,2},{1,3},{2,0},{3,1},{4,6},{5,7},{6,4},{7,5},{8,10},{9,11},{10,... | collective-permute-start | bytes 786440 | tf_op jit(solution)/shard_map/ppermute | solution.py:398
  19.9 2.1 %copy-start.7 = (bf16[32,1536]{1,0:T(8,128)(2,1)}, bf16[32,1536]{1,0:T(8,128)(2,1)S(1)}, u32[]{:S(2)}) copy-start(bf16[32,1536]{1,0:T(8,128)(2,1)S(1)} %collective-permute-done.4.refs_1_.refs_5_) | copy-start | bytes 294916
  21.9 2.1 %collective-permute-start.5 = (bf16[64,2048]{1,0:T(8,128)(2,1)S(1)}, bf16[64,2048]{1,0:T(8,128)(2,1)S(1)}, u32[]{:S(2)}, u32[]{:S(2)}) collective-permute-start(bf16[64,2048]{1,0:T(8,128)(2,1)S(1)} %project.8.refs_3_), channel_id=1, source_target_pairs={{0,1},{1,0},{2,3},{3,2},{4,5},{5,4},{6,7},{7,6},{8,9},{9,8},{10,11... | collective-permute-start | bytes 786440 | tf_op jit(solution)/shard_map/ppermute | solution.py:398
  22.0 3.0 %slice-start = ((s8[6291456]{0:T(1024)(128)(4,1)}), s8[4194304]{0:T(1024)(128)(4,1)S(1)}, s32[]{:S(2)}) async-start(s8[6291456]{0:T(1024)(128)(4,1)} %bitcast.6), calls=%async_computation | async-start | bytes 8388608
  24.0 1.6 %slice-start.1 = ((s8[6291456]{0:T(1024)(128)(4,1)}), s8[2097152]{0:T(1024)(128)(4,1)S(1)}, s32[]{:S(2)}) async-start(s8[6291456]{0:T(1024)(128)(4,1)} %bitcast.6), calls=%async_computation.1 | async-start | bytes 4194304
  24.1 9.2 %collective-permute-start.6 = (bf16[64,2048]{1,0:T(8,128)(2,1)S(1)}, bf16[64,2048]{1,0:T(8,128)(2,1)S(1)}, u32[]{:S(2)}, u32[]{:S(2)}) collective-permute-start(bf16[64,2048]{1,0:T(8,128)(2,1)S(1)} %add.4.refs_5_.refs_2_), channel_id=1, source_target_pairs={{0,2},{1,3},{2,0},{3,1},{4,6},{5,7},{6,4},{7,5},{8,10},{9,11},{10,... | collective-permute-start | bytes 786440 | tf_op jit(solution)/shard_map/ppermute | solution.py:398
  26.8 1.7 %collective-permute-start.10 = (bf16[128,1024]{1,0:T(8,128)(2,1)S(1)}, bf16[128,1024]{1,0:T(8,128)(2,1)S(1)}, u32[]{:S(2)}, u32[]{:S(2)}) collective-permute-start(bf16[128,1024]{1,0:T(8,128)(2,1)S(1)} %project.10.refs_5_), channel_id=1, source_target_pairs={{0,1},{1,0},{2,3},{3,2},{4,5},{5,4},{6,7},{7,6},{8,9},{9,8},{10,11... | collective-permute-start | bytes 786440 | tf_op jit(solution)/shard_map/ppermute | solution.py:398
  28.6 10.3 %collective-permute-start.12 = (bf16[128,1024]{1,0:T(8,128)(2,1)S(1)}, bf16[128,1024]{1,0:T(8,128)(2,1)S(1)}, u32[]{:S(2)}, u32[]{:S(2)}) collective-permute-start(bf16[128,1024]{1,0:T(8,128)(2,1)S(1)} %add.5.refs_4_), channel_id=1, source_target_pairs={{0,2},{1,3},{2,0},{3,1},{4,6},{5,7},{6,4},{7,5},{8,10},{9,11},{10,... | collective-permute-start | bytes 786440 | tf_op jit(solution)/shard_map/ppermute | solution.py:398
  33.5 3.3 %collective-permute-start.11 = (bf16[128,1024]{1,0:T(8,128)(2,1)S(1)}, bf16[128,1024]{1,0:T(8,128)(2,1)S(1)}, u32[]{:S(2)}, u32[]{:S(2)}) collective-permute-start(bf16[128,1024]{1,0:T(8,128)(2,1)S(1)} %hidden.1.refs_0_), channel_id=1, source_target_pairs={{0,1},{1,0},{2,3},{3,2},{4,5},{5,4},{6,7},{7,6},{8,9},{9,8},{10,11... | collective-permute-start | bytes 786440 | tf_op jit(solution)/shard_map/ppermute | solution.py:398
  39.5 2.7 %collective-permute-start.13 = (bf16[128,2176]{1,0:T(8,128)(2,1)S(1)}, bf16[128,2176]{1,0:T(8,128)(2,1)S(1)}, u32[]{:S(2)}, u32[]{:S(2)}) collective-permute-start(bf16[128,2176]{1,0:T(8,128)(2,1)S(1)} %pre.1.refs_5_.mine_ref.refs_0_), channel_id=1, source_target_pairs={{0,1},{1,0},{2,3},{3,2},{4,5},{5,4},{6,7},{7,6},{8,9},{9,8},{10,11... | collective-permute-start | bytes 1671176 | tf_op jit(solution)/shard_map/ppermute | solution.py:398
  42.2 4.6 %copy-start.2 = (bf16[32,1536]{1,0:T(8,128)(2,1)S(1)}, bf16[32,1536]{1,0:T(8,128)(2,1)}, u32[]{:S(2)}) copy-start(bf16[32,1536]{1,0:T(8,128)(2,1)} %copy-done.1) | copy-start | bytes 294916
  42.2 4.6 %copy-start.4 = (bf16[32,1536]{1,0:T(8,128)(2,1)S(1)}, bf16[32,1536]{1,0:T(8,128)(2,1)}, u32[]{:S(2)}) copy-start(bf16[32,1536]{1,0:T(8,128)(2,1)} %copy-done.3) | copy-start | bytes 294916
  42.2 4.6 %copy-start.6 = (bf16[32,1536]{1,0:T(8,128)(2,1)S(1)}, bf16[32,1536]{1,0:T(8,128)(2,1)}, u32[]{:S(2)}) copy-start(bf16[32,1536]{1,0:T(8,128)(2,1)} %copy-done.5) | copy-start | bytes 294916
  42.2 4.6 %copy-start.8 = (bf16[32,1536]{1,0:T(8,128)(2,1)S(1)}, bf16[32,1536]{1,0:T(8,128)(2,1)}, u32[]{:S(2)}) copy-start(bf16[32,1536]{1,0:T(8,128)(2,1)} %copy-done.7) | copy-start | bytes 294916
  43.2 12.4 %collective-permute-start.14 = (bf16[32,1664]{1,0:T(8,128)(2,1)S(1)}, bf16[32,1664]{1,0:T(8,128)(2,1)S(1)}, u32[]{:S(2)}, u32[]{:S(2)}) collective-permute-start(bf16[32,1664]{1,0:T(8,128)(2,1)S(1)} %get-tuple-element.24), channel_id=1, source_target_pairs={{0,8},{4,12},{8,0},{12,4},{1,9},{5,13},{9,1},{13,5},{2,10},{6,14},... | collective-permute-start | bytes 319496 | tf_op jit(solution)/shard_map/ppermute | solution.py:398
  45.4 10.3 %collective-permute-start.15 = (bf16[32,1664]{1,0:T(8,128)(2,1)S(1)}, bf16[32,1664]{1,0:T(8,128)(2,1)S(1)}, u32[]{:S(2)}, u32[]{:S(2)}) collective-permute-start(bf16[32,1664]{1,0:T(8,128)(2,1)S(1)} %get-tuple-element.25), channel_id=1, source_target_pairs={{0,12},{4,8},{8,4},{12,0},{1,13},{5,9},{9,5},{13,1},{2,14},{6,10},... | collective-permute-start | bytes 319496 | tf_op jit(solution)/shard_map/ppermute | solution.py:398
  46.7 8.9 %collective-permute-start.16 = (bf16[32,1664]{1,0:T(8,128)(2,1)S(1)}, bf16[32,1664]{1,0:T(8,128)(2,1)S(1)}, u32[]{:S(2)}, u32[]{:S(2)}) collective-permute-start(bf16[32,1664]{1,0:T(8,128)(2,1)S(1)} %get-tuple-element.26), channel_id=1, source_target_pairs={{0,4},{4,0},{8,12},{12,8},{1,5},{5,1},{9,13},{13,9},{2,6},{6,2},{1... | collective-permute-start | bytes 319496 | tf_op jit(solution)/shard_map/ppermute | solution.py:398
  46.8 8.9 %copy-start.9 = (s32[128,2]{0,1:T(2,128)S(1)}, s32[128,2]{0,1:T(2,128)}, u32[]{:S(2)}) copy-start(s32[128,2]{0,1:T(2,128)} %param.8) | copy-start | bytes 3076
